TPU v7x, 256 devices: a whole 4x4x8 slice. The times are simulated.
256 devices in a mesh: bricks: 256 (over y, x, z, core).
Axes of the slice: x: 4, y: 4, z: 8, core: 2. Of those that a mesh axis runs over, the one named last changes fastest.
Arguments:
- load_field: float32 [3, 4096, 16, 128], P(None, 'bricks'), may hold values from -6 to 6
- material_class: int32 [4096, 16, 128], P('bricks'), may hold values from 0 to 7
- occupancy: int32 [256, 1, 8], P('bricks'), may hold values 0 or 1
- moduli: float32 [8], replicated, may hold values from 0.3 to 3
Outputs:
- correction: float32 [3, 4096, 16, 128], P(None, 'bricks')
All inputs are finite; a program needn't handle non-finite values. No bound on the sum of `occupancy` on one device may be relied on, other than what follows from the above.
Results may differ from a plain program's by a relative error of at most 0.0001.
Values sent between devices are 32-bit elements; how exact they have to be, the bound alone decides.
No kernel may reach another device: no remote copies, remote signals or barrier semaphores. Data moves between devices by JAX's collectives and lax.ppermute only.
A program may use at most 128 MiB of HBM per device.

v0:
```python
import jax
import jax.numpy as jnp
from jax import lax
from jax.sharding import PartitionSpec as P

diag_shift = 0.5
couple = 0.25
center = (26.0 + diag_shift) / 27.0
lam_top = 3.0
lam_low = 0.3
cheb_mid = (lam_top + lam_low) / 2.0
cheb_half = (lam_top - lam_low) / 2.0
cheb_ratio = cheb_mid / cheb_half
deepest = 5
semi_from = 3


def partner_2(shard, axis, bit):
    return lax.ppermute(shard, axis, [(i, i ^ 1 << bit) for i in range(lax.axis_size(axis))])


def passed_along(block, axis, distance):
    devices = range(lax.axis_size(axis))
    route = [(i - distance, i) for i in devices if i - distance in devices]
    return lax.ppermute(block, axis, route)


def with_halo(shard, sides, width):
    for axis, dim in sides:
        size, length = (lax.axis_size(axis), shard.shape[dim])
        up = [(i, (i + 1) % size) for i in range(size - 1)]
        down = [(j, i) for i, j in up]
        last = lax.slice_in_dim(shard, length - width, length, axis=dim)
        first = lax.slice_in_dim(shard, 0, width, axis=dim)
        before = lax.ppermute(last, axis, up)
        after = lax.ppermute(first, axis, down)
        shard = jnp.concatenate([before, shard, after], axis=dim)
    return shard


def triple_sum(values, along):
    n = values.shape[along]
    zero = jnp.zeros_like(lax.slice_in_dim(values, 0, 1, axis=along))
    before = jnp.concatenate([zero, lax.slice_in_dim(values, 0, n - 1, axis=along)], axis=along)
    after = jnp.concatenate([lax.slice_in_dim(values, 1, n, axis=along), zero], axis=along)
    return before + values + after


def operate_padded(padded, root, solid, factor):
    inner = padded[:, 1:-1]
    boxed = padded[:, :-2] + padded[:, 1:-1] + padded[:, 2:]
    boxed = triple_sum(triple_sum(boxed, 2), 3)
    w = ((27.0 + diag_shift) * inner - boxed) / 27.0
    mixture = (1.0 - couple) * w + couple * jnp.sum(w, axis=0, keepdims=True)
    return factor * root * solid * mixture


def smooth(b, start_x, root, solid, factor, operator_fn):
    inv_diag = solid / (factor * center * root * root)
    if start_x is None:
        residue = b
    else:
        residue = b - operator_fn(start_x)
    update = inv_diag * residue / cheb_mid
    x = update if start_x is None else start_x + update
    rho_old = 1.0 / cheb_ratio
    for k in range(2):
        rho_new = 1.0 / (2.0 * cheb_ratio - rho_old)
        residue = b - operator_fn(x)
        update = rho_new * rho_old * update + 2.0 * rho_new / cheb_half * (inv_diag * residue)
        x = x + update
        rho_old = rho_new
    return x


def coarsen(values, all_dims):
    c, z, h, y = values.shape
    if all_dims:
        return jnp.mean(values.reshape(c, z // 2, 2, h // 2, 2, y // 2, 2), axis=(2, 4, 6))
    return jnp.mean(values.reshape(c, z // 2, 2, h, y // 2, 2), axis=(2, 5))


def refine(values, all_dims):
    finer = jnp.repeat(values, 2, axis=1)
    if all_dims:
        finer = jnp.repeat(finer, 2, axis=2)
    return jnp.repeat(finer, 2, axis=3)


def merge_pair(b, root, solid, bit_no):
    stacked = jnp.concatenate([b, root, solid], axis=0)
    partner = partner_2(stacked, "bricks", bit_no)
    bit_val = lax.axis_index("bricks") // 2**bit_no % 2
    lower_part = jnp.where(bit_val == 0, stacked, partner)
    upper_part = jnp.where(bit_val == 0, partner, stacked)
    merged = jnp.concatenate([lower_part, upper_part], axis=1)
    return (merged[:3], merged[3:4], merged[4:5])


def paired_level(level_no, b, root, solid):
    bit_no = level_no - semi_from
    b, root, solid = merge_pair(b, root, solid, bit_no)
    stride = 2 ** (bit_no + 1)
    factor = 0.25**level_no

    def operator_fn(u):
        inner = u * (root * solid)
        lower_rim = passed_along(inner[:, -1:], "bricks", stride)
        upper_rim = passed_along(inner[:, :1], "bricks", -stride)
        padded = jnp.concatenate([lower_rim, inner, upper_rim], axis=1)
        return operate_padded(padded, root, solid, factor)

    x = smooth(b, None, root, solid, factor, operator_fn)
    if level_no < deepest:
        residue = b - operator_fn(x)
        coarse = paired_level(
            level_no + 1, coarsen(residue, False), coarsen(root, False), coarsen(solid, False)
        )
        x = smooth(b, x + refine(coarse, False), root, solid, factor, operator_fn)
    bit_val = lax.axis_index("bricks") // 2**bit_no % 2
    half_len = x.shape[1] // 2
    return lax.dynamic_slice_in_dim(x, bit_val * half_len, half_len, 1)


def descend(level_no, residue, root, solid, same_level):
    coarse_load = coarsen(residue, True)
    coarse_root = coarsen(root, True)
    coarse_solid = coarsen(solid, True)
    if level_no + 1 < semi_from:
        return same_level(level_no + 1, coarse_load, coarse_root, coarse_solid)
    return paired_level(semi_from, coarse_load, coarse_root, coarse_solid)


def fine_level(level_no, b, root, solid):
    factor = 0.25**level_no

    def operator_fn(u):
        padded = with_halo(u * (root * solid), (("bricks", 1),), 1)
        return operate_padded(padded, root, solid, factor)

    x = smooth(b, None, root, solid, factor, operator_fn)
    residue = b - operator_fn(x)
    coarse = descend(level_no, residue, root, solid, fine_level)
    return smooth(b, x + refine(coarse, True), root, solid, factor, operator_fn)


def body(load_field, material_class, occupancy, moduli):
    modulus = jnp.zeros(material_class.shape, jnp.float32)
    for k in range(moduli.shape[0]):
        modulus = modulus + jnp.where(material_class == k, moduli[k], 0.0)
    root = jnp.sqrt(modulus)[None]
    brick_edge = load_field.shape[1]
    bricks_map = occupancy.astype(jnp.float32)
    bricks_map = jnp.repeat(
        jnp.repeat(jnp.repeat(bricks_map, brick_edge, axis=0), brick_edge, axis=1),
        brick_edge,
        axis=2,
    )
    solid = bricks_map[None]
    return fine_level(0, load_field, root, solid)


def solution(mesh):
    in_specs = (
        P(None, "bricks", None, None),
        P("bricks", None, None),
        P("bricks", None, None),
        P(),
    )
    out_specs = P(None, "bricks", None, None)
    return jax.shard_map(body, mesh=mesh, in_specs=in_specs, out_specs=out_specs, check_vma=False)
```

profile of v0, /device:TPU:24, one launch (start us, length us, event | category | flops | bytes accessed | tf_op | source)
XLA Modules:
  0.0 487.8 jit_solution(17333647495587658218)
XLA Ops:
  11.7 9.6 %collective-permute-start.1 = (f32[3,1,16,128]{3,2,1,0:T(8,128)S(1)}, f32[3,1,16,128]{3,2,1,0:T(8,128)S(1)}, u32[]{:S(2)}, u32[]{:S(2)}) collective-permute-start(f32[3,1,16,128]{3,2,1,0:T(8,128)S(1)} %get-tuple-element.164), channel_id=1, source_target_pairs={{1,0},{2,1},{3,2},{4,3},{5,4},{6,5},{7,6},{8,7},{9,8},{10,9},{11,1... | collective-permute-start | bytes 73736 | tf_op jit(solution)/shard_map/ppermute | solution.py:36
  25.5 7.9 %collective-permute-start.3 = (f32[3,1,16,128]{3,2,1,0:T(8,128)S(1)}, f32[3,1,16,128]{3,2,1,0:T(8,128)S(1)}, u32[]{:S(2)}, u32[]{:S(2)}) collective-permute-start(f32[3,1,16,128]{3,2,1,0:T(8,128)S(1)} %get-tuple-element.158), channel_id=1, source_target_pairs={{1,0},{2,1},{3,2},{4,3},{5,4},{6,5},{7,6},{8,7},{9,8},{10,9},{11,1... | collective-permute-start | bytes 73736 | tf_op jit(solution)/shard_map/ppermute | solution.py:36
  33.4 9.8 %reshape_broadcast_in_dim.3 = f32[8,2,8,2,64,2]{5,4,3,2,1,0:T(8,128)} reshape(f32[16,16,128]{2,1,0:T(8,128)S(1)} %get-tuple-element.126) | data formatting | bytes 262144 | tf_op jit(solution)/shard_map/reshape;broadcast_in_dim | solution.py:79
  50.7 7.9 %collective-permute-start.5 = (f32[3,1,16,128]{3,2,1,0:T(8,128)S(1)}, f32[3,1,16,128]{3,2,1,0:T(8,128)S(1)}, u32[]{:S(2)}, u32[]{:S(2)}) collective-permute-start(f32[3,1,16,128]{3,2,1,0:T(8,128)S(1)} %get-tuple-element.152), channel_id=1, source_target_pairs={{1,0},{2,1},{3,2},{4,3},{5,4},{6,5},{7,6},{8,7},{9,8},{10,9},{11,1... | collective-permute-start | bytes 73736 | tf_op jit(solution)/shard_map/ppermute | solution.py:36
  60.8 26.5 %reshape.379 = f32[3,8,2,8,2,64,2]{6,5,4,3,2,1,0:T(8,128)} reshape(f32[3,16,16,128]{3,2,1,0:T(8,128)S(1)} %multiply_subtract_fusion) | data formatting | bytes 786432 | tf_op jit(solution)/shard_map/reshape | solution.py:79
  87.3 9.4 %reduce_sum.422 = f32[3,8,8,64]{3,2,1,0:T(8,128)S(1)} reduce(f32[3,8,2,8,2,64,2]{6,5,4,3,2,1,0:T(8,128)} %reshape.379, f32[]{:T(128)} %constant.269.clone.1), dimensions={2,4,6}, to_apply=%region_3.4 | reduce | flops 86016 | bytes 442372 | tf_op jit(solution)/shard_map/reduce_sum | solution.py:79
  98.7 7.9 %collective-permute-start.7 = (f32[3,1,8,64]{3,2,1,0:T(8,128)S(1)}, f32[3,1,8,64]{3,2,1,0:T(8,128)S(1)}, u32[]{:S(2)}, u32[]{:S(2)}) collective-permute-start(f32[3,1,8,64]{3,2,1,0:T(8,128)S(1)} %get-tuple-element.202), channel_id=1, source_target_pairs={{1,0},{2,1},{3,2},{4,3},{5,4},{6,5},{7,6},{8,7},{9,8},{10,9},{11,1... | collective-permute-start | bytes 18440 | tf_op jit(solution)/shard_map/ppermute | solution.py:36
  110.3 7.9 %collective-permute-start.9 = (f32[3,1,8,64]{3,2,1,0:T(8,128)S(1)}, f32[3,1,8,64]{3,2,1,0:T(8,128)S(1)}, u32[]{:S(2)}, u32[]{:S(2)}) collective-permute-start(f32[3,1,8,64]{3,2,1,0:T(8,128)S(1)} %get-tuple-element.196), channel_id=1, source_target_pairs={{1,0},{2,1},{3,2},{4,3},{5,4},{6,5},{7,6},{8,7},{9,8},{10,9},{11,1... | collective-permute-start | bytes 18440 | tf_op jit(solution)/shard_map/ppermute | solution.py:36
  122.5 7.9 %collective-permute-start.11 = (f32[3,1,8,64]{3,2,1,0:T(8,128)S(1)}, f32[3,1,8,64]{3,2,1,0:T(8,128)S(1)}, u32[]{:S(2)}, u32[]{:S(2)}) collective-permute-start(f32[3,1,8,64]{3,2,1,0:T(8,128)S(1)} %get-tuple-element.190), channel_id=1, source_target_pairs={{1,0},{2,1},{3,2},{4,3},{5,4},{6,5},{7,6},{8,7},{9,8},{10,9},{11,1... | collective-permute-start | bytes 18440 | tf_op jit(solution)/shard_map/ppermute | solution.py:36
  140.5 7.9 %collective-permute-start.13 = (f32[3,1,4,32]{3,2,1,0:T(4,128)S(1)}, f32[3,1,4,32]{3,2,1,0:T(4,128)S(1)}, u32[]{:S(2)}, u32[]{:S(2)}) collective-permute-start(f32[3,1,4,32]{3,2,1,0:T(4,128)S(1)} %get-tuple-element.320), channel_id=1, source_target_pairs={{1,0},{2,1},{3,2},{4,3},{5,4},{6,5},{7,6},{8,7},{9,8},{10,9},{11,1... | collective-permute-start | bytes 4616 | tf_op jit(solution)/shard_map/ppermute | solution.py:36
  165.6 7.9 %collective-permute-start.17 = (f32[3,1,4,32]{3,2,1,0:T(4,128)S(1)}, f32[3,1,4,32]{3,2,1,0:T(4,128)S(1)}, u32[]{:S(2)}, u32[]{:S(2)}) collective-permute-start(f32[3,1,4,32]{3,2,1,0:T(4,128)S(1)} %get-tuple-element.308), channel_id=1, source_target_pairs={{1,0},{2,1},{3,2},{4,3},{5,4},{6,5},{7,6},{8,7},{9,8},{10,9},{11,1... | collective-permute-start | bytes 4616 | tf_op jit(solution)/shard_map/ppermute | solution.py:36
  180.2 8.1 %collective-permute-start.20 = (f32[3,1,2,16]{1,3,2,0:T(8,128)S(1)}, f32[3,1,2,16]{1,3,2,0:T(8,128)S(1)}, u32[]{:S(2)}, u32[]{:S(2)}) collective-permute-start(f32[3,1,2,16]{1,3,2,0:T(8,128)S(1)} %get-tuple-element.240), channel_id=1, source_target_pairs={{2,0},{3,1},{4,2},{5,3},{6,4},{7,5},{8,6},{9,7},{10,8},{11,9},{12,... | collective-permute-start | bytes 1160 | tf_op jit(solution)/shard_map/ppermute | solution.py:25
  192.5 8.5 %collective-permute-start.22 = (f32[3,1,2,16]{1,3,2,0:T(8,128)S(1)}, f32[3,1,2,16]{1,3,2,0:T(8,128)S(1)}, u32[]{:S(2)}, u32[]{:S(2)}) collective-permute-start(f32[3,1,2,16]{1,3,2,0:T(8,128)S(1)} %get-tuple-element.234), channel_id=1, source_target_pairs={{2,0},{3,1},{4,2},{5,3},{6,4},{7,5},{8,6},{9,7},{10,8},{11,9},{12,... | collective-permute-start | bytes 1160 | tf_op jit(solution)/shard_map/ppermute | solution.py:25
  205.2 8.5 %collective-permute-start.24 = (f32[3,1,2,16]{1,3,2,0:T(8,128)S(1)}, f32[3,1,2,16]{1,3,2,0:T(8,128)S(1)}, u32[]{:S(2)}, u32[]{:S(2)}) collective-permute-start(f32[3,1,2,16]{1,3,2,0:T(8,128)S(1)} %get-tuple-element.228), channel_id=1, source_target_pairs={{2,0},{3,1},{4,2},{5,3},{6,4},{7,5},{8,6},{9,7},{10,8},{11,9},{12,... | collective-permute-start | bytes 1160 | tf_op jit(solution)/shard_map/ppermute | solution.py:25
  223.1 9.0 %collective-permute-start.27 = (f32[3,1,2,8]{1,3,2,0:T(8,128)S(1)}, f32[3,1,2,8]{1,3,2,0:T(8,128)S(1)}, u32[]{:S(2)}, u32[]{:S(2)}) collective-permute-start(f32[3,1,2,8]{1,3,2,0:T(8,128)S(1)} %get-tuple-element.302), channel_id=1, source_target_pairs={{4,0},{5,1},{6,2},{7,3},{8,4},{9,5},{10,6},{11,7},{12,8},{13,9},{1... | collective-permute-start | bytes 584 | tf_op jit(solution)/shard_map/ppermute | solution.py:25
  236.0 9.3 %collective-permute-start.29 = (f32[3,1,2,8]{1,3,2,0:T(8,128)S(1)}, f32[3,1,2,8]{1,3,2,0:T(8,128)S(1)}, u32[]{:S(2)}, u32[]{:S(2)}) collective-permute-start(f32[3,1,2,8]{1,3,2,0:T(8,128)S(1)} %get-tuple-element.296), channel_id=1, source_target_pairs={{4,0},{5,1},{6,2},{7,3},{8,4},{9,5},{10,6},{11,7},{12,8},{13,9},{1... | collective-permute-start | bytes 584 | tf_op jit(solution)/shard_map/ppermute | solution.py:25
  249.2 9.3 %collective-permute-start.31 = (f32[3,1,2,8]{1,3,2,0:T(8,128)S(1)}, f32[3,1,2,8]{1,3,2,0:T(8,128)S(1)}, u32[]{:S(2)}, u32[]{:S(2)}) collective-permute-start(f32[3,1,2,8]{1,3,2,0:T(8,128)S(1)} %get-tuple-element.290), channel_id=1, source_target_pairs={{4,0},{5,1},{6,2},{7,3},{8,4},{9,5},{10,6},{11,7},{12,8},{13,9},{1... | collective-permute-start | bytes 584 | tf_op jit(solution)/shard_map/ppermute | solution.py:25
  267.4 10.8 %collective-permute-start.34 = (f32[3,1,2,4]{3,2,1,0:T(2,128)S(1)}, f32[3,1,2,4]{3,2,1,0:T(2,128)S(1)}, u32[]{:S(2)}, u32[]{:S(2)}) collective-permute-start(f32[3,1,2,4]{3,2,1,0:T(2,128)S(1)} %get-tuple-element.336), channel_id=1, source_target_pairs={{8,0},{9,1},{10,2},{11,3},{12,4},{13,5},{14,6},{15,7},{16,8},{17,9... | collective-permute-start | bytes 296 | tf_op jit(solution)/shard_map/ppermute | solution.py:25
  281.8 11.1 %collective-permute-start.36 = (f32[3,1,2,4]{3,2,1,0:T(2,128)S(1)}, f32[3,1,2,4]{3,2,1,0:T(2,128)S(1)}, u32[]{:S(2)}, u32[]{:S(2)}) collective-permute-start(f32[3,1,2,4]{3,2,1,0:T(2,128)S(1)} %get-tuple-element.330), channel_id=1, source_target_pairs={{8,0},{9,1},{10,2},{11,3},{12,4},{13,5},{14,6},{15,7},{16,8},{17,9... | collective-permute-start | bytes 296 | tf_op jit(solution)/shard_map/ppermute | solution.py:25
  297.6 8.8 %collective-permute-start.38 = (f32[3,1,2,8]{1,3,2,0:T(8,128)S(1)}, f32[3,1,2,8]{1,3,2,0:T(8,128)S(1)}, u32[]{:S(2)}, u32[]{:S(2)}) collective-permute-start(f32[3,1,2,8]{1,3,2,0:T(8,128)S(1)} %get-tuple-element.284), channel_id=1, source_target_pairs={{4,0},{5,1},{6,2},{7,3},{8,4},{9,5},{10,6},{11,7},{12,8},{13,9},{1... | collective-permute-start | bytes 584 | tf_op jit(solution)/shard_map/ppermute | solution.py:25
  310.3 9.6 %collective-permute-start.40 = (f32[3,1,2,8]{1,3,2,0:T(8,128)S(1)}, f32[3,1,2,8]{1,3,2,0:T(8,128)S(1)}, u32[]{:S(2)}, u32[]{:S(2)}) collective-permute-start(f32[3,1,2,8]{1,3,2,0:T(8,128)S(1)} %get-tuple-element.278), channel_id=1, source_target_pairs={{4,0},{5,1},{6,2},{7,3},{8,4},{9,5},{10,6},{11,7},{12,8},{13,9},{1... | collective-permute-start | bytes 584 | tf_op jit(solution)/shard_map/ppermute | solution.py:25
  323.8 9.5 %collective-permute-start.42 = (f32[3,1,2,8]{1,3,2,0:T(8,128)S(1)}, f32[3,1,2,8]{1,3,2,0:T(8,128)S(1)}, u32[]{:S(2)}, u32[]{:S(2)}) collective-permute-start(f32[3,1,2,8]{1,3,2,0:T(8,128)S(1)} %get-tuple-element.272), channel_id=1, source_target_pairs={{4,0},{5,1},{6,2},{7,3},{8,4},{9,5},{10,6},{11,7},{12,8},{13,9},{1... | collective-permute-start | bytes 584 | tf_op jit(solution)/shard_map/ppermute | solution.py:25
  337.8 7.9 %collective-permute-start.44 = (f32[3,1,2,16]{1,3,2,0:T(8,128)S(1)}, f32[3,1,2,16]{1,3,2,0:T(8,128)S(1)}, u32[]{:S(2)}, u32[]{:S(2)}) collective-permute-start(f32[3,1,2,16]{1,3,2,0:T(8,128)S(1)} %get-tuple-element.222), channel_id=1, source_target_pairs={{2,0},{3,1},{4,2},{5,3},{6,4},{7,5},{8,6},{9,7},{10,8},{11,9},{12,... | collective-permute-start | bytes 1160 | tf_op jit(solution)/shard_map/ppermute | solution.py:25
  349.9 8.5 %collective-permute-start.46 = (f32[3,1,2,16]{1,3,2,0:T(8,128)S(1)}, f32[3,1,2,16]{1,3,2,0:T(8,128)S(1)}, u32[]{:S(2)}, u32[]{:S(2)}) collective-permute-start(f32[3,1,2,16]{1,3,2,0:T(8,128)S(1)} %get-tuple-element.216), channel_id=1, source_target_pairs={{2,0},{3,1},{4,2},{5,3},{6,4},{7,5},{8,6},{9,7},{10,8},{11,9},{12,... | collective-permute-start | bytes 1160 | tf_op jit(solution)/shard_map/ppermute | solution.py:25
  362.5 8.5 %collective-permute-start.48 = (f32[3,1,2,16]{1,3,2,0:T(8,128)S(1)}, f32[3,1,2,16]{1,3,2,0:T(8,128)S(1)}, u32[]{:S(2)}, u32[]{:S(2)}) collective-permute-start(f32[3,1,2,16]{1,3,2,0:T(8,128)S(1)} %get-tuple-element.210), channel_id=1, source_target_pairs={{2,0},{3,1},{4,2},{5,3},{6,4},{7,5},{8,6},{9,7},{10,8},{11,9},{12,... | collective-permute-start | bytes 1160 | tf_op jit(solution)/shard_map/ppermute | solution.py:25
  375.8 7.9 %collective-permute-start.50 = (f32[3,1,4,32]{3,2,1,0:T(4,128)S(1)}, f32[3,1,4,32]{3,2,1,0:T(4,128)S(1)}, u32[]{:S(2)}, u32[]{:S(2)}) collective-permute-start(f32[3,1,4,32]{3,2,1,0:T(4,128)S(1)} %get-tuple-element.266), channel_id=1, source_target_pairs={{1,0},{2,1},{3,2},{4,3},{5,4},{6,5},{7,6},{8,7},{9,8},{10,9},{11,1... | collective-permute-start | bytes 4616 | tf_op jit(solution)/shard_map/ppermute | solution.py:36
  387.2 7.9 %collective-permute-start.52 = (f32[3,1,4,32]{3,2,1,0:T(4,128)S(1)}, f32[3,1,4,32]{3,2,1,0:T(4,128)S(1)}, u32[]{:S(2)}, u32[]{:S(2)}) collective-permute-start(f32[3,1,4,32]{3,2,1,0:T(4,128)S(1)} %get-tuple-element.260), channel_id=1, source_target_pairs={{1,0},{2,1},{3,2},{4,3},{5,4},{6,5},{7,6},{8,7},{9,8},{10,9},{11,1... | collective-permute-start | bytes 4616 | tf_op jit(solution)/shard_map/ppermute | solution.py:36
  398.7 7.9 %collective-permute-start.54 = (f32[3,1,4,32]{3,2,1,0:T(4,128)S(1)}, f32[3,1,4,32]{3,2,1,0:T(4,128)S(1)}, u32[]{:S(2)}, u32[]{:S(2)}) collective-permute-start(f32[3,1,4,32]{3,2,1,0:T(4,128)S(1)} %get-tuple-element.254), channel_id=1, source_target_pairs={{1,0},{2,1},{3,2},{4,3},{5,4},{6,5},{7,6},{8,7},{9,8},{10,9},{11,1... | collective-permute-start | bytes 4616 | tf_op jit(solution)/shard_map/ppermute | solution.py:36
  410.8 7.9 %collective-permute-start.56 = (f32[3,1,8,64]{3,2,1,0:T(8,128)S(1)}, f32[3,1,8,64]{3,2,1,0:T(8,128)S(1)}, u32[]{:S(2)}, u32[]{:S(2)}) collective-permute-start(f32[3,1,8,64]{3,2,1,0:T(8,128)S(1)} %get-tuple-element.184), channel_id=1, source_target_pairs={{1,0},{2,1},{3,2},{4,3},{5,4},{6,5},{7,6},{8,7},{9,8},{10,9},{11,1... | collective-permute-start | bytes 18440 | tf_op jit(solution)/shard_map/ppermute | solution.py:36
  422.4 7.9 %collective-permute-start.58 = (f32[3,1,8,64]{3,2,1,0:T(8,128)S(1)}, f32[3,1,8,64]{3,2,1,0:T(8,128)S(1)}, u32[]{:S(2)}, u32[]{:S(2)}) collective-permute-start(f32[3,1,8,64]{3,2,1,0:T(8,128)S(1)} %get-tuple-element.178), channel_id=1, source_target_pairs={{1,0},{2,1},{3,2},{4,3},{5,4},{6,5},{7,6},{8,7},{9,8},{10,9},{11,1... | collective-permute-start | bytes 18440 | tf_op jit(solution)/shard_map/ppermute | solution.py:36
  452.2 8.1 %collective-permute-start.62 = (f32[3,1,16,128]{3,2,1,0:T(8,128)S(1)}, f32[3,1,16,128]{3,2,1,0:T(8,128)S(1)}, u32[]{:S(2)}, u32[]{:S(2)}) collective-permute-start(f32[3,1,16,128]{3,2,1,0:T(8,128)S(1)} %get-tuple-element.146), channel_id=1, source_target_pairs={{1,0},{2,1},{3,2},{4,3},{5,4},{6,5},{7,6},{8,7},{9,8},{10,9},{11,1... | collective-permute-start | bytes 73736 | tf_op jit(solution)/shard_map/ppermute | solution.py:36
  476.8 7.9 %collective-permute-start.66 = (f32[3,1,16,128]{3,2,1,0:T(8,128)S(1)}, f32[3,1,16,128]{3,2,1,0:T(8,128)S(1)}, u32[]{:S(2)}, u32[]{:S(2)}) collective-permute-start(f32[3,1,16,128]{3,2,1,0:T(8,128)S(1)} %get-tuple-element.134), channel_id=1, source_target_pairs={{1,0},{2,1},{3,2},{4,3},{5,4},{6,5},{7,6},{8,7},{9,8},{10,9},{11,1... | collective-permute-start | bytes 73736 | tf_op jit(solution)/shard_map/ppermute | solution.py:36
  (515 shorter events, 191.9 us)
Async XLA Ops:
  9.7 11.7 %collective-permute-start = (f32[3,1,16,128]{3,2,1,0:T(8,128)S(1)}, f32[3,1,16,128]{3,2,1,0:T(8,128)S(1)}, u32[]{:S(2)}, u32[]{:S(2)}) collective-permute-start(f32[3,1,16,128]{3,2,1,0:T(8,128)S(1)} %get-tuple-element.163), channel_id=1, source_target_pairs={{0,1},{1,2},{2,3},{3,4},{4,5},{5,6},{6,7},{7,8},{8,9},{9,10},{10,1... | collective-permute-start | bytes 73736 | tf_op jit(solution)/shard_map/ppermute | solution.py:35
  11.7 11.1 %collective-permute-start.1 = (f32[3,1,16,128]{3,2,1,0:T(8,128)S(1)}, f32[3,1,16,128]{3,2,1,0:T(8,128)S(1)}, u32[]{:S(2)}, u32[]{:S(2)}) collective-permute-start(f32[3,1,16,128]{3,2,1,0:T(8,128)S(1)} %get-tuple-element.164), channel_id=1, source_target_pairs={{1,0},{2,1},{3,2},{4,3},{5,4},{6,5},{7,6},{8,7},{9,8},{10,9},{11,1... | collective-permute-start | bytes 73736 | tf_op jit(solution)/shard_map/ppermute | solution.py:36
  23.5 23.6 %collective-permute-start.2 = (f32[3,1,16,128]{3,2,1,0:T(8,128)S(1)}, f32[3,1,16,128]{3,2,1,0:T(8,128)S(1)}, u32[]{:S(2)}, u32[]{:S(2)}) collective-permute-start(f32[3,1,16,128]{3,2,1,0:T(8,128)S(1)} %get-tuple-element.157), channel_id=1, source_target_pairs={{0,1},{1,2},{2,3},{3,4},{4,5},{5,6},{6,7},{7,8},{8,9},{9,10},{10,1... | collective-permute-start | bytes 73736 | tf_op jit(solution)/shard_map/ppermute | solution.py:35
  25.5 21.7 %collective-permute-start.3 = (f32[3,1,16,128]{3,2,1,0:T(8,128)S(1)}, f32[3,1,16,128]{3,2,1,0:T(8,128)S(1)}, u32[]{:S(2)}, u32[]{:S(2)}) collective-permute-start(f32[3,1,16,128]{3,2,1,0:T(8,128)S(1)} %get-tuple-element.158), channel_id=1, source_target_pairs={{1,0},{2,1},{3,2},{4,3},{5,4},{6,5},{7,6},{8,7},{9,8},{10,9},{11,1... | collective-permute-start | bytes 73736 | tf_op jit(solution)/shard_map/ppermute | solution.py:36
  108.4 11.1 %collective-permute-start.8 = (f32[3,1,8,64]{3,2,1,0:T(8,128)S(1)}, f32[3,1,8,64]{3,2,1,0:T(8,128)S(1)}, u32[]{:S(2)}, u32[]{:S(2)}) collective-permute-start(f32[3,1,8,64]{3,2,1,0:T(8,128)S(1)} %get-tuple-element.195), channel_id=1, source_target_pairs={{0,1},{1,2},{2,3},{3,4},{4,5},{5,6},{6,7},{7,8},{8,9},{9,10},{10,1... | collective-permute-start | bytes 18440 | tf_op jit(solution)/shard_map/ppermute | solution.py:35
  120.6 10.4 %collective-permute-start.10 = (f32[3,1,8,64]{3,2,1,0:T(8,128)S(1)}, f32[3,1,8,64]{3,2,1,0:T(8,128)S(1)}, u32[]{:S(2)}, u32[]{:S(2)}) collective-permute-start(f32[3,1,8,64]{3,2,1,0:T(8,128)S(1)} %get-tuple-element.189), channel_id=1, source_target_pairs={{0,1},{1,2},{2,3},{3,4},{4,5},{5,6},{6,7},{7,8},{8,9},{9,10},{10,1... | collective-permute-start | bytes 18440 | tf_op jit(solution)/shard_map/ppermute | solution.py:35
  138.5 10.6 %collective-permute-start.12 = (f32[3,1,4,32]{3,2,1,0:T(4,128)S(1)}, f32[3,1,4,32]{3,2,1,0:T(4,128)S(1)}, u32[]{:S(2)}, u32[]{:S(2)}) collective-permute-start(f32[3,1,4,32]{3,2,1,0:T(4,128)S(1)} %get-tuple-element.319), channel_id=1, source_target_pairs={{0,1},{1,2},{2,3},{3,4},{4,5},{5,6},{6,7},{7,8},{8,9},{9,10},{10,1... | collective-permute-start | bytes 4616 | tf_op jit(solution)/shard_map/ppermute | solution.py:35
  151.5 10.7 %collective-permute-start.14 = (f32[3,1,4,32]{3,2,1,0:T(4,128)S(1)}, f32[3,1,4,32]{3,2,1,0:T(4,128)S(1)}, u32[]{:S(2)}, u32[]{:S(2)}) collective-permute-start(f32[3,1,4,32]{3,2,1,0:T(4,128)S(1)} %get-tuple-element.313), channel_id=1, source_target_pairs={{0,1},{1,2},{2,3},{3,4},{4,5},{5,6},{6,7},{7,8},{8,9},{9,10},{10,1... | collective-permute-start | bytes 4616 | tf_op jit(solution)/shard_map/ppermute | solution.py:35
  178.3 10.4 %collective-permute-start.19 = (f32[3,1,2,16]{1,3,2,0:T(8,128)S(1)}, f32[3,1,2,16]{1,3,2,0:T(8,128)S(1)}, u32[]{:S(2)}, u32[]{:S(2)}) collective-permute-start(f32[3,1,2,16]{1,3,2,0:T(8,128)S(1)} %get-tuple-element.239), channel_id=1, source_target_pairs={{0,2},{1,3},{2,4},{3,5},{4,6},{5,7},{6,8},{7,9},{8,10},{9,11},{10,... | collective-permute-start | bytes 1160 | tf_op jit(solution)/shard_map/ppermute | solution.py:25
  190.6 10.7 %collective-permute-start.21 = (f32[3,1,2,16]{1,3,2,0:T(8,128)S(1)}, f32[3,1,2,16]{1,3,2,0:T(8,128)S(1)}, u32[]{:S(2)}, u32[]{:S(2)}) collective-permute-start(f32[3,1,2,16]{1,3,2,0:T(8,128)S(1)} %get-tuple-element.233), channel_id=1, source_target_pairs={{0,2},{1,3},{2,4},{3,5},{4,6},{5,7},{6,8},{7,9},{8,10},{9,11},{10,... | collective-permute-start | bytes 1160 | tf_op jit(solution)/shard_map/ppermute | solution.py:25
  192.5 10.2 %collective-permute-start.22 = (f32[3,1,2,16]{1,3,2,0:T(8,128)S(1)}, f32[3,1,2,16]{1,3,2,0:T(8,128)S(1)}, u32[]{:S(2)}, u32[]{:S(2)}) collective-permute-start(f32[3,1,2,16]{1,3,2,0:T(8,128)S(1)} %get-tuple-element.234), channel_id=1, source_target_pairs={{2,0},{3,1},{4,2},{5,3},{6,4},{7,5},{8,6},{9,7},{10,8},{11,9},{12,... | collective-permute-start | bytes 1160 | tf_op jit(solution)/shard_map/ppermute | solution.py:25
  203.3 10.5 %collective-permute-start.23 = (f32[3,1,2,16]{1,3,2,0:T(8,128)S(1)}, f32[3,1,2,16]{1,3,2,0:T(8,128)S(1)}, u32[]{:S(2)}, u32[]{:S(2)}) collective-permute-start(f32[3,1,2,16]{1,3,2,0:T(8,128)S(1)} %get-tuple-element.227), channel_id=1, source_target_pairs={{0,2},{1,3},{2,4},{3,5},{4,6},{5,7},{6,8},{7,9},{8,10},{9,11},{10,... | collective-permute-start | bytes 1160 | tf_op jit(solution)/shard_map/ppermute | solution.py:25
  205.2 10.2 %collective-permute-start.24 = (f32[3,1,2,16]{1,3,2,0:T(8,128)S(1)}, f32[3,1,2,16]{1,3,2,0:T(8,128)S(1)}, u32[]{:S(2)}, u32[]{:S(2)}) collective-permute-start(f32[3,1,2,16]{1,3,2,0:T(8,128)S(1)} %get-tuple-element.228), channel_id=1, source_target_pairs={{2,0},{3,1},{4,2},{5,3},{6,4},{7,5},{8,6},{9,7},{10,8},{11,9},{12,... | collective-permute-start | bytes 1160 | tf_op jit(solution)/shard_map/ppermute | solution.py:25
  221.0 11.2 %collective-permute-start.26 = (f32[3,1,2,8]{1,3,2,0:T(8,128)S(1)}, f32[3,1,2,8]{1,3,2,0:T(8,128)S(1)}, u32[]{:S(2)}, u32[]{:S(2)}) collective-permute-start(f32[3,1,2,8]{1,3,2,0:T(8,128)S(1)} %get-tuple-element.301), channel_id=1, source_target_pairs={{0,4},{1,5},{2,6},{3,7},{4,8},{5,9},{6,10},{7,11},{8,12},{9,13},{1... | collective-permute-start | bytes 584 | tf_op jit(solution)/shard_map/ppermute | solution.py:25
  223.1 10.5 %collective-permute-start.27 = (f32[3,1,2,8]{1,3,2,0:T(8,128)S(1)}, f32[3,1,2,8]{1,3,2,0:T(8,128)S(1)}, u32[]{:S(2)}, u32[]{:S(2)}) collective-permute-start(f32[3,1,2,8]{1,3,2,0:T(8,128)S(1)} %get-tuple-element.302), channel_id=1, source_target_pairs={{4,0},{5,1},{6,2},{7,3},{8,4},{9,5},{10,6},{11,7},{12,8},{13,9},{1... | collective-permute-start | bytes 584 | tf_op jit(solution)/shard_map/ppermute | solution.py:25
  234.0 11.4 %collective-permute-start.28 = (f32[3,1,2,8]{1,3,2,0:T(8,128)S(1)}, f32[3,1,2,8]{1,3,2,0:T(8,128)S(1)}, u32[]{:S(2)}, u32[]{:S(2)}) collective-permute-start(f32[3,1,2,8]{1,3,2,0:T(8,128)S(1)} %get-tuple-element.295), channel_id=1, source_target_pairs={{0,4},{1,5},{2,6},{3,7},{4,8},{5,9},{6,10},{7,11},{8,12},{9,13},{1... | collective-permute-start | bytes 584 | tf_op jit(solution)/shard_map/ppermute | solution.py:25
  236.0 10.8 %collective-permute-start.29 = (f32[3,1,2,8]{1,3,2,0:T(8,128)S(1)}, f32[3,1,2,8]{1,3,2,0:T(8,128)S(1)}, u32[]{:S(2)}, u32[]{:S(2)}) collective-permute-start(f32[3,1,2,8]{1,3,2,0:T(8,128)S(1)} %get-tuple-element.296), channel_id=1, source_target_pairs={{4,0},{5,1},{6,2},{7,3},{8,4},{9,5},{10,6},{11,7},{12,8},{13,9},{1... | collective-permute-start | bytes 584 | tf_op jit(solution)/shard_map/ppermute | solution.py:25
  247.2 11.3 %collective-permute-start.30 = (f32[3,1,2,8]{1,3,2,0:T(8,128)S(1)}, f32[3,1,2,8]{1,3,2,0:T(8,128)S(1)}, u32[]{:S(2)}, u32[]{:S(2)}) collective-permute-start(f32[3,1,2,8]{1,3,2,0:T(8,128)S(1)} %get-tuple-element.289), channel_id=1, source_target_pairs={{0,4},{1,5},{2,6},{3,7},{4,8},{5,9},{6,10},{7,11},{8,12},{9,13},{1... | collective-permute-start | bytes 584 | tf_op jit(solution)/shard_map/ppermute | solution.py:25
  249.2 10.8 %collective-permute-start.31 = (f32[3,1,2,8]{1,3,2,0:T(8,128)S(1)}, f32[3,1,2,8]{1,3,2,0:T(8,128)S(1)}, u32[]{:S(2)}, u32[]{:S(2)}) collective-permute-start(f32[3,1,2,8]{1,3,2,0:T(8,128)S(1)} %get-tuple-element.290), channel_id=1, source_target_pairs={{4,0},{5,1},{6,2},{7,3},{8,4},{9,5},{10,6},{11,7},{12,8},{13,9},{1... | collective-permute-start | bytes 584 | tf_op jit(solution)/shard_map/ppermute | solution.py:25
  265.5 12.8 %collective-permute-start.33 = (f32[3,1,2,4]{3,2,1,0:T(2,128)S(1)}, f32[3,1,2,4]{3,2,1,0:T(2,128)S(1)}, u32[]{:S(2)}, u32[]{:S(2)}) collective-permute-start(f32[3,1,2,4]{3,2,1,0:T(2,128)S(1)} %get-tuple-element.335), channel_id=1, source_target_pairs={{0,8},{1,9},{2,10},{3,11},{4,12},{5,13},{6,14},{7,15},{8,16},{9,17... | collective-permute-start | bytes 296 | tf_op jit(solution)/shard_map/ppermute | solution.py:25
  267.4 12.1 %collective-permute-start.34 = (f32[3,1,2,4]{3,2,1,0:T(2,128)S(1)}, f32[3,1,2,4]{3,2,1,0:T(2,128)S(1)}, u32[]{:S(2)}, u32[]{:S(2)}) collective-permute-start(f32[3,1,2,4]{3,2,1,0:T(2,128)S(1)} %get-tuple-element.336), channel_id=1, source_target_pairs={{8,0},{9,1},{10,2},{11,3},{12,4},{13,5},{14,6},{15,7},{16,8},{17,9... | collective-permute-start | bytes 296 | tf_op jit(solution)/shard_map/ppermute | solution.py:25
  279.9 13.0 %collective-permute-start.35 = (f32[3,1,2,4]{3,2,1,0:T(2,128)S(1)}, f32[3,1,2,4]{3,2,1,0:T(2,128)S(1)}, u32[]{:S(2)}, u32[]{:S(2)}) collective-permute-start(f32[3,1,2,4]{3,2,1,0:T(2,128)S(1)} %get-tuple-element.329), channel_id=1, source_target_pairs={{0,8},{1,9},{2,10},{3,11},{4,12},{5,13},{6,14},{7,15},{8,16},{9,17... | collective-permute-start | bytes 296 | tf_op jit(solution)/shard_map/ppermute | solution.py:25
  281.8 12.4 %collective-permute-start.36 = (f32[3,1,2,4]{3,2,1,0:T(2,128)S(1)}, f32[3,1,2,4]{3,2,1,0:T(2,128)S(1)}, u32[]{:S(2)}, u32[]{:S(2)}) collective-permute-start(f32[3,1,2,4]{3,2,1,0:T(2,128)S(1)} %get-tuple-element.330), channel_id=1, source_target_pairs={{8,0},{9,1},{10,2},{11,3},{12,4},{13,5},{14,6},{15,7},{16,8},{17,9... | collective-permute-start | bytes 296 | tf_op jit(solution)/shard_map/ppermute | solution.py:25
  294.8 11.6 %collective-permute-start.37 = (f32[3,1,2,8]{1,3,2,0:T(8,128)S(1)}, f32[3,1,2,8]{1,3,2,0:T(8,128)S(1)}, u32[]{:S(2)}, u32[]{:S(2)}) collective-permute-start(f32[3,1,2,8]{1,3,2,0:T(8,128)S(1)} %get-tuple-element.283), channel_id=1, source_target_pairs={{0,4},{1,5},{2,6},{3,7},{4,8},{5,9},{6,10},{7,11},{8,12},{9,13},{1... | collective-permute-start | bytes 584 | tf_op jit(solution)/shard_map/ppermute | solution.py:25
  297.6 10.4 %collective-permute-start.38 = (f32[3,1,2,8]{1,3,2,0:T(8,128)S(1)}, f32[3,1,2,8]{1,3,2,0:T(8,128)S(1)}, u32[]{:S(2)}, u32[]{:S(2)}) collective-permute-start(f32[3,1,2,8]{1,3,2,0:T(8,128)S(1)} %get-tuple-element.284), channel_id=1, source_target_pairs={{4,0},{5,1},{6,2},{7,3},{8,4},{9,5},{10,6},{11,7},{12,8},{13,9},{1... | collective-permute-start | bytes 584 | tf_op jit(solution)/shard_map/ppermute | solution.py:25
  308.4 11.6 %collective-permute-start.39 = (f32[3,1,2,8]{1,3,2,0:T(8,128)S(1)}, f32[3,1,2,8]{1,3,2,0:T(8,128)S(1)}, u32[]{:S(2)}, u32[]{:S(2)}) collective-permute-start(f32[3,1,2,8]{1,3,2,0:T(8,128)S(1)} %get-tuple-element.277), channel_id=1, source_target_pairs={{0,4},{1,5},{2,6},{3,7},{4,8},{5,9},{6,10},{7,11},{8,12},{9,13},{1... | collective-permute-start | bytes 584 | tf_op jit(solution)/shard_map/ppermute | solution.py:25
  310.3 11.1 %collective-permute-start.40 = (f32[3,1,2,8]{1,3,2,0:T(8,128)S(1)}, f32[3,1,2,8]{1,3,2,0:T(8,128)S(1)}, u32[]{:S(2)}, u32[]{:S(2)}) collective-permute-start(f32[3,1,2,8]{1,3,2,0:T(8,128)S(1)} %get-tuple-element.278), channel_id=1, source_target_pairs={{4,0},{5,1},{6,2},{7,3},{8,4},{9,5},{10,6},{11,7},{12,8},{13,9},{1... | collective-permute-start | bytes 584 | tf_op jit(solution)/shard_map/ppermute | solution.py:25
  321.9 11.5 %collective-permute-start.41 = (f32[3,1,2,8]{1,3,2,0:T(8,128)S(1)}, f32[3,1,2,8]{1,3,2,0:T(8,128)S(1)}, u32[]{:S(2)}, u32[]{:S(2)}) collective-permute-start(f32[3,1,2,8]{1,3,2,0:T(8,128)S(1)} %get-tuple-element.271), channel_id=1, source_target_pairs={{0,4},{1,5},{2,6},{3,7},{4,8},{5,9},{6,10},{7,11},{8,12},{9,13},{1... | collective-permute-start | bytes 584 | tf_op jit(solution)/shard_map/ppermute | solution.py:25
  323.8 11.0 %collective-permute-start.42 = (f32[3,1,2,8]{1,3,2,0:T(8,128)S(1)}, f32[3,1,2,8]{1,3,2,0:T(8,128)S(1)}, u32[]{:S(2)}, u32[]{:S(2)}) collective-permute-start(f32[3,1,2,8]{1,3,2,0:T(8,128)S(1)} %get-tuple-element.272), channel_id=1, source_target_pairs={{4,0},{5,1},{6,2},{7,3},{8,4},{9,5},{10,6},{11,7},{12,8},{13,9},{1... | collective-permute-start | bytes 584 | tf_op jit(solution)/shard_map/ppermute | solution.py:25
  335.6 10.2 %collective-permute-start.43 = (f32[3,1,2,16]{1,3,2,0:T(8,128)S(1)}, f32[3,1,2,16]{1,3,2,0:T(8,128)S(1)}, u32[]{:S(2)}, u32[]{:S(2)}) collective-permute-start(f32[3,1,2,16]{1,3,2,0:T(8,128)S(1)} %get-tuple-element.221), channel_id=1, source_target_pairs={{0,2},{1,3},{2,4},{3,5},{4,6},{5,7},{6,8},{7,9},{8,10},{9,11},{10,... | collective-permute-start | bytes 1160 | tf_op jit(solution)/shard_map/ppermute | solution.py:25
  348.0 10.5 %collective-permute-start.45 = (f32[3,1,2,16]{1,3,2,0:T(8,128)S(1)}, f32[3,1,2,16]{1,3,2,0:T(8,128)S(1)}, u32[]{:S(2)}, u32[]{:S(2)}) collective-permute-start(f32[3,1,2,16]{1,3,2,0:T(8,128)S(1)} %get-tuple-element.215), channel_id=1, source_target_pairs={{0,2},{1,3},{2,4},{3,5},{4,6},{5,7},{6,8},{7,9},{8,10},{9,11},{10,... | collective-permute-start | bytes 1160 | tf_op jit(solution)/shard_map/ppermute | solution.py:25
  360.6 10.5 %collective-permute-start.47 = (f32[3,1,2,16]{1,3,2,0:T(8,128)S(1)}, f32[3,1,2,16]{1,3,2,0:T(8,128)S(1)}, u32[]{:S(2)}, u32[]{:S(2)}) collective-permute-start(f32[3,1,2,16]{1,3,2,0:T(8,128)S(1)} %get-tuple-element.209), channel_id=1, source_target_pairs={{0,2},{1,3},{2,4},{3,5},{4,6},{5,7},{6,8},{7,9},{8,10},{9,11},{10,... | collective-permute-start | bytes 1160 | tf_op jit(solution)/shard_map/ppermute | solution.py:25
  (52 other events, 875.1 us)
where the time goes:
time: 490 us; the launch traced here: 488 us
  starting transfers between devices  334 us (68%)
  local copies, waits for them, and re-layouts  58.8 us (12%)
  waiting for transfers between devices  50 us (10%)
  other arithmetic  42.3 us (9%)
    ppermute x28, starting transfers between devices, passed_along(): return lax.ppermute(block, axis, route)  155 us
    ppermute x18, starting transfers between devices, with_halo(): after = lax.ppermute(first, axis, down)  143 us
    ppermute x18, starting transfers between devices, with_halo(): before = lax.ppermute(last, axis, up)  34.5 us
    reshape x3, local copies, waits for them, and re-layouts, coarsen(): values.reshape(c, z // 2, 2, h // 2, 2, y // 2, 2)  30.9 us
    ppermute x28, waiting for transfers between devices, passed_along(): return lax.ppermute(block, axis, route)  20.8 us
    ppermute x18, waiting for transfers between devices, with_halo(): after = lax.ppermute(first, axis, down)  19.3 us
    reduce_sum x7, other arithmetic, coarsen(): jnp.mean(values.reshape(c, z // 2, 2, h // 2, 2, y // 2, 2), axis=(2, 4, 6))  14.8 us
  transfers between devices with their start and end apart: 67, of which 36 were waited for; matrix products, arithmetic and copies ran while one was open for 4% of the time, Pallas kernels for 0%

commit v1 on v0

v1 whole, which is shorter than its diff:
```python
import jax
import jax.numpy as jnp
from jax import lax
from jax.experimental import pallas as pl
from jax.experimental.pallas import tpu as pltpu
from jax.sharding import PartitionSpec as P

F32 = jnp.float32
center = 26.5 / 27.0
cheb_mid = 1.65
cheb_half = 1.35
sigma = cheb_mid / cheb_half
kappa = (0.75, 0.75, 1.5)
HALO = 10
EXT = 16 + 2 * HALO


def cheb_pairs():
    rho, out = 1.0 / sigma, []
    for _ in range(2):
        new = 1.0 / (2.0 * sigma - rho)
        out.append((new * rho, 2.0 * new / cheb_half))
        rho = new
    return out


(A1, C1), (A2, C2) = cheb_pairs()
INV_MID = 1.0 / cheb_mid


def iota(shape, axis):
    return lax.broadcasted_iota(jnp.int32, shape, axis)


def lane_sum(s, step, period):
    axis = s.ndim - 1
    lane = iota(s.shape, axis) & (period - 1)
    before = jnp.where(lane >= step, pltpu.roll(s, step, axis), 0.0)
    after = jnp.where(lane < period - step, pltpu.roll(s, 128 - step, axis), 0.0)
    return s + before + after


def row_sum(s):
    axis = s.ndim - 2
    n = s.shape[axis]
    row = iota(s.shape, axis)
    before = jnp.where(row >= 1, pltpu.roll(s, 1, axis), 0.0)
    after = jnp.where(row < n - 1, pltpu.roll(s, n - 1, axis), 0.0)
    return s + before + after


def lane_pair(s, step):
    axis = s.ndim - 1
    upper = (iota(s.shape, axis) & step) != 0
    return s + jnp.where(upper, pltpu.roll(s, step, axis), pltpu.roll(s, 128 - step, axis))


def safe(root):
    return jnp.where(root > 0.0, root, 1.0)


def solid_lanes(occ_ref, rows):
    lane = iota((rows, 128), 1) >> 4
    out = jnp.zeros((rows, 128), F32)
    for k in range(8):
        out = jnp.where(lane == k, occ_ref[0, 0, k].astype(F32), out)
    return out


def pack_kernel(load_ref, class_ref, occ_ref, moduli_ref, x_ref, o_ref, root_ref):
    odd = lax.axis_index("bricks") & 1

    def fill(z, _):
        cls = class_ref[z]
        modulus = jnp.zeros(cls.shape, F32)
        for k in range(8):
            modulus = jnp.where(cls == k, moduli_ref[k], modulus)
        root_ref[z] = jnp.sqrt(modulus)
        return 0

    lax.fori_loop(0, 16, fill, 0, unroll=4)
    solid = solid_lanes(occ_ref, 16)
    x_ref[37] = solid
    o_ref[37] = solid
    for ref, first in ((x_ref, (1 - odd)), (o_ref, odd)):
        for c in range(3):
            for j in range(9):
                ref[c * 9 + j] = load_ref[c, first * 7 + j]
        for j in range(10):
            ref[27 + j] = root_ref[first * 6 + j]


def down_kernel(
    load_ref, root_own_ref, occ_ref, x_ref, o_ref,
    msg_ref, edge_ref, v0_ref, beta0_ref, root0_ref, v1_ref, beta1_ref, root1_ref, sol_ref,
    b_s, va_s, d_s, sol_s, t_s, tr_s,
):
    odd = lax.axis_index("bricks") & 1
    is_odd = odd == 1

    def left(k):
        return jnp.where(is_odd, x_ref[k], o_ref[k])

    def right(k):
        return jnp.where(is_odd, o_ref[k], x_ref[k])

    own_solid = solid_lanes(occ_ref, 16)
    left_solid, right_solid = left(37), right(37)
    sol_ref[...] = jnp.zeros((8, 128), F32)
    sol_ref[0:1, :] = left_solid[:1]
    sol_ref[1:2, :] = own_solid[:1]
    sol_ref[2:3, :] = right_solid[:1]
    for j in range(HALO):
        sol_s[j] = left_solid
        sol_s[26 + j] = right_solid
        root0_ref[j] = safe(left(27 + j))
        root0_ref[26 + j] = safe(right(27 + j))

    def own(z, _):
        sol_s[z + HALO] = own_solid
        root0_ref[z + HALO] = root_own_ref[z]
        return 0

    lax.fori_loop(0, 16, own, 0, unroll=4)

    def start(e, b0, b1, b2):
        s = b0 + b1 + b2
        third = s * (1.0 / 3.0)
        scale = sol_s[e] / (center * root0_ref[e])
        for c, p in enumerate((b0 - third, b1 - third, s)):
            b_s[c, e] = p
            beta = p * scale
            beta0_ref[c, e] = beta
            va_s[c, e] = beta * INV_MID

    for j in range(9):
        start(1 + j, left(j), left(9 + j), left(18 + j))
        start(26 + j, right(j), right(9 + j), right(18 + j))

    def own_start(z, _):
        start(z + HALO, load_ref[0, z], load_ref[1, z], load_ref[2, z])
        return 0

    lax.fori_loop(0, 16, own_start, 0, unroll=2)

    def stencil(ref, c, e):
        mid = ref[c, e]
        s = ref[c, e - 1] + mid + ref[c, e + 1]
        return mid, 27.5 * mid - lane_sum(row_sum(s), 1, 128)

    def app1(e, _):
        sol = sol_s[e]
        for c in range(3):
            v, t = stencil(va_s, c, e)
            pre = beta0_ref[c, e] - (sol * (kappa[c] / 26.5)) * t
            d = A1 * v + C1 * pre
            d_s[c, e] = d
            v0_ref[c, e] = v + d
        return 0

    lax.fori_loop(2, 34, app1, 0, unroll=2)

    def app2(e, _):
        sol = sol_s[e]
        for c in range(3):
            v, t = stencil(v0_ref, c, e)
            pre = beta0_ref[c, e] - (sol * (kappa[c] / 26.5)) * t
            va_s[c, e] = v + A2 * d_s[c, e] + C2 * pre
        return 0

    lax.fori_loop(3, 33, app2, 0, unroll=2)

    def resid(k, _):
        e = 4 + 2 * k
        for c in range(3):
            total = None
            for j in range(2):
                v, t = stencil(va_s, c, e + j)
                v0_ref[c, e + j] = v
                r = b_s[c, e + j] - (sol_s[e + j] * root0_ref[e + j]) * (kappa[c] / 27.0) * t
                total = r if total is None else total + r
            t_s[c, k] = total
        return 0

    lax.fori_loop(0, 14, resid, 0)

    def root_pair(k, _):
        tr_s[k] = root0_ref[2 * k] + root0_ref[2 * k + 1]
        return 0

    lax.fori_loop(0, 18, root_pair, 0, unroll=2)

    root1 = lane_pair(tr_s[:, pl.ds(0, 8, 2), :] + tr_s[:, pl.ds(1, 8, 2), :], 1) * 0.125
    root1_ref[...] = root1
    rt = root1[2:16]
    sol = jnp.concatenate(
        [
            jnp.broadcast_to(left_solid[None, :8], (3, 8, 128)),
            jnp.broadcast_to(own_solid[None, :8], (8, 8, 128)),
            jnp.broadcast_to(right_solid[None, :8], (3, 8, 128)),
        ],
        axis=0,
    )
    scale1 = sol / (0.25 * center * rt)
    zero = jnp.zeros((1, 8, 128), F32)

    def stencil1(v):
        before = jnp.concatenate([zero, v[:-1]], axis=0)
        after = jnp.concatenate([v[1:], zero], axis=0)
        return 27.5 * v - lane_sum(row_sum(before + v + after), 2, 128)

    gather = 4 * (iota((8, 128), 1) & 31)
    group = (iota((8, 128), 1) >> 5) == (iota((8, 128), 0) >> 1)

    def compact(q):
        q = q + pltpu.roll(q, 126, 1)
        q = jnp.take_along_axis(q, gather, axis=1)
        return jnp.sum(jnp.where(group, q, 0.0), axis=0, keepdims=True) * 0.125

    for c in range(3):
        b1 = lane_pair(t_s[c, :, pl.ds(0, 8, 2), :] + t_s[c, :, pl.ds(1, 8, 2), :], 1) * 0.125
        beta = b1 * scale1
        m = sol * (kappa[c] / 26.5)
        v = beta * INV_MID
        d = A1 * v + C1 * (beta - m * stencil1(v))
        v = v + d
        d = A2 * d + C2 * (beta - m * stencil1(v))
        v = v + d
        v1_ref[c] = v
        beta1_ref[c] = beta
        r = (b1 - (sol * rt) * (0.25 * kappa[c] / 27.0) * stencil1(v))[3:11]
        for z in range(4):
            msg_ref[4 * c + z : 4 * c + z + 1, :] = compact(r[2 * z] + r[2 * z + 1])
        for j in range(4):
            to_after, to_before = v[6 + j], v[4 + j]
            k = 8 * (4 * c + j)
            msg_ref[24 + k : 32 + k, :] = jnp.where(is_odd, to_before, to_after)
            edge_ref[k : k + 8, :] = jnp.where(is_odd, to_after, to_before)
        to_after, to_before = beta[7], beta[6]
        k = 8 * (12 + c)
        msg_ref[24 + k : 32 + k, :] = jnp.where(is_odd, to_before, to_after)
        edge_ref[k : k + 8, :] = jnp.where(is_odd, to_after, to_before)
    for z in range(4):
        msg_ref[12 + z : 13 + z, :] = compact(root1[5 + 2 * z] + root1[6 + 2 * z])
    msg_ref[16:24, :] = jnp.take_along_axis(own_solid[:8], gather, axis=1)


def up_kernel(
    row_ref, far_ref, far2_ref, msg_in_ref, edge_in_ref,
    v0_ref, beta0_ref, root0_ref, v1_ref, beta1_ref, root1_ref, sol_ref,
    out_ref,
    all_s, w_s, f_s, e2_s, pe_s, a_s, bb_s, d_s,
):
    me = lax.axis_index("bricks")
    odd = me & 1
    is_odd = odd == 1

    for t in range(16):
        rows = slice(24 * t, 24 * t + 24)
        far, far2 = far_ref[rows, :], far2_ref[rows, :]
        all_s[t] = jnp.where(is_odd, far2, far)
        all_s[16 + t] = row_ref[rows, :]
        all_s[32 + t] = jnp.where(is_odd, far, far2)
    base = me - odd - 16
    here = me & 15
    other = here ^ 1
    order_left = jnp.where(is_odd, here, other)
    order_right = jnp.where(is_odd, other, here)
    for w in range(34):
        dev = base + w
        rel = (dev >> 4) - (me >> 4)
        order = jnp.where(rel == 0, here, jnp.where(rel < 0, order_left, order_right))
        x = (dev & 15) ^ order
        slot = (rel + 1) * 16 + (x ^ ((x & 8) >> 1))
        for c in range(4):
            w_s[c, 4 * w : 4 * w + 4, :] = all_s[slot, 4 * c : 4 * c + 4, :]
        w_s[4, 4 * w : 4 * w + 4, :] = all_s[slot, 16:20, :]

    def stencil(v, level):
        n = v.shape[0]
        s = v + pltpu.roll(v, 1, 0) + pltpu.roll(v, n - 1, 0)
        if level == 2:
            lane = iota(s.shape, 1)
            s = (
                s
                + jnp.where(lane >= 32, pltpu.roll(s, 32, 1), 0.0)
                + jnp.where(lane < 96, pltpu.roll(s, 96, 1), 0.0)
            )
        else:
            s = s + pltpu.roll(s, 64, 1)
        return 27.5 * v - lane_sum(s, 2 ** (level - 2), 32)

    def first(beta, m, level):
        v = beta * INV_MID
        d = A1 * v + C1 * (beta - m * stencil(v, level))
        v = v + d
        d = A2 * d + C2 * (beta - m * stencil(v, level))
        return v + d

    def again(v, beta, m, level):
        d = INV_MID * (beta - m * stencil(v, level))
        v = v + d
        d = A1 * d + C1 * (beta - m * stencil(v, level))
        v = v + d
        d = A2 * d + C2 * (beta - m * stencil(v, level))
        return v + d

    def coarsen(values, level):
        n = values.shape[0]
        half = (n // 2 + 7) // 8 * 8
        if 2 * half > n:
            f_s[n : 2 * half, :] = jnp.zeros((2 * half - n, 128), F32)
        f_s[0:n, :] = values
        s = f_s[pl.ds(0, half, 2), :] + f_s[pl.ds(1, half, 2), :]
        s = lane_pair(s, 2 ** (level - 2))
        if level == 2:
            return lane_pair(s, 32) * 0.125
        return s * 0.25

    def refine(values, first_row, count):
        n = values.shape[0]
        f_s[pl.ds(0, n, 2), :] = values
        f_s[pl.ds(1, n, 2), :] = values
        return f_s[first_row : first_row + count, :]

    roots = {2: safe(w_s[3])}
    sols = {2: w_s[4]}
    for level in (2, 3, 4):
        roots[level + 1] = safe(coarsen(roots[level], level))
        sols[level + 1] = coarsen(sols[level], level)

    def beta_scale(level):
        sol = sols[level]
        sol = sol * sol if level == 5 else sol
        return sol / (0.25**level * center * roots[level])

    def mask(level):
        sol = sols[level]
        return sol * sol * sol if level == 5 else sol

    scales = {level: beta_scale(level) for level in (2, 3, 4, 5)}
    masks = {level: mask(level) for level in (2, 3, 4, 5)}
    g5 = jnp.where(sols[5] > 0.0, 1.0 / (roots[5] * jnp.where(sols[5] > 0.0, sols[5], 1.0)), 0.0)
    windows = {4: (0, 40), 3: (24, 48), 2: (56, 80)}

    for c in range(3):
        b = w_s[c]
        betas, vs = {}, {}
        for level in (2, 3, 4):
            beta = b * scales[level]
            v = first(beta, masks[level] * (kappa[c] / 26.5), level)
            r = b - (sols[level] * roots[level]) * (0.25**level * kappa[c] / 27.0) * stencil(v, level)
            betas[level], vs[level] = beta, v
            b = coarsen(r, level)
        e = first(b * scales[5], masks[5] * (kappa[c] / 26.5), 5) * g5
        first_row = 0
        for level in (4, 3, 2):
            lo, hi = windows[level]
            e = refine(e, lo - first_row, hi - lo)
            root, sol = roots[level][lo:hi], sols[level][lo:hi]
            v = vs[level][lo:hi] + (root * sol) * e
            v = again(v, betas[level][lo:hi], masks[level][lo:hi] * (kappa[c] / 26.5), level)
            e = jnp.where(sol > 0.0, v / root, e)
            first_row = 2 * lo
        e2_s[c] = e

    rows = {}
    for k, name in enumerate(("left", "own", "right")):
        rows[name] = sol_ref[k : k + 1, :]

    def layers(name, n):
        return jnp.broadcast_to(rows[name][None], (n, 8, 128))

    sol = jnp.concatenate([layers("left", 5), layers("own", 8), layers("right", 5)], axis=0)
    root1 = root1_ref[...]
    spread = (iota((8, 128), 0) >> 1) * 32 + (iota((8, 128), 1) >> 2)
    zero = jnp.zeros((1, 8, 128), F32)

    def stencil1(v):
        before = jnp.concatenate([zero, v[:-1]], axis=0)
        after = jnp.concatenate([v[1:], zero], axis=0)
        return 27.5 * v - lane_sum(row_sum(before + v + after), 2, 128)

    def from_left(k):
        return jnp.where(is_odd, msg_in_ref[24 + 8 * k : 32 + 8 * k, :], edge_in_ref[8 * k : 8 * k + 8, :])[None]

    def from_right(k):
        return jnp.where(is_odd, edge_in_ref[8 * k : 8 * k + 8, :], msg_in_ref[24 + 8 * k : 32 + 8 * k, :])[None]

    for c in range(3):
        v = jnp.concatenate(
            [from_left(4 * c + j) for j in range(4)]
            + [v1_ref[c][2:12]]
            + [from_right(4 * c + j) for j in range(4)],
            axis=0,
        )
        beta = jnp.concatenate([zero, from_left(12 + c), beta1_ref[c], from_right(12 + c), zero], axis=0)
        slabs = []
        for j in range(10):
            row = e2_s[c, pl.ds(5 + 4 * odd + j, 1), :]
            slab = jnp.take_along_axis(jnp.broadcast_to(row, (8, 128)), spread, axis=1)[None]
            slabs += [slab, slab]
        e = jnp.concatenate(slabs[1:19], axis=0)
        m = sol * (kappa[c] / 26.5)
        v = v + (root1 * sol) * e
        d = INV_MID * (beta - m * stencil1(v))
        v = v + d
        d = A1 * d + C1 * (beta - m * stencil1(v))
        v = v + d
        d = A2 * d + C2 * (beta - m * stencil1(v))
        v = v + d
        e = jnp.where(sol > 0.0, v / root1, e)[3:15]
        pe_s[c, :, pl.ds(0, 8, 2), :] = e
        pe_s[c, :, pl.ds(1, 8, 2), :] = e

    shift = HALO - 4

    def sol0(k):
        row = jnp.where(k < 4, rows["left"], jnp.where(k < 20, rows["own"], rows["right"]))
        return jnp.broadcast_to(row, (16, 128))

    def begin(k, _):
        g = root0_ref[k + shift] * sol0(k)
        for c in range(3):
            a_s[c, k] = v0_ref[c, k + shift] + g * pe_s[c, k >> 1]
        return 0

    lax.fori_loop(1, 23, begin, 0, unroll=2)

    def stencil0(ref, c, k):
        mid = ref[c, k]
        s = ref[c, k - 1] + mid + ref[c, k + 1]
        return mid, 27.5 * mid - lane_sum(row_sum(s), 1, 128)

    def app0(k, _):
        sol = sol0(k)
        for c in range(3):
            v, t = stencil0(a_s, c, k)
            d = INV_MID * (beta0_ref[c, k + shift] - (sol * (kappa[c] / 26.5)) * t)
            d_s[c, k] = d
            bb_s[c, k] = v + d
        return 0

    lax.fori_loop(2, 22, app0, 0, unroll=2)

    def app1(k, _):
        sol = sol0(k)
        for c in range(3):
            v, t = stencil0(bb_s, c, k)
            pre = beta0_ref[c, k + shift] - (sol * (kappa[c] / 26.5)) * t
            d = A1 * d_s[c, k] + C1 * pre
            d_s[c, k] = d
            a_s[c, k] = v + d
        return 0

    lax.fori_loop(3, 21, app1, 0, unroll=2)
    own_solid = jnp.broadcast_to(rows["own"], (16, 128))

    def app2(k, _):
        inverse = 1.0 / root0_ref[k + shift]
        x = []
        for c in range(3):
            v, t = stencil0(a_s, c, k)
            pre = beta0_ref[c, k + shift] - (own_solid * (kappa[c] / 26.5)) * t
            v = v + A2 * d_s[c, k] + C2 * pre
            x.append(jnp.where(own_solid > 0.0, v * inverse, pe_s[c, k >> 1]))
        third = x[2] * (1.0 / 3.0)
        out_ref[0, k - 4] = x[0] + third
        out_ref[1, k - 4] = x[1] + third
        out_ref[2, k - 4] = third - x[0] - x[1]
        return 0

    lax.fori_loop(4, 20, app2, 0, unroll=2)


VMEM = pl.BlockSpec(memory_space=pltpu.VMEM)
SMEM = pl.BlockSpec(memory_space=pltpu.SMEM)
PARAMS = pltpu.CompilerParams(vmem_limit_bytes=40 * 2**20)


def shaped(*shape):
    return jax.ShapeDtypeStruct(shape, F32)


def swap_bits(values, bits):
    n = lax.axis_size("bricks")
    return lax.ppermute(values, "bricks", [(i, i ^ bits) for i in range(n)])


def swap_before(values, distance):
    n = lax.axis_size("bricks")
    pairs = []
    for i in range(0, n, 2):
        if i - distance >= 0:
            pairs += [(i, i - distance), (i - distance, i)]
    return lax.ppermute(values, "bricks", sorted(pairs))


def body(load_field, material_class, occupancy, moduli):
    x_msg, o_msg, root = pl.pallas_call(
        pack_kernel,
        out_shape=(shaped(38, 16, 128), shaped(38, 16, 128), shaped(16, 16, 128)),
        in_specs=[VMEM, VMEM, SMEM, SMEM],
        out_specs=(VMEM, VMEM, VMEM),
        compiler_params=PARAMS,
        name="pack",
    )(load_field, material_class, occupancy, moduli)
    x_in = swap_bits(x_msg, 1)
    o_in = swap_before(o_msg, 1)
    msg, edge, *fine = pl.pallas_call(
        down_kernel,
        out_shape=(
            shaped(144, 128), shaped(120, 128),
            shaped(3, EXT, 16, 128), shaped(3, EXT, 16, 128), shaped(EXT, 16, 128),
            shaped(3, 14, 8, 128), shaped(3, 14, 8, 128), shaped(18, 8, 128), shaped(8, 128),
        ),
        in_specs=[VMEM, VMEM, SMEM, VMEM, VMEM],
        out_specs=(VMEM,) * 9,
        scratch_shapes=[
            pltpu.VMEM((3, EXT, 16, 128), F32),
            pltpu.VMEM((3, EXT, 16, 128), F32),
            pltpu.VMEM((3, EXT, 16, 128), F32),
            pltpu.VMEM((EXT, 16, 128), F32),
            pltpu.VMEM((3, 14, 16, 128), F32),
            pltpu.VMEM((18, 16, 128), F32),
        ],
        compiler_params=PARAMS,
        name="down",
    )(load_field, root, occupancy, x_in, o_in)
    msg_in = swap_bits(msg, 1)
    edge_in = swap_before(edge, 1)
    row = jnp.concatenate([msg[:24], msg_in[:24]], axis=0)
    for bits in (2, 4, 12):
        row = jnp.concatenate([row, swap_bits(row, bits)], axis=0)
    far = swap_before(row, 15)
    far2 = swap_bits(far, 1)
    return pl.pallas_call(
        up_kernel,
        out_shape=shaped(3, 16, 16, 128),
        in_specs=[VMEM] * 12,
        out_specs=VMEM,
        scratch_shapes=[
            pltpu.VMEM((48, 24, 128), F32),
            pltpu.VMEM((5, 136, 128), F32),
            pltpu.VMEM((144, 128), F32),
            pltpu.VMEM((3, 24, 128), F32),
            pltpu.VMEM((3, 12, 16, 128), F32),
            pltpu.VMEM((3, 24, 16, 128), F32),
            pltpu.VMEM((3, 24, 16, 128), F32),
            pltpu.VMEM((3, 24, 16, 128), F32),
        ],
        compiler_params=PARAMS,
        name="up",
    )(row, far, far2, msg_in, edge_in, *fine)


def solution(mesh):
    in_specs = (
        P(None, "bricks", None, None),
        P("bricks", None, None),
        P("bricks", None, None),
        P(),
    )
    out_specs = P(None, "bricks", None, None)
    return jax.shard_map(body, mesh=mesh, in_specs=in_specs, out_specs=out_specs, check_vma=False)
```

time: 490 us -> 76.2 us (0.16)
  starting transfers between devices: 334 us -> 19.4 us
  local copies, waits for them, and re-layouts: 58.8 us -> 3.23 us
  other arithmetic: 42.3 us -> 0.02 us
  Pallas kernels: 0 us -> 22 us
  waiting for transfers between devices: 50 us -> 31.3 us
    ppermute x67 -> x9, starting transfers between devices: 334 us -> 19.4 us  [the longest x3 18.1 us: swap_before(): return lax.ppermute(values, 'bricks', sorted(pairs))]
    reshape x17 -> x0, local copies, waits for them, and re-layouts: 36 us -> none  [the longest x3 30.9 us: coarsen(): values.reshape(c, z // 2, 2, h // 2, 2, y // 2, 2)]
    pallas_call x0 -> x3, Pallas kernels: none -> 22 us  [the longest x1 14.5 us: body(): pl.pallas_call(up_kernel, out_shape=shaped(3, 16, 16, 128), in_specs=[VME...]
    reduce_sum x45 -> x0, other arithmetic: 19.9 us -> none  [the longest x7 14.8 us: coarsen(): jnp.mean(values.reshape(c, z // 2, 2, h // 2, 2, y // 2, 2), axis=(2, 4, 6))]
    ppermute x67 -> x9, waiting for transfers between devices: 50 us -> 31.3 us  [the longest x6 15.8 us: swap_bits(): return lax.ppermute(values, 'bricks', [(i, i ^ bits) for i in range(n)])]
    another operation x1 -> x0, local copies, waits for them, and re-layouts: 9.79 us -> none  [coarsen(): values.reshape(c, z // 2, 2, h // 2, 2, y // 2, 2)]
    mul x78 -> x0, other arithmetic: 8.74 us -> none  [the longest x19 7.23 us: operator_fn(): padded = with_halo(u * (root * solid), (('bricks', 1),), 1)]
    div x9 -> x0, other arithmetic: 6.15 us -> none  [the longest x1 6.11 us: smooth(): inv_diag = solid / (factor * center * root * root)]
  transfers between devices with their start and end apart: 67 -> 9, of which waited for: 36 -> 7; matrix products, arithmetic and copies ran while one was open for 4% -> 0% of each run, Pallas kernels for 0% -> 0%
where the time goes in v1:
time: 76.2 us; the launch traced here: 76 us
  waiting for transfers between devices  31.3 us (41%)
  Pallas kernels  22 us (29%)
  starting transfers between devices  19.4 us (25%)
  local copies, waits for them, and re-layouts  3.23 us (4%)
    ppermute x3, starting transfers between devices, swap_before(): return lax.ppermute(values, 'bricks', sorted(pairs))  18.1 us
    ppermute x6, waiting for transfers between devices, swap_bits(): return lax.ppermute(values, 'bricks', [(i, i ^ bits) for i in range(n)])  15.8 us
    ppermute x3, waiting for transfers between devices, swap_before(): return lax.ppermute(values, 'bricks', sorted(pairs))  15.5 us
    pallas_call x1, Pallas kernels, body(): pl.pallas_call(up_kernel, out_shape=shaped(3, 16, 16, 128), in_specs=[VME...  14.5 us
    pallas_call x1, Pallas kernels, body(): pl.pallas_call(down_kernel, out_shape=(shaped(144, 128), shaped(120, 128)...  6.76 us
    unnamed x10, local copies, waits for them, and re-layouts  3.22 us
  transfers between devices with their start and end apart: 9, of which 7 were waited for; matrix products, arithmetic and copies ran while one was open for 0% of the time, Pallas kernels for 0%

profile of v1, /device:TPU:24, one launch (start us, length us, event | category | flops | bytes accessed | tf_op | source)
XLA Modules:
  0.0 76.0 jit_solution(16834214087432165723)
XLA Ops:
  0.0 0.0 copy-start
  0.0 1.0 %copy-done = f32[3,16,16,128]{3,2,1,0:T(8,128)S(1)} copy-done((f32[3,16,16,128]{3,2,1,0:T(8,128)S(1)}, f32[3,16,16,128]{3,2,1,0:T(8,128)}, u32[]{:S(2)}) %copy-start) | copy-done | bytes 393240
  1.0 0.0 copy-start.1
  1.0 0.9 %copy-done.1 = s32[16,16,128]{2,1,0:T(8,128)S(1)} copy-done((s32[16,16,128]{2,1,0:T(8,128)S(1)}, s32[16,16,128]{2,1,0:T(8,128)}, u32[]{:S(2)}) %copy-start.1) | copy-done | bytes 131096
  1.9 0.0 copy-start.2
  1.9 0.7 copy-done.2
  2.6 0.0 copy-start.3
  2.6 0.7 copy-done.3
  3.2 0.7 pack.1
  3.9 0.1 collective-permute-start
  4.0 10.2 %collective-permute-start.1 = (f32[38,16,128]{2,1,0:T(8,128)S(1)}, f32[38,16,128]{2,1,0:T(8,128)S(1)}, u32[]{:S(2)}, u32[]{:S(2)}) collective-permute-start(f32[38,16,128]{2,1,0:T(8,128)S(1)} %get-tuple-element.19), channel_id=1, source_target_pairs={{1,2},{2,1},{3,4},{4,3},{5,6},{6,5},{7,8},{8,7},{9,10},{10,9},{11,... | collective-permute-start | bytes 933896 | tf_op jit(solution)/shard_map/ppermute | solution.py:496
  14.3 0.0 collective-permute-done.x_ref
  14.3 4.6 %collective-permute-done.1.o_ref = f32[38,16,128]{2,1,0:T(8,128)S(1)} collective-permute-done((f32[38,16,128]{2,1,0:T(8,128)S(1)}, f32[38,16,128]{2,1,0:T(8,128)S(1)}, u32[]{:S(2)}, u32[]{:S(2)}) %collective-permute-start.1) | collective-permute-done | bytes 311328 | tf_op jit(solution)/shard_map/ppermute | solution.py:496
  18.8 6.8 %down.1 = (f32[144,128]{1,0:T(8,128)S(1)}, f32[120,128]{1,0:T(8,128)S(1)}, f32[3,36,16,128]{3,2,1,0:T(8,128)S(1)}, f32[3,36,16,128]{3,2,1,0:T(8,128)S(1)}, f32[3...) custom-call(f32[3,16,16,128]{3,2,1,0:T(8,128)S(1)} %copy-done, ...), custom_call_target="tpu_custom_call" | custom-call | tf_op jit(solution)/shard_map/down/pallas_call | solution.py:510
  25.6 0.1 collective-permute-start.2
  25.7 1.2 %collective-permute-done.2.msg_in_ref = f32[144,128]{1,0:T(8,128)S(1)} collective-permute-done((f32[144,128]{1,0:T(8,128)S(1)}, f32[144,128]{1,0:T(8,128)S(1)}, u32[]{:S(2)}, u32[]{:S(2)}) %collective-permute-start.2) | collective-permute-done | bytes 73760 | tf_op jit(solution)/shard_map/ppermute | solution.py:487
  27.0 0.0 collective-permute-start.3
  27.0 3.8 %collective-permute-done.3 = f32[48,128]{1,0:T(8,128)S(1)} collective-permute-done((f32[48,128]{1,0:T(8,128)S(1)}, f32[48,128]{1,0:T(8,128)S(1)}, u32[]{:S(2)}, u32[]{:S(2)}) %collective-permute-start.3) | collective-permute-done | bytes 24608 | tf_op jit(solution)/shard_map/ppermute | solution.py:487
  30.8 0.0 collective-permute-start.4
  30.8 5.0 %collective-permute-done.4 = f32[96,128]{1,0:T(8,128)S(1)} collective-permute-done((f32[96,128]{1,0:T(8,128)S(1)}, f32[96,128]{1,0:T(8,128)S(1)}, u32[]{:S(2)}, u32[]{:S(2)}) %collective-permute-start.4) | collective-permute-done | bytes 49184 | tf_op jit(solution)/shard_map/ppermute | solution.py:487
  35.8 1.0 %collective-permute-start.5 = (f32[192,128]{1,0:T(8,128)S(1)}, f32[192,128]{1,0:T(8,128)S(1)}, u32[]{:S(2)}, u32[]{:S(2)}) collective-permute-start(f32[192,128]{1,0:T(8,128)S(1)} %pad_maximum_fusion), channel_id=1, source_target_pairs={{0,12},{1,13},{2,14},{3,15},{4,8},{5,9},{6,10},{7,11},{8,4},{9,5},... | collective-permute-start | bytes 294920 | tf_op jit(solution)/shard_map/ppermute | solution.py:487
  36.8 5.8 %collective-permute-done.5 = f32[192,128]{1,0:T(8,128)S(1)} collective-permute-done((f32[192,128]{1,0:T(8,128)S(1)}, f32[192,128]{1,0:T(8,128)S(1)}, u32[]{:S(2)}, u32[]{:S(2)}) %collective-permute-start.5) | collective-permute-done | bytes 98336 | tf_op jit(solution)/shard_map/ppermute | solution.py:487
  42.6 1.9 %collective-permute-start.6 = (f32[384,128]{1,0:T(8,128)S(1)}, f32[384,128]{1,0:T(8,128)S(1)}, u32[]{:S(2)}, u32[]{:S(2)}) collective-permute-start(f32[384,128]{1,0:T(8,128)S(1)} %constant_dynamic-update-slice_fusion.row_ref), channel_id=1, source_target_pairs={{1,16},{3,18},{5,20},{7,22},{9,24},{11,26},{13,28},{15,30},{16,1},... | collective-permute-start | bytes 589832 | tf_op jit(solution)/shard_map/ppermute | solution.py:496
  44.6 7.2 %collective-permute-done.6.far_ref = f32[384,128]{1,0:T(8,128)S(1)} collective-permute-done((f32[384,128]{1,0:T(8,128)S(1)}, f32[384,128]{1,0:T(8,128)S(1)}, u32[]{:S(2)}, u32[]{:S(2)}) %collective-permute-start.6) | collective-permute-done | bytes 196640 | tf_op jit(solution)/shard_map/ppermute | solution.py:496
  51.7 0.0 collective-permute-start.7
  51.7 6.0 %collective-permute-start.8 = (f32[120,128]{1,0:T(8,128)S(1)}, f32[120,128]{1,0:T(8,128)S(1)}, u32[]{:S(2)}, u32[]{:S(2)}) collective-permute-start(f32[120,128]{1,0:T(8,128)S(1)} %get-tuple-element.21), channel_id=1, source_target_pairs={{1,2},{2,1},{3,4},{4,3},{5,6},{6,5},{7,8},{8,7},{9,10},{10,9},{11,... | collective-permute-start | bytes 184328 | tf_op jit(solution)/shard_map/ppermute | solution.py:496
  57.7 3.7 %collective-permute-done.8.edge_in_ref = f32[120,128]{1,0:T(8,128)S(1)} collective-permute-done((f32[120,128]{1,0:T(8,128)S(1)}, f32[120,128]{1,0:T(8,128)S(1)}, u32[]{:S(2)}, u32[]{:S(2)}) %collective-permute-start.8) | collective-permute-done | bytes 61472 | tf_op jit(solution)/shard_map/ppermute | solution.py:496
  61.5 0.0 collective-permute-done.7.far2_ref
  61.5 14.5 %up.1 = f32[3,16,16,128]{3,2,1,0:T(8,128)} custom-call(f32[384,128]{1,0:T(8,128)S(1)} %constant_dynamic-update-slice_fusion.row_ref, f32[384,128]{1,0:T(8,128)S(1)} %collective-permute-done.6.far_ref, f32[384,128]{1,0:T(8,128)S(1)} %collective-permute-done.7.far2_ref, f32[144,128]{1,0:T(8,128)S(1)} %collective-permute-done.2.msg_in_ref, ...), custom_call_target="tpu_custom_call" | custom-call | tf_op jit(solution)/shard_map/up/pallas_call | solution.py:537
  (8 shorter events, 0.0 us)
Async XLA Ops:
  0.0 1.0 %copy-start = (f32[3,16,16,128]{3,2,1,0:T(8,128)S(1)}, f32[3,16,16,128]{3,2,1,0:T(8,128)}, u32[]{:S(2)}) copy-start(f32[3,16,16,128]{3,2,1,0:T(8,128)} %load_ref.3) | copy-start | bytes 1179652
  1.0 0.9 %copy-start.1 = (s32[16,16,128]{2,1,0:T(8,128)S(1)}, s32[16,16,128]{2,1,0:T(8,128)}, u32[]{:S(2)}) copy-start(s32[16,16,128]{2,1,0:T(8,128)} %class_ref.1) | copy-start | bytes 393220
  1.9 0.7 copy-start.2
  2.6 0.7 copy-start.3
  3.9 10.3 %collective-permute-start = (f32[38,16,128]{2,1,0:T(8,128)S(1)}, f32[38,16,128]{2,1,0:T(8,128)S(1)}, u32[]{:S(2)}, u32[]{:S(2)}) collective-permute-start(f32[38,16,128]{2,1,0:T(8,128)S(1)} %get-tuple-element.18), channel_id=1, source_target_pairs={{0,1},{1,0},{2,3},{3,2},{4,5},{5,4},{6,7},{7,6},{8,9},{9,8},{10,11... | collective-permute-start | bytes 933896 | tf_op jit(solution)/shard_map/ppermute | solution.py:487
  4.0 14.8 %collective-permute-start.1 = (f32[38,16,128]{2,1,0:T(8,128)S(1)}, f32[38,16,128]{2,1,0:T(8,128)S(1)}, u32[]{:S(2)}, u32[]{:S(2)}) collective-permute-start(f32[38,16,128]{2,1,0:T(8,128)S(1)} %get-tuple-element.19), channel_id=1, source_target_pairs={{1,2},{2,1},{3,4},{4,3},{5,6},{6,5},{7,8},{8,7},{9,10},{10,9},{11,... | collective-permute-start | bytes 933896 | tf_op jit(solution)/shard_map/ppermute | solution.py:496
  25.6 1.4 %collective-permute-start.2 = (f32[144,128]{1,0:T(8,128)S(1)}, f32[144,128]{1,0:T(8,128)S(1)}, u32[]{:S(2)}, u32[]{:S(2)}) collective-permute-start(f32[144,128]{1,0:T(8,128)S(1)} %get-tuple-element.20), channel_id=1, source_target_pairs={{0,1},{1,0},{2,3},{3,2},{4,5},{5,4},{6,7},{7,6},{8,9},{9,8},{10,11... | collective-permute-start | bytes 221192 | tf_op jit(solution)/shard_map/ppermute | solution.py:487
  27.0 3.8 %collective-permute-start.3 = (f32[48,128]{1,0:T(8,128)S(1)}, f32[48,128]{1,0:T(8,128)S(1)}, u32[]{:S(2)}, u32[]{:S(2)}) collective-permute-start(f32[48,128]{1,0:T(8,128)S(1)} %pad_maximum_fusion.2), channel_id=1, source_target_pairs={{0,2},{1,3},{2,0},{3,1},{4,6},{5,7},{6,4},{7,5},{8,10},{9,11},{10,... | collective-permute-start | bytes 73736 | tf_op jit(solution)/shard_map/ppermute | solution.py:487
  30.8 5.0 %collective-permute-start.4 = (f32[96,128]{1,0:T(8,128)S(1)}, f32[96,128]{1,0:T(8,128)S(1)}, u32[]{:S(2)}, u32[]{:S(2)}) collective-permute-start(f32[96,128]{1,0:T(8,128)S(1)} %pad_maximum_fusion.1), channel_id=1, source_target_pairs={{0,4},{1,5},{2,6},{3,7},{4,0},{5,1},{6,2},{7,3},{8,12},{9,13},{10,... | collective-permute-start | bytes 147464 | tf_op jit(solution)/shard_map/ppermute | solution.py:487
  35.8 6.8 %collective-permute-start.5 = (f32[192,128]{1,0:T(8,128)S(1)}, f32[192,128]{1,0:T(8,128)S(1)}, u32[]{:S(2)}, u32[]{:S(2)}) collective-permute-start(f32[192,128]{1,0:T(8,128)S(1)} %pad_maximum_fusion), channel_id=1, source_target_pairs={{0,12},{1,13},{2,14},{3,15},{4,8},{5,9},{6,10},{7,11},{8,4},{9,5},... | collective-permute-start | bytes 294920 | tf_op jit(solution)/shard_map/ppermute | solution.py:487
  42.6 9.1 %collective-permute-start.6 = (f32[384,128]{1,0:T(8,128)S(1)}, f32[384,128]{1,0:T(8,128)S(1)}, u32[]{:S(2)}, u32[]{:S(2)}) collective-permute-start(f32[384,128]{1,0:T(8,128)S(1)} %constant_dynamic-update-slice_fusion.row_ref), channel_id=1, source_target_pairs={{1,16},{3,18},{5,20},{7,22},{9,24},{11,26},{13,28},{15,30},{16,1},... | collective-permute-start | bytes 589832 | tf_op jit(solution)/shard_map/ppermute | solution.py:496
  51.7 9.8 %collective-permute-start.7 = (f32[384,128]{1,0:T(8,128)S(1)}, f32[384,128]{1,0:T(8,128)S(1)}, u32[]{:S(2)}, u32[]{:S(2)}) collective-permute-start(f32[384,128]{1,0:T(8,128)S(1)} %collective-permute-done.6.far_ref), channel_id=1, source_target_pairs={{0,1},{1,0},{2,3},{3,2},{4,5},{5,4},{6,7},{7,6},{8,9},{9,8},{10,11... | collective-permute-start | bytes 589832 | tf_op jit(solution)/shard_map/ppermute | solution.py:487
  51.7 9.7 %collective-permute-start.8 = (f32[120,128]{1,0:T(8,128)S(1)}, f32[120,128]{1,0:T(8,128)S(1)}, u32[]{:S(2)}, u32[]{:S(2)}) collective-permute-start(f32[120,128]{1,0:T(8,128)S(1)} %get-tuple-element.21), channel_id=1, source_target_pairs={{1,2},{2,1},{3,4},{4,3},{5,6},{6,5},{7,8},{8,7},{9,10},{10,9},{11,... | collective-permute-start | bytes 184328 | tf_op jit(solution)/shard_map/ppermute | solution.py:496

commit v2 on v1

--- a/solution.py
+++ b/solution.py
@@ -34,10 +34,10 @@
 
 def lane_sum(s, step, period):
     axis = s.ndim - 1
-    lane = iota(s.shape, axis) & (period - 1)
-    before = jnp.where(lane >= step, pltpu.roll(s, step, axis), 0.0)
-    after = jnp.where(lane < period - step, pltpu.roll(s, 128 - step, axis), 0.0)
-    return s + before + after
+    lane = iota((1,) * axis + (128,), axis) & (period - 1)
+    low = jnp.where(lane >= step, 1.0, 0.0).astype(F32)
+    high = jnp.where(lane < period - step, 1.0, 0.0).astype(F32)
+    return s + low * pltpu.roll(s, step, axis) + high * pltpu.roll(s, 128 - step, axis)
 
 
 def row_sum(s):
@@ -59,39 +59,51 @@
     return jnp.where(root > 0.0, root, 1.0)
 
 
-def solid_lanes(occ_ref, rows):
-    lane = iota((rows, 128), 1) >> 4
-    out = jnp.zeros((rows, 128), F32)
-    for k in range(8):
-        out = jnp.where(lane == k, occ_ref[0, 0, k].astype(F32), out)
-    return out
-
-
-def pack_kernel(load_ref, class_ref, occ_ref, moduli_ref, x_ref, o_ref, root_ref):
+def pack_kernel(load_ref, class_ref, occ_ref, moduli_ref, x_ref, o_ref, root_ref, class_s, occ_s, moduli_s, sems):
     odd = lax.axis_index("bricks") & 1
+    small = [
+        pltpu.make_async_copy(class_ref, class_s, sems.at[0]),
+        pltpu.make_async_copy(occ_ref, occ_s, sems.at[1]),
+        pltpu.make_async_copy(moduli_ref, moduli_s, sems.at[2]),
+    ]
+    for copy in small:
+        copy.start()
+    large = []
+    for k, (ref, first) in enumerate(((x_ref, 1 - odd), (o_ref, odd))):
+        for c in range(3):
+            copy = pltpu.make_async_copy(
+                load_ref.at[c, pl.ds(first * 7, 9)], ref.at[pl.ds(9 * c, 9)], sems.at[3 + 3 * k + c]
+            )
+            copy.start()
+            large.append(copy)
+    for copy in small:
+        copy.wait()
 
     def fill(z, _):
-        cls = class_ref[z]
+        cls = class_s[z]
         modulus = jnp.zeros(cls.shape, F32)
         for k in range(8):
-            modulus = jnp.where(cls == k, moduli_ref[k], modulus)
+            modulus = jnp.where(cls == k, moduli_s[k], modulus)
         root_ref[z] = jnp.sqrt(modulus)
         return 0
 
-    lax.fori_loop(0, 16, fill, 0, unroll=4)
-    solid = solid_lanes(occ_ref, 16)
+    lax.fori_loop(0, 16, fill, 0, unroll=8)
+    lane = iota((16, 128), 1) >> 4
+    solid = jnp.zeros((16, 128), F32)
+    for k in range(8):
+        solid = jnp.where(lane == k, occ_s[0, 0, k].astype(F32), solid)
+    root_ref[16] = solid
     x_ref[37] = solid
     o_ref[37] = solid
-    for ref, first in ((x_ref, (1 - odd)), (o_ref, odd)):
-        for c in range(3):
-            for j in range(9):
-                ref[c * 9 + j] = load_ref[c, first * 7 + j]
+    for ref, first in ((x_ref, 1 - odd), (o_ref, odd)):
         for j in range(10):
             ref[27 + j] = root_ref[first * 6 + j]
+    for copy in large:
+        copy.wait()
 
 
 def down_kernel(
-    load_ref, root_own_ref, occ_ref, x_ref, o_ref,
+    load_ref, root_own_ref, x_ref, o_ref,
     msg_ref, edge_ref, v0_ref, beta0_ref, root0_ref, v1_ref, beta1_ref, root1_ref, sol_ref,
     b_s, va_s, d_s, sol_s, t_s, tr_s,
 ):
@@ -104,7 +116,7 @@
     def right(k):
         return jnp.where(is_odd, o_ref[k], x_ref[k])
 
-    own_solid = solid_lanes(occ_ref, 16)
+    own_solid = root_own_ref[16]
     left_solid, right_solid = left(37), right(37)
     sol_ref[...] = jnp.zeros((8, 128), F32)
     sol_ref[0:1, :] = left_solid[:1]
@@ -121,7 +133,7 @@
         root0_ref[z + HALO] = root_own_ref[z]
         return 0
 
-    lax.fori_loop(0, 16, own, 0, unroll=4)
+    lax.fori_loop(0, 16, own, 0, unroll=16)
 
     def start(e, b0, b1, b2):
         s = b0 + b1 + b2
@@ -141,7 +153,7 @@
         start(z + HALO, load_ref[0, z], load_ref[1, z], load_ref[2, z])
         return 0
 
-    lax.fori_loop(0, 16, own_start, 0, unroll=2)
+    lax.fori_loop(0, 16, own_start, 0, unroll=8)
 
     def stencil(ref, c, e):
         mid = ref[c, e]
@@ -158,7 +170,7 @@
             v0_ref[c, e] = v + d
         return 0
 
-    lax.fori_loop(2, 34, app1, 0, unroll=2)
+    lax.fori_loop(2, 34, app1, 0, unroll=8)
 
     def app2(e, _):
         sol = sol_s[e]
@@ -168,7 +180,7 @@
             va_s[c, e] = v + A2 * d_s[c, e] + C2 * pre
         return 0
 
-    lax.fori_loop(3, 33, app2, 0, unroll=2)
+    lax.fori_loop(3, 33, app2, 0, unroll=10)
 
     def resid(k, _):
         e = 4 + 2 * k
@@ -182,13 +194,13 @@
             t_s[c, k] = total
         return 0
 
-    lax.fori_loop(0, 14, resid, 0)
+    lax.fori_loop(0, 14, resid, 0, unroll=7)
 
     def root_pair(k, _):
         tr_s[k] = root0_ref[2 * k] + root0_ref[2 * k + 1]
         return 0
 
-    lax.fori_loop(0, 18, root_pair, 0, unroll=2)
+    lax.fori_loop(0, 18, root_pair, 0, unroll=18)
 
     root1 = lane_pair(tr_s[:, pl.ds(0, 8, 2), :] + tr_s[:, pl.ds(1, 8, 2), :], 1) * 0.125
     root1_ref[...] = root1
@@ -276,19 +288,30 @@
             w_s[c, 4 * w : 4 * w + 4, :] = all_s[slot, 4 * c : 4 * c + 4, :]
         w_s[4, 4 * w : 4 * w + 4, :] = all_s[slot, 16:20, :]
 
+    lane = iota((1, 1, 128), 2)
+
+    def lane_mask(cond):
+        return jnp.where(cond, 1.0, 0.0).astype(F32)
+
+    masks_x = (lane_mask(lane >= 32), lane_mask(lane < 96))
+    masks_y = {
+        level: (lane_mask((lane & 31) >= step), lane_mask((lane & 31) < 32 - step))
+        for level, step in ((2, 1), (3, 2), (4, 4), (5, 8))
+    }
+    scale27 = jnp.concatenate([jnp.full((1, 1, 128), k, F32) for k in kappa], axis=0)
+    by26 = scale27 * (1.0 / 26.5)
+
     def stencil(v, level):
-        n = v.shape[0]
-        s = v + pltpu.roll(v, 1, 0) + pltpu.roll(v, n - 1, 0)
+        n = v.shape[1]
+        s = v + pltpu.roll(v, 1, 1) + pltpu.roll(v, n - 1, 1)
         if level == 2:
-            lane = iota(s.shape, 1)
-            s = (
-                s
-                + jnp.where(lane >= 32, pltpu.roll(s, 32, 1), 0.0)
-                + jnp.where(lane < 96, pltpu.roll(s, 96, 1), 0.0)
-            )
+            s = s + masks_x[0] * pltpu.roll(s, 32, 2) + masks_x[1] * pltpu.roll(s, 96, 2)
         else:
-            s = s + pltpu.roll(s, 64, 1)
-        return 27.5 * v - lane_sum(s, 2 ** (level - 2), 32)
+            s = s + pltpu.roll(s, 64, 2)
+        step = 2 ** (level - 2)
+        low, high = masks_y[level]
+        s = s + low * pltpu.roll(s, step, 2) + high * pltpu.roll(s, 128 - step, 2)
+        return 27.5 * v - s
 
     def first(beta, m, level):
         v = beta * INV_MID
@@ -306,63 +329,57 @@
         return v + d
 
     def coarsen(values, level):
-        n = values.shape[0]
+        k, n = values.shape[:2]
         half = (n // 2 + 7) // 8 * 8
         if 2 * half > n:
-            f_s[n : 2 * half, :] = jnp.zeros((2 * half - n, 128), F32)
-        f_s[0:n, :] = values
-        s = f_s[pl.ds(0, half, 2), :] + f_s[pl.ds(1, half, 2), :]
+            f_s[0:k, n : 2 * half, :] = jnp.zeros((k, 2 * half - n, 128), F32)
+        f_s[0:k, 0:n, :] = values
+        s = f_s[0:k, pl.ds(0, half, 2), :] + f_s[0:k, pl.ds(1, half, 2), :]
         s = lane_pair(s, 2 ** (level - 2))
         if level == 2:
             return lane_pair(s, 32) * 0.125
         return s * 0.25
 
     def refine(values, first_row, count):
-        n = values.shape[0]
-        f_s[pl.ds(0, n, 2), :] = values
-        f_s[pl.ds(1, n, 2), :] = values
-        return f_s[first_row : first_row + count, :]
-
-    roots = {2: safe(w_s[3])}
-    sols = {2: w_s[4]}
+        n = values.shape[1]
+        f_s[0:3, pl.ds(0, n, 2), :] = values
+        f_s[0:3, pl.ds(1, n, 2), :] = values
+        return f_s[0:3, first_row : first_row + count, :]
+
+    both = w_s[3:5]
+    roots, sols = {2: safe(both[0:1])}, {2: both[1:2]}
     for level in (2, 3, 4):
-        roots[level + 1] = safe(coarsen(roots[level], level))
-        sols[level + 1] = coarsen(sols[level], level)
-
-    def beta_scale(level):
-        sol = sols[level]
-        sol = sol * sol if level == 5 else sol
-        return sol / (0.25**level * center * roots[level])
-
-    def mask(level):
-        sol = sols[level]
-        return sol * sol * sol if level == 5 else sol
-
-    scales = {level: beta_scale(level) for level in (2, 3, 4, 5)}
-    masks = {level: mask(level) for level in (2, 3, 4, 5)}
-    g5 = jnp.where(sols[5] > 0.0, 1.0 / (roots[5] * jnp.where(sols[5] > 0.0, sols[5], 1.0)), 0.0)
+        both = coarsen(jnp.concatenate([roots[level], sols[level]], axis=0), level)
+        roots[level + 1], sols[level + 1] = safe(both[0:1]), both[1:2]
+    sol5 = sols[5]
+    sol5_safe = jnp.where(sol5 > 0.0, sol5, 1.0)
+    inverse = {level: 1.0 / roots[level] for level in (2, 3, 4, 5)}
+    powers = {level: (sols[level], sols[level]) for level in (2, 3, 4)}
+    powers[5] = (sol5 * sol5, sol5 * sol5 * sol5)
+    g5 = jnp.where(sol5 > 0.0, inverse[5] / sol5_safe, 0.0)
+    scales = {level: powers[level][0] * inverse[level] * (1.0 / (0.25**level * center)) for level in (2, 3, 4, 5)}
+    masks = {level: powers[level][1] * by26 for level in (2, 3, 4, 5)}
     windows = {4: (0, 40), 3: (24, 48), 2: (56, 80)}
 
-    for c in range(3):
-        b = w_s[c]
-        betas, vs = {}, {}
-        for level in (2, 3, 4):
-            beta = b * scales[level]
-            v = first(beta, masks[level] * (kappa[c] / 26.5), level)
-            r = b - (sols[level] * roots[level]) * (0.25**level * kappa[c] / 27.0) * stencil(v, level)
-            betas[level], vs[level] = beta, v
-            b = coarsen(r, level)
-        e = first(b * scales[5], masks[5] * (kappa[c] / 26.5), 5) * g5
-        first_row = 0
-        for level in (4, 3, 2):
-            lo, hi = windows[level]
-            e = refine(e, lo - first_row, hi - lo)
-            root, sol = roots[level][lo:hi], sols[level][lo:hi]
-            v = vs[level][lo:hi] + (root * sol) * e
-            v = again(v, betas[level][lo:hi], masks[level][lo:hi] * (kappa[c] / 26.5), level)
-            e = jnp.where(sol > 0.0, v / root, e)
-            first_row = 2 * lo
-        e2_s[c] = e
+    b = w_s[0:3]
+    betas, vs = {}, {}
+    for level in (2, 3, 4):
+        beta = b * scales[level]
+        v = first(beta, masks[level], level)
+        r = b - (sols[level] * roots[level]) * (scale27 * (0.25**level / 27.0)) * stencil(v, level)
+        betas[level], vs[level] = beta, v
+        b = coarsen(r, level)
+    e = first(b * scales[5], masks[5], 5) * g5
+    first_row = 0
+    for level in (4, 3, 2):
+        lo, hi = windows[level]
+        e = refine(e, lo - first_row, hi - lo)
+        root, sol = roots[level][:, lo:hi], sols[level][:, lo:hi]
+        v = vs[level][:, lo:hi] + (root * sol) * e
+        v = again(v, betas[level][:, lo:hi], masks[level][:, lo:hi], level)
+        e = jnp.where(sol > 0.0, v * inverse[level][:, lo:hi], e)
+        first_row = 2 * lo
+    e2_s[...] = e
 
     rows = {}
     for k, name in enumerate(("left", "own", "right")):
@@ -425,7 +442,7 @@
             a_s[c, k] = v0_ref[c, k + shift] + g * pe_s[c, k >> 1]
         return 0
 
-    lax.fori_loop(1, 23, begin, 0, unroll=2)
+    lax.fori_loop(1, 23, begin, 0, unroll=11)
 
     def stencil0(ref, c, k):
         mid = ref[c, k]
@@ -441,7 +458,7 @@
             bb_s[c, k] = v + d
         return 0
 
-    lax.fori_loop(2, 22, app0, 0, unroll=2)
+    lax.fori_loop(2, 22, app0, 0, unroll=10)
 
     def app1(k, _):
         sol = sol0(k)
@@ -453,7 +470,7 @@
             a_s[c, k] = v + d
         return 0
 
-    lax.fori_loop(3, 21, app1, 0, unroll=2)
+    lax.fori_loop(3, 21, app1, 0, unroll=9)
     own_solid = jnp.broadcast_to(rows["own"], (16, 128))
 
     def app2(k, _):
@@ -470,11 +487,11 @@
         out_ref[2, k - 4] = third - x[0] - x[1]
         return 0
 
-    lax.fori_loop(4, 20, app2, 0, unroll=2)
+    lax.fori_loop(4, 20, app2, 0, unroll=8)
 
 
 VMEM = pl.BlockSpec(memory_space=pltpu.VMEM)
-SMEM = pl.BlockSpec(memory_space=pltpu.SMEM)
+HBM = pl.BlockSpec(memory_space=pltpu.HBM)
 PARAMS = pltpu.CompilerParams(vmem_limit_bytes=40 * 2**20)
 
 
@@ -499,10 +516,16 @@
 def body(load_field, material_class, occupancy, moduli):
     x_msg, o_msg, root = pl.pallas_call(
         pack_kernel,
-        out_shape=(shaped(38, 16, 128), shaped(38, 16, 128), shaped(16, 16, 128)),
-        in_specs=[VMEM, VMEM, SMEM, SMEM],
+        out_shape=(shaped(38, 16, 128), shaped(38, 16, 128), shaped(17, 16, 128)),
+        in_specs=[HBM, HBM, HBM, HBM],
         out_specs=(VMEM, VMEM, VMEM),
-        compiler_params=PARAMS,
+        scratch_shapes=[
+            pltpu.VMEM((16, 16, 128), jnp.int32),
+            pltpu.SMEM((1, 1, 8), jnp.int32),
+            pltpu.SMEM((8,), F32),
+            pltpu.SemaphoreType.DMA((9,)),
+        ],
+        compiler_params=pltpu.CompilerParams(vmem_limit_bytes=56 * 2**20),
         name="pack",
     )(load_field, material_class, occupancy, moduli)
     x_in = swap_bits(x_msg, 1)
@@ -514,7 +537,7 @@
             shaped(3, EXT, 16, 128), shaped(3, EXT, 16, 128), shaped(EXT, 16, 128),
             shaped(3, 14, 8, 128), shaped(3, 14, 8, 128), shaped(18, 8, 128), shaped(8, 128),
         ),
-        in_specs=[VMEM, VMEM, SMEM, VMEM, VMEM],
+        in_specs=[VMEM] * 4,
         out_specs=(VMEM,) * 9,
         scratch_shapes=[
             pltpu.VMEM((3, EXT, 16, 128), F32),
@@ -526,12 +549,14 @@
         ],
         compiler_params=PARAMS,
         name="down",
-    )(load_field, root, occupancy, x_in, o_in)
+    )(load_field, root, x_in, o_in)
     msg_in = swap_bits(msg, 1)
     edge_in = swap_before(edge, 1)
     row = jnp.concatenate([msg[:24], msg_in[:24]], axis=0)
     for bits in (2, 4, 12):
         row = jnp.concatenate([row, swap_bits(row, bits)], axis=0)
+        if bits == 4:
+            row, edge_in = lax.optimization_barrier((row, edge_in))
     far = swap_before(row, 15)
     far2 = swap_bits(far, 1)
     return pl.pallas_call(
@@ -542,7 +567,7 @@
         scratch_shapes=[
             pltpu.VMEM((48, 24, 128), F32),
             pltpu.VMEM((5, 136, 128), F32),
-            pltpu.VMEM((144, 128), F32),
+            pltpu.VMEM((3, 144, 128), F32),
             pltpu.VMEM((3, 24, 128), F32),
             pltpu.VMEM((3, 12, 16, 128), F32),
             pltpu.VMEM((3, 24, 16, 128), F32),

time: 76.2 us -> 61.4 us (0.81)
  Pallas kernels: 22 us -> 12.6 us
  waiting for transfers between devices: 31.3 us -> 28.2 us
  local copies, waits for them, and re-layouts: 3.23 us -> 0.93 us
    pallas_call x1, Pallas kernels: 14.5 us -> 7.42 us  [body(): pl.pallas_call(up_kernel, out_shape=shaped(3, 16, 16, 128), in_specs=[VME...]
    pallas_call x1, Pallas kernels: 6.76 us -> 3.1 us  [body(): pl.pallas_call(down_kernel, out_shape=(shaped(144, 128), shaped(120, 128)...]
    ppermute x6, waiting for transfers between devices: 15.8 us -> 13.2 us  [swap_bits(): return lax.ppermute(values, 'bricks', [(i, i ^ bits) for i in range(n)])]
    unnamed x10 -> x5, local copies, waits for them, and re-layouts: 3.22 us -> 0.92 us
    pallas_call x1, Pallas kernels: 0.72 us -> 2.11 us  [body(): pl.pallas_call(pack_kernel, out_shape=(shaped(38, 16, 128), shaped(38, 16...]
    ppermute x6, starting transfers between devices: 1.23 us -> 0.2 us  [swap_bits(): return lax.ppermute(values, 'bricks', [(i, i ^ bits) for i in range(n)])]
where the time goes in v2:
time: 61.4 us; the launch traced here: 60.9 us
  waiting for transfers between devices  28.2 us (46%)
  starting transfers between devices  19.1 us (31%)
  Pallas kernels  12.6 us (21%)
  local copies, waits for them, and re-layouts  0.93 us (2%)
    ppermute x3, starting transfers between devices, swap_before(): return lax.ppermute(values, 'bricks', sorted(pairs))  18.9 us
    ppermute x3, waiting for transfers between devices, swap_before(): return lax.ppermute(values, 'bricks', sorted(pairs))  15 us
    ppermute x6, waiting for transfers between devices, swap_bits(): return lax.ppermute(values, 'bricks', [(i, i ^ bits) for i in range(n)])  13.2 us
    pallas_call x1, Pallas kernels, body(): pl.pallas_call(up_kernel, out_shape=shaped(3, 16, 16, 128), in_specs=[VME...  7.42 us
    pallas_call x1, Pallas kernels, body(): pl.pallas_call(down_kernel, out_shape=(shaped(144, 128), shaped(120, 128)...  3.1 us
    pallas_call x1, Pallas kernels, body(): pl.pallas_call(pack_kernel, out_shape=(shaped(38, 16, 128), shaped(38, 16...  2.11 us
  transfers between devices with their start and end apart: 9, of which 7 were waited for; matrix products, arithmetic and copies ran while one was open for 0% of the time, Pallas kernels for 0%

profile of v2, /device:TPU:24, one launch (start us, length us, event | category | flops | bytes accessed | tf_op | source)
XLA Modules:
  0.0 60.9 jit_solution(14412882208896169004)
XLA Ops:
  0.0 0.0 copy-start
  0.0 2.1 %pack.1 = (f32[38,16,128]{2,1,0:T(8,128)}, f32[38,16,128]{2,1,0:T(8,128)}, f32[17,16,128]{2,1,0:T(8,128)}) custom-call(f32[3,16,16,128]{3,2,1,0:T(8,128)} %load_ref.3, s32[16,16,128]{2,1,0:T(8,128)} %class_ref.1, s32[1,1,8]{2,1,0:T(1,128)} %occ_ref.1, f32[8]{0:T(128)} %moduli_ref.1), custom_call_target="tpu_custom_call" | custom-call | tf_op jit(solution)/shard_map/pack/pallas_call | solution.py:517
  2.1 0.1 collective-permute-start
  2.2 10.2 %collective-permute-start.1 = (f32[38,16,128]{2,1,0:T(8,128)}, f32[38,16,128]{2,1,0:T(8,128)S(1)}, u32[]{:S(2)}, u32[]{:S(2)}) collective-permute-start(f32[38,16,128]{2,1,0:T(8,128)} %get-tuple-element.21), channel_id=1, source_target_pairs={{1,2},{2,1},{3,4},{4,3},{5,6},{6,5},{7,8},{8,7},{9,10},{10,9},{11,... | collective-permute-start | bytes 933896 | tf_op jit(solution)/shard_map/ppermute | solution.py:513
  12.5 0.0 collective-permute-done.x_ref
  12.5 4.8 %collective-permute-done.1.o_ref = f32[38,16,128]{2,1,0:T(8,128)S(1)} collective-permute-done((f32[38,16,128]{2,1,0:T(8,128)}, f32[38,16,128]{2,1,0:T(8,128)S(1)}, u32[]{:S(2)}, u32[]{:S(2)}) %collective-permute-start.1) | collective-permute-done | bytes 311328 | tf_op jit(solution)/shard_map/ppermute | solution.py:513
  17.2 0.0 copy-done
  17.2 0.0 copy-start.1
  17.2 0.9 %copy-done.1 = f32[17,16,128]{2,1,0:T(8,128)S(1)} copy-done((f32[17,16,128]{2,1,0:T(8,128)S(1)}, f32[17,16,128]{2,1,0:T(8,128)}, u32[]{:S(2)}) %copy-start.1) | copy-done | bytes 139288
  18.1 3.1 %down.1 = (f32[144,128]{1,0:T(8,128)S(1)}, f32[120,128]{1,0:T(8,128)S(1)}, f32[3,36,16,128]{3,2,1,0:T(8,128)S(1)}, f32[3,36,16,128]{3,2,1,0:T(8,128)S(1)}, f32[3...) custom-call(f32[3,16,16,128]{3,2,1,0:T(8,128)S(1)} %copy-done, ...), custom_call_target="tpu_custom_call" | custom-call | tf_op jit(solution)/shard_map/down/pallas_call | solution.py:533
  21.3 0.1 collective-permute-start.2
  21.4 1.2 %collective-permute-done.2.msg_in_ref = f32[144,128]{1,0:T(8,128)S(1)} collective-permute-done((f32[144,128]{1,0:T(8,128)S(1)}, f32[144,128]{1,0:T(8,128)S(1)}, u32[]{:S(2)}, u32[]{:S(2)}) %collective-permute-start.2) | collective-permute-done | bytes 73760 | tf_op jit(solution)/shard_map/ppermute | solution.py:504
  22.6 0.0 collective-permute-start.3
  22.6 3.8 %collective-permute-done.3 = f32[48,128]{1,0:T(8,128)S(1)} collective-permute-done((f32[48,128]{1,0:T(8,128)S(1)}, f32[48,128]{1,0:T(8,128)S(1)}, u32[]{:S(2)}, u32[]{:S(2)}) %collective-permute-start.3) | collective-permute-done | bytes 24608 | tf_op jit(solution)/shard_map/ppermute | solution.py:504
  26.5 0.0 collective-permute-start.4
  26.5 6.7 %collective-permute-start.5 = (f32[120,128]{1,0:T(8,128)S(1)}, f32[120,128]{1,0:T(8,128)S(1)}, u32[]{:S(2)}, u32[]{:S(2)}) collective-permute-start(f32[120,128]{1,0:T(8,128)S(1)} %get-tuple-element.23), channel_id=1, source_target_pairs={{1,2},{2,1},{3,4},{4,3},{5,6},{6,5},{7,8},{8,7},{9,10},{10,9},{11,... | collective-permute-start | bytes 184328 | tf_op jit(solution)/shard_map/ppermute | solution.py:513
  33.2 0.0 collective-permute-done.4
  33.2 3.0 %collective-permute-done.5.edge_in_ref = f32[120,128]{1,0:T(8,128)S(1)} collective-permute-done((f32[120,128]{1,0:T(8,128)S(1)}, f32[120,128]{1,0:T(8,128)S(1)}, u32[]{:S(2)}, u32[]{:S(2)}) %collective-permute-start.5) | collective-permute-done | bytes 61472 | tf_op jit(solution)/shard_map/ppermute | solution.py:513
  36.2 0.0 collective-permute-start.6
  36.2 6.7 %collective-permute-done.6 = f32[192,128]{1,0:T(8,128)S(1)} collective-permute-done((f32[192,128]{1,0:T(8,128)S(1)}, f32[192,128]{1,0:T(8,128)S(1)}, u32[]{:S(2)}, u32[]{:S(2)}) %collective-permute-start.6) | collective-permute-done | bytes 98336 | tf_op jit(solution)/shard_map/ppermute | solution.py:504
  43.0 1.9 %collective-permute-start.7 = (f32[384,128]{1,0:T(8,128)S(1)}, f32[384,128]{1,0:T(8,128)S(1)}, u32[]{:S(2)}, u32[]{:S(2)}) collective-permute-start(f32[384,128]{1,0:T(8,128)S(1)} %constant_dynamic-update-slice_fusion.row_ref), channel_id=1, source_target_pairs={{1,16},{3,18},{5,20},{7,22},{9,24},{11,26},{13,28},{15,30},{16,1},... | collective-permute-start | bytes 589832 | tf_op jit(solution)/shard_map/ppermute | solution.py:513
  44.9 7.2 %collective-permute-done.7.far_ref = f32[384,128]{1,0:T(8,128)S(1)} collective-permute-done((f32[384,128]{1,0:T(8,128)S(1)}, f32[384,128]{1,0:T(8,128)S(1)}, u32[]{:S(2)}, u32[]{:S(2)}) %collective-permute-start.7) | collective-permute-done | bytes 196640 | tf_op jit(solution)/shard_map/ppermute | solution.py:513
  52.1 0.0 collective-permute-start.8
  52.1 1.4 %collective-permute-done.8.far2_ref = f32[384,128]{1,0:T(8,128)S(1)} collective-permute-done((f32[384,128]{1,0:T(8,128)S(1)}, f32[384,128]{1,0:T(8,128)S(1)}, u32[]{:S(2)}, u32[]{:S(2)}) %collective-permute-start.8) | collective-permute-done | bytes 196640 | tf_op jit(solution)/shard_map/ppermute | solution.py:504
  53.5 7.4 %up.1 = f32[3,16,16,128]{3,2,1,0:T(8,128)} custom-call(f32[384,128]{1,0:T(8,128)S(1)} %constant_dynamic-update-slice_fusion.row_ref, f32[384,128]{1,0:T(8,128)S(1)} %collective-permute-done.7.far_ref, f32[384,128]{1,0:T(8,128)S(1)} %collective-permute-done.8.far2_ref, f32[144,128]{1,0:T(8,128)S(1)} %collective-permute-done.2.msg_in_ref, ...), custom_call_target="tpu_custom_call" | custom-call | tf_op jit(solution)/shard_map/up/pallas_call | solution.py:562
  (7 shorter events, 0.0 us)
Async XLA Ops:
  0.0 17.2 %copy-start = (f32[3,16,16,128]{3,2,1,0:T(8,128)S(1)}, f32[3,16,16,128]{3,2,1,0:T(8,128)}, u32[]{:S(2)}) copy-start(f32[3,16,16,128]{3,2,1,0:T(8,128)} %load_ref.3) | copy-start | bytes 1179652
  2.1 10.3 %collective-permute-start = (f32[38,16,128]{2,1,0:T(8,128)}, f32[38,16,128]{2,1,0:T(8,128)S(1)}, u32[]{:S(2)}, u32[]{:S(2)}) collective-permute-start(f32[38,16,128]{2,1,0:T(8,128)} %get-tuple-element.20), channel_id=1, source_target_pairs={{0,1},{1,0},{2,3},{3,2},{4,5},{5,4},{6,7},{7,6},{8,9},{9,8},{10,11... | collective-permute-start | bytes 933896 | tf_op jit(solution)/shard_map/ppermute | solution.py:504
  2.2 15.0 %collective-permute-start.1 = (f32[38,16,128]{2,1,0:T(8,128)}, f32[38,16,128]{2,1,0:T(8,128)S(1)}, u32[]{:S(2)}, u32[]{:S(2)}) collective-permute-start(f32[38,16,128]{2,1,0:T(8,128)} %get-tuple-element.21), channel_id=1, source_target_pairs={{1,2},{2,1},{3,4},{4,3},{5,6},{6,5},{7,8},{8,7},{9,10},{10,9},{11,... | collective-permute-start | bytes 933896 | tf_op jit(solution)/shard_map/ppermute | solution.py:513
  17.2 0.9 %copy-start.1 = (f32[17,16,128]{2,1,0:T(8,128)S(1)}, f32[17,16,128]{2,1,0:T(8,128)}, u32[]{:S(2)}) copy-start(f32[17,16,128]{2,1,0:T(8,128)} %get-tuple-element.19.root_own_ref) | copy-start | bytes 417796
  21.3 1.4 %collective-permute-start.2 = (f32[144,128]{1,0:T(8,128)S(1)}, f32[144,128]{1,0:T(8,128)S(1)}, u32[]{:S(2)}, u32[]{:S(2)}) collective-permute-start(f32[144,128]{1,0:T(8,128)S(1)} %get-tuple-element.22), channel_id=1, source_target_pairs={{0,1},{1,0},{2,3},{3,2},{4,5},{5,4},{6,7},{7,6},{8,9},{9,8},{10,11... | collective-permute-start | bytes 221192 | tf_op jit(solution)/shard_map/ppermute | solution.py:504
  22.6 3.8 %collective-permute-start.3 = (f32[48,128]{1,0:T(8,128)S(1)}, f32[48,128]{1,0:T(8,128)S(1)}, u32[]{:S(2)}, u32[]{:S(2)}) collective-permute-start(f32[48,128]{1,0:T(8,128)S(1)} %pad_maximum_fusion.2), channel_id=1, source_target_pairs={{0,2},{1,3},{2,0},{3,1},{4,6},{5,7},{6,4},{7,5},{8,10},{9,11},{10,... | collective-permute-start | bytes 73736 | tf_op jit(solution)/shard_map/ppermute | solution.py:504
  26.5 6.7 %collective-permute-start.4 = (f32[96,128]{1,0:T(8,128)S(1)}, f32[96,128]{1,0:T(8,128)S(1)}, u32[]{:S(2)}, u32[]{:S(2)}) collective-permute-start(f32[96,128]{1,0:T(8,128)S(1)} %pad_maximum_fusion.1), channel_id=1, source_target_pairs={{0,4},{1,5},{2,6},{3,7},{4,0},{5,1},{6,2},{7,3},{8,12},{9,13},{10,... | collective-permute-start | bytes 147464 | tf_op jit(solution)/shard_map/ppermute | solution.py:504
  26.5 9.8 %collective-permute-start.5 = (f32[120,128]{1,0:T(8,128)S(1)}, f32[120,128]{1,0:T(8,128)S(1)}, u32[]{:S(2)}, u32[]{:S(2)}) collective-permute-start(f32[120,128]{1,0:T(8,128)S(1)} %get-tuple-element.23), channel_id=1, source_target_pairs={{1,2},{2,1},{3,4},{4,3},{5,6},{6,5},{7,8},{8,7},{9,10},{10,9},{11,... | collective-permute-start | bytes 184328 | tf_op jit(solution)/shard_map/ppermute | solution.py:513
  36.2 6.7 %collective-permute-start.6 = (f32[192,128]{1,0:T(8,128)S(1)}, f32[192,128]{1,0:T(8,128)S(1)}, u32[]{:S(2)}, u32[]{:S(2)}) collective-permute-start(f32[192,128]{1,0:T(8,128)S(1)} %pad_maximum_fusion), channel_id=1, source_target_pairs={{0,12},{1,13},{2,14},{3,15},{4,8},{5,9},{6,10},{7,11},{8,4},{9,5},... | collective-permute-start | bytes 294920 | tf_op jit(solution)/shard_map/ppermute | solution.py:504
  43.0 9.1 %collective-permute-start.7 = (f32[384,128]{1,0:T(8,128)S(1)}, f32[384,128]{1,0:T(8,128)S(1)}, u32[]{:S(2)}, u32[]{:S(2)}) collective-permute-start(f32[384,128]{1,0:T(8,128)S(1)} %constant_dynamic-update-slice_fusion.row_ref), channel_id=1, source_target_pairs={{1,16},{3,18},{5,20},{7,22},{9,24},{11,26},{13,28},{15,30},{16,1},... | collective-permute-start | bytes 589832 | tf_op jit(solution)/shard_map/ppermute | solution.py:513
  52.1 1.4 %collective-permute-start.8 = (f32[384,128]{1,0:T(8,128)S(1)}, f32[384,128]{1,0:T(8,128)S(1)}, u32[]{:S(2)}, u32[]{:S(2)}) collective-permute-start(f32[384,128]{1,0:T(8,128)S(1)} %collective-permute-done.7.far_ref), channel_id=1, source_target_pairs={{0,1},{1,0},{2,3},{3,2},{4,5},{5,4},{6,7},{7,6},{8,9},{9,8},{10,11... | collective-permute-start | bytes 589832 | tf_op jit(solution)/shard_map/ppermute | solution.py:504

commit v3 on v2

--- a/solution.py
+++ b/solution.py
@@ -102,10 +102,84 @@
         copy.wait()
 
 
+def start0(e, loads, scale, b_ref, beta_ref, va_ref):
+    total = loads[0] + loads[1] + loads[2]
+    third = total * (1.0 / 3.0)
+    for c, p in enumerate((loads[0] - third, loads[1] - third, total)):
+        b_ref[c, e] = p
+        beta = p * scale
+        beta_ref[c, e] = beta
+        va_ref[c, e] = beta * INV_MID
+
+
+def stencil0(ref, c, e):
+    mid = ref[c, e]
+    s = ref[c, e - 1] + mid + ref[c, e + 1]
+    return mid, 27.5 * mid - lane_sum(row_sum(s), 1, 128)
+
+
+def first0(e, sol, beta_ref, va_ref, d_ref, vb_ref):
+    for c in range(3):
+        v, t = stencil0(va_ref, c, e)
+        d = A1 * v + C1 * (beta_ref[c, e] - (sol * (kappa[c] / 26.5)) * t)
+        d_ref[c, e] = d
+        vb_ref[c, e] = v + d
+
+
+def second0(e, sol, beta_ref, vb_ref, d_ref, v0_ref):
+    for c in range(3):
+        v, t = stencil0(vb_ref, c, e)
+        pre = beta_ref[c, e] - (sol * (kappa[c] / 26.5)) * t
+        v0_ref[c, e] = v + A2 * d_ref[c, e] + C2 * pre
+
+
+def residual0(k, sols, root_ref, b_ref, v0_ref, t_ref):
+    for c in range(3):
+        total = None
+        for j in range(2):
+            e = 4 + 2 * k + j
+            _, t = stencil0(v0_ref, c, e)
+            r = b_ref[c, e] - (sols[j] * root_ref[e]) * (kappa[c] / 27.0) * t
+            total = r if total is None else total + r
+        t_ref[c, k] = total
+
+
+def inner_kernel(load_ref, own_ref, b_ref, beta_ref, root0_ref, va_ref, d_ref, vb_ref, v0_ref, t_ref):
+    solid = own_ref[16]
+
+    def start(z, _):
+        root = own_ref[z]
+        root0_ref[z + HALO] = root
+        scale = solid / (center * root)
+        start0(z + HALO, [load_ref[c, z] for c in range(3)], scale, b_ref, beta_ref, va_ref)
+        return 0
+
+    lax.fori_loop(0, 16, start, 0, unroll=8)
+
+    def app1(e, _):
+        first0(e, solid, beta_ref, va_ref, d_ref, vb_ref)
+        return 0
+
+    lax.fori_loop(HALO + 1, HALO + 15, app1, 0, unroll=7)
+
+    def app2(e, _):
+        second0(e, solid, beta_ref, vb_ref, d_ref, v0_ref)
+        return 0
+
+    lax.fori_loop(HALO + 2, HALO + 14, app2, 0, unroll=6)
+
+    def resid(k, _):
+        residual0(k, (solid, solid), root0_ref, b_ref, v0_ref, t_ref)
+        return 0
+
+    lax.fori_loop(5, 9, resid, 0, unroll=4)
+
+
 def down_kernel(
-    load_ref, root_own_ref, x_ref, o_ref,
-    msg_ref, edge_ref, v0_ref, beta0_ref, root0_ref, v1_ref, beta1_ref, root1_ref, sol_ref,
-    b_s, va_s, d_s, sol_s, t_s, tr_s,
+    own_ref, x_ref, o_ref, b_in, beta_in, root_in, va_in, d_in, vb_in, v0_in, t_in,
+    b_ref, beta0_ref, root0_ref, va_ref, d_ref, vb_ref, v0_ref, t_s,
+    msg_ref, edge_ref, v1_ref, beta1_ref, root1_ref, sol_ref,
+    sol_s, tr_s,
 ):
     odd = lax.axis_index("bricks") & 1
     is_odd = odd == 1
@@ -116,7 +190,7 @@
     def right(k):
         return jnp.where(is_odd, o_ref[k], x_ref[k])
 
-    own_solid = root_own_ref[16]
+    own_solid = own_ref[16]
     left_solid, right_solid = left(37), right(37)
     sol_ref[...] = jnp.zeros((8, 128), F32)
     sol_ref[0:1, :] = left_solid[:1]
@@ -125,76 +199,35 @@
     for j in range(HALO):
         sol_s[j] = left_solid
         sol_s[26 + j] = right_solid
+        sol_s[HALO + j if j < 5 else 16 + j] = own_solid
         root0_ref[j] = safe(left(27 + j))
         root0_ref[26 + j] = safe(right(27 + j))
-
-    def own(z, _):
-        sol_s[z + HALO] = own_solid
-        root0_ref[z + HALO] = root_own_ref[z]
-        return 0
-
-    lax.fori_loop(0, 16, own, 0, unroll=16)
-
-    def start(e, b0, b1, b2):
-        s = b0 + b1 + b2
-        third = s * (1.0 / 3.0)
-        scale = sol_s[e] / (center * root0_ref[e])
-        for c, p in enumerate((b0 - third, b1 - third, s)):
-            b_s[c, e] = p
-            beta = p * scale
-            beta0_ref[c, e] = beta
-            va_s[c, e] = beta * INV_MID
-
     for j in range(9):
-        start(1 + j, left(j), left(9 + j), left(18 + j))
-        start(26 + j, right(j), right(9 + j), right(18 + j))
-
-    def own_start(z, _):
-        start(z + HALO, load_ref[0, z], load_ref[1, z], load_ref[2, z])
-        return 0
-
-    lax.fori_loop(0, 16, own_start, 0, unroll=8)
-
-    def stencil(ref, c, e):
-        mid = ref[c, e]
-        s = ref[c, e - 1] + mid + ref[c, e + 1]
-        return mid, 27.5 * mid - lane_sum(row_sum(s), 1, 128)
-
-    def app1(e, _):
-        sol = sol_s[e]
-        for c in range(3):
-            v, t = stencil(va_s, c, e)
-            pre = beta0_ref[c, e] - (sol * (kappa[c] / 26.5)) * t
-            d = A1 * v + C1 * pre
-            d_s[c, e] = d
-            v0_ref[c, e] = v + d
-        return 0
-
-    lax.fori_loop(2, 34, app1, 0, unroll=8)
-
-    def app2(e, _):
-        sol = sol_s[e]
-        for c in range(3):
-            v, t = stencil(v0_ref, c, e)
-            pre = beta0_ref[c, e] - (sol * (kappa[c] / 26.5)) * t
-            va_s[c, e] = v + A2 * d_s[c, e] + C2 * pre
-        return 0
-
-    lax.fori_loop(3, 33, app2, 0, unroll=10)
-
-    def resid(k, _):
-        e = 4 + 2 * k
-        for c in range(3):
-            total = None
-            for j in range(2):
-                v, t = stencil(va_s, c, e + j)
-                v0_ref[c, e + j] = v
-                r = b_s[c, e + j] - (sol_s[e + j] * root0_ref[e + j]) * (kappa[c] / 27.0) * t
-                total = r if total is None else total + r
-            t_s[c, k] = total
-        return 0
-
-    lax.fori_loop(0, 14, resid, 0, unroll=7)
+        for e, side, solid in ((1 + j, left, left_solid), (26 + j, right, right_solid)):
+            scale = solid / (center * root0_ref[e])
+            start0(e, [side(9 * c + j) for c in range(3)], scale, b_ref, beta0_ref, va_ref)
+
+    def app1(j, _):
+        for e in (2 + j, 25 + j):
+            first0(e, sol_s[e], beta0_ref, va_ref, d_ref, vb_ref)
+        return 0
+
+    lax.fori_loop(0, 9, app1, 0, unroll=9)
+
+    def app2(j, _):
+        for e in (3 + j, 24 + j):
+            second0(e, sol_s[e], beta0_ref, vb_ref, d_ref, v0_ref)
+        return 0
+
+    lax.fori_loop(0, 9, app2, 0, unroll=9)
+
+    def resid(j, _):
+        for k in (j, 9 + j):
+            e = 4 + 2 * k
+            residual0(k, (sol_s[e], sol_s[e + 1]), root0_ref, b_ref, v0_ref, t_s)
+        return 0
+
+    lax.fori_loop(0, 5, resid, 0, unroll=5)
 
     def root_pair(k, _):
         tr_s[k] = root0_ref[2 * k] + root0_ref[2 * k + 1]
@@ -229,6 +262,16 @@
         q = jnp.take_along_axis(q, gather, axis=1)
         return jnp.sum(jnp.where(group, q, 0.0), axis=0, keepdims=True) * 0.125
 
+    odd_lane = (iota((8, 128), 1) & 1) == 1
+    to_after, to_before = [], []
+
+    def pair(a, b):
+        return jnp.where(odd_lane, b, a)
+
+    def send_edge(k, after, before):
+        msg_ref[24 + 8 * k : 32 + 8 * k, :] = jnp.where(is_odd, before, after)
+        edge_ref[8 * k : 8 * k + 8, :] = jnp.where(is_odd, after, before)
+
     for c in range(3):
         b1 = lane_pair(t_s[c, :, pl.ds(0, 8, 2), :] + t_s[c, :, pl.ds(1, 8, 2), :], 1) * 0.125
         beta = b1 * scale1
@@ -243,50 +286,52 @@
         r = (b1 - (sol * rt) * (0.25 * kappa[c] / 27.0) * stencil1(v))[3:11]
         for z in range(4):
             msg_ref[4 * c + z : 4 * c + z + 1, :] = compact(r[2 * z] + r[2 * z + 1])
-        for j in range(4):
-            to_after, to_before = v[6 + j], v[4 + j]
-            k = 8 * (4 * c + j)
-            msg_ref[24 + k : 32 + k, :] = jnp.where(is_odd, to_before, to_after)
-            edge_ref[k : k + 8, :] = jnp.where(is_odd, to_after, to_before)
-        to_after, to_before = beta[7], beta[6]
-        k = 8 * (12 + c)
-        msg_ref[24 + k : 32 + k, :] = jnp.where(is_odd, to_before, to_after)
-        edge_ref[k : k + 8, :] = jnp.where(is_odd, to_after, to_before)
+        for j in range(2):
+            send_edge(2 * c + j, pair(v[6 + 2 * j], v[7 + 2 * j]), pair(v[4 + 2 * j], v[5 + 2 * j]))
+        to_after.append(beta[7])
+        to_before.append(beta[6])
+    send_edge(6, pair(*to_after[:2]), pair(*to_before[:2]))
+    send_edge(7, to_after[2], to_before[2])
     for z in range(4):
         msg_ref[12 + z : 13 + z, :] = compact(root1[5 + 2 * z] + root1[6 + 2 * z])
     msg_ref[16:24, :] = jnp.take_along_axis(own_solid[:8], gather, axis=1)
 
 
 def up_kernel(
-    row_ref, far_ref, far2_ref, msg_in_ref, edge_in_ref,
+    row_ref, far_ref, far2_ref, msg_in_ref,
     v0_ref, beta0_ref, root0_ref, v1_ref, beta1_ref, root1_ref, sol_ref,
     out_ref,
-    all_s, w_s, f_s, e2_s, pe_s, a_s, bb_s, d_s,
+    all_s, solid_s, w_s, f_s, e2_s, pe_s, a_s, bb_s, d_s,
 ):
     me = lax.axis_index("bricks")
     odd = me & 1
     is_odd = odd == 1
 
     for t in range(16):
-        rows = slice(24 * t, 24 * t + 24)
+        rows = slice(16 * t, 16 * t + 16)
         far, far2 = far_ref[rows, :], far2_ref[rows, :]
         all_s[t] = jnp.where(is_odd, far2, far)
         all_s[16 + t] = row_ref[rows, :]
         all_s[32 + t] = jnp.where(is_odd, far, far2)
+    far, far2 = far_ref[256:272, :], far2_ref[256:272, :]
+    solid_s[0:16, :] = jnp.where(is_odd, far2, far)
+    solid_s[16:32, :] = row_ref[256:272, :]
+    solid_s[32:48, :] = jnp.where(is_odd, far, far2)
     base = me - odd - 16
-    here = me & 15
-    other = here ^ 1
-    order_left = jnp.where(is_odd, here, other)
-    order_right = jnp.where(is_odd, other, here)
+    here = (me >> 1) & 7
     for w in range(34):
         dev = base + w
         rel = (dev >> 4) - (me >> 4)
-        order = jnp.where(rel == 0, here, jnp.where(rel < 0, order_left, order_right))
-        x = (dev & 15) ^ order
-        slot = (rel + 1) * 16 + (x ^ ((x & 8) >> 1))
+        chip = (dev >> 1) & 7
+        holder = jnp.where(rel == 0, odd, jnp.where(rel < 0, 0, 1))
+        beside = (chip ^ here) & 1
+        via = (chip + beside * (1 - 2 * holder)) & 7
+        x = via ^ here
+        block = ((w & 1) ^ holder ^ beside) + 2 * beside + 4 * (((x >> 1) ^ (x >> 2)) & 1) + 8 * (x >> 2)
+        slot = (rel + 1) * 16 + block
         for c in range(4):
             w_s[c, 4 * w : 4 * w + 4, :] = all_s[slot, 4 * c : 4 * c + 4, :]
-        w_s[4, 4 * w : 4 * w + 4, :] = all_s[slot, 16:20, :]
+        w_s[4, 4 * w : 4 * w + 4, :] = jnp.broadcast_to(solid_s[pl.ds(slot, 1), :], (4, 128))
 
     lane = iota((1, 1, 128), 2)
 
@@ -398,20 +443,28 @@
         after = jnp.concatenate([v[1:], zero], axis=0)
         return 27.5 * v - lane_sum(row_sum(before + v + after), 2, 128)
 
-    def from_left(k):
-        return jnp.where(is_odd, msg_in_ref[24 + 8 * k : 32 + 8 * k, :], edge_in_ref[8 * k : 8 * k + 8, :])[None]
-
-    def from_right(k):
-        return jnp.where(is_odd, edge_in_ref[8 * k : 8 * k + 8, :], msg_in_ref[24 + 8 * k : 32 + 8 * k, :])[None]
+    odd_lane = (iota((8, 128), 1) & 1) == 1
+    across = jnp.where(is_odd, here == 7, here == 0)
+
+    def edge_slabs(k, left):
+        mine = msg_in_ref[24 + 8 * k : 32 + 8 * k, :]
+        other = jnp.where(across, far_ref[272 + 8 * k : 280 + 8 * k, :], row_ref[272 + 8 * k : 280 + 8 * k, :])
+        p = jnp.where(is_odd == left, mine, other)
+        first = jnp.where(odd_lane, pltpu.roll(p, 1, 1), p)
+        second = jnp.where(odd_lane, p, pltpu.roll(p, 127, 1))
+        return [first[None], second[None]]
+
+    edges = {}
+    for left in (True, False):
+        slabs = [edge_slabs(k, left) for k in range(8)]
+        edges[left] = [slabs[2 * c] + slabs[2 * c + 1] for c in range(3)], [slabs[6][0], slabs[6][1], slabs[7][0]]
 
     for c in range(3):
         v = jnp.concatenate(
-            [from_left(4 * c + j) for j in range(4)]
-            + [v1_ref[c][2:12]]
-            + [from_right(4 * c + j) for j in range(4)],
+            edges[True][0][c] + [v1_ref[c][2:12]] + edges[False][0][c],
             axis=0,
         )
-        beta = jnp.concatenate([zero, from_left(12 + c), beta1_ref[c], from_right(12 + c), zero], axis=0)
+        beta = jnp.concatenate([zero, edges[True][1][c], beta1_ref[c], edges[False][1][c], zero], axis=0)
         slabs = []
         for j in range(10):
             row = e2_s[c, pl.ds(5 + 4 * odd + j, 1), :]
@@ -443,11 +496,6 @@
         return 0
 
     lax.fori_loop(1, 23, begin, 0, unroll=11)
-
-    def stencil0(ref, c, k):
-        mid = ref[c, k]
-        s = ref[c, k - 1] + mid + ref[c, k + 1]
-        return mid, 27.5 * mid - lane_sum(row_sum(s), 1, 128)
 
     def app0(k, _):
         sol = sol0(k)
@@ -504,13 +552,24 @@
     return lax.ppermute(values, "bricks", [(i, i ^ bits) for i in range(n)])
 
 
-def swap_before(values, distance):
+def swap_before(values):
+    n = lax.axis_size("bricks")
+    return lax.ppermute(values, "bricks", [(i, i + 1 if i % 2 else i - 1) for i in range(1, n - 1)])
+
+
+def swap_ring(values):
     n = lax.axis_size("bricks")
     pairs = []
     for i in range(0, n, 2):
-        if i - distance >= 0:
-            pairs += [(i, i - distance), (i - distance, i)]
+        j = i // 16 * 16 + (i - 1) % 16
+        pairs += [(i, j), (j, i)]
     return lax.ppermute(values, "bricks", sorted(pairs))
+
+
+def next_rows(values):
+    n = lax.axis_size("bricks")
+    pairs = [(i, i + 16 if i % 2 == 0 else i - 16) for i in range(n)]
+    return lax.ppermute(values, "bricks", [(i, j) for i, j in pairs if 0 <= j < n])
 
 
 def body(load_field, material_class, occupancy, moduli):
@@ -518,7 +577,7 @@
         pack_kernel,
         out_shape=(shaped(38, 16, 128), shaped(38, 16, 128), shaped(17, 16, 128)),
         in_specs=[HBM, HBM, HBM, HBM],
-        out_specs=(VMEM, VMEM, VMEM),
+        out_specs=(VMEM,) * 3,
         scratch_shapes=[
             pltpu.VMEM((16, 16, 128), jnp.int32),
             pltpu.SMEM((1, 1, 8), jnp.int32),
@@ -529,43 +588,62 @@
         name="pack",
     )(load_field, material_class, occupancy, moduli)
     x_in = swap_bits(x_msg, 1)
-    o_in = swap_before(o_msg, 1)
-    msg, edge, *fine = pl.pallas_call(
+    o_in = swap_before(o_msg)
+    ext = shaped(3, EXT, 16, 128)
+    fine = (ext, ext, shaped(EXT, 16, 128), ext, ext, ext, ext, shaped(3, 14, 16, 128))
+    inner = pl.pallas_call(
+        inner_kernel,
+        out_shape=fine,
+        in_specs=[VMEM] * 2,
+        out_specs=(VMEM,) * 8,
+        compiler_params=PARAMS,
+        cost_estimate=pl.CostEstimate(flops=10_000_000, bytes_accessed=4_000_000, transcendentals=0),
+        name="inner",
+    )(load_field, root)
+    _, beta0, root0, _, _, _, v0, _, msg, edge, v1, beta1, root1, solid_rows = pl.pallas_call(
         down_kernel,
-        out_shape=(
-            shaped(144, 128), shaped(120, 128),
-            shaped(3, EXT, 16, 128), shaped(3, EXT, 16, 128), shaped(EXT, 16, 128),
+        out_shape=fine
+        + (
+            shaped(88, 128), shaped(64, 128),
             shaped(3, 14, 8, 128), shaped(3, 14, 8, 128), shaped(18, 8, 128), shaped(8, 128),
         ),
-        in_specs=[VMEM] * 4,
-        out_specs=(VMEM,) * 9,
+        in_specs=[VMEM] * 11,
+        out_specs=(VMEM,) * 14,
+        input_output_aliases={3 + k: k for k in range(8)},
         scratch_shapes=[
-            pltpu.VMEM((3, EXT, 16, 128), F32),
-            pltpu.VMEM((3, EXT, 16, 128), F32),
-            pltpu.VMEM((3, EXT, 16, 128), F32),
             pltpu.VMEM((EXT, 16, 128), F32),
-            pltpu.VMEM((3, 14, 16, 128), F32),
             pltpu.VMEM((18, 16, 128), F32),
         ],
         compiler_params=PARAMS,
         name="down",
-    )(load_field, root, x_in, o_in)
+    )(root, x_in, o_in, *inner)
+    row_of = iota((8, 128), 0)
+
+    def joined(a, b, bit):
+        return jnp.where((row_of & bit) == 0, a, b)
+
     msg_in = swap_bits(msg, 1)
-    edge_in = swap_before(edge, 1)
-    row = jnp.concatenate([msg[:24], msg_in[:24]], axis=0)
-    for bits in (2, 4, 12):
-        row = jnp.concatenate([row, swap_bits(row, bits)], axis=0)
-        if bits == 4:
-            row, edge_in = lax.optimization_barrier((row, edge_in))
-    far = swap_before(row, 15)
+    blocks = jnp.concatenate([msg[:16], msg_in[:16]], axis=0)
+    solids = joined(msg[16:24], msg_in[16:24], 1)
+    got = swap_ring(jnp.concatenate([blocks, solids, edge], axis=0))
+    blocks = jnp.concatenate([blocks, got[:32]], axis=0)
+    solids = joined(solids, got[32:40], 2)
+    edge_in = got[40:]
+    got = swap_bits(jnp.concatenate([blocks, solids], axis=0), 4)
+    blocks = jnp.concatenate([blocks, got[:64]], axis=0)
+    solids = joined(solids, got[64:], 4)
+    got = swap_bits(jnp.concatenate([blocks, solids], axis=0), 12)
+    row = jnp.concatenate([blocks, got[:128], solids, got[128:], edge_in], axis=0)
+    far = next_rows(row)
     far2 = swap_bits(far, 1)
     return pl.pallas_call(
         up_kernel,
         out_shape=shaped(3, 16, 16, 128),
-        in_specs=[VMEM] * 12,
+        in_specs=[VMEM] * 11,
         out_specs=VMEM,
         scratch_shapes=[
-            pltpu.VMEM((48, 24, 128), F32),
+            pltpu.VMEM((48, 16, 128), F32),
+            pltpu.VMEM((48, 128), F32),
             pltpu.VMEM((5, 136, 128), F32),
             pltpu.VMEM((3, 144, 128), F32),
             pltpu.VMEM((3, 24, 128), F32),
@@ -576,7 +654,7 @@
         ],
         compiler_params=PARAMS,
         name="up",
-    )(row, far, far2, msg_in, edge_in, *fine)
+    )(row, far, far2, msg_in, v0, beta0, root0, v1, beta1, root1, solid_rows)
 
 
 def solution(mesh):

time: 61.4 us -> 56.1 us (0.914)
  starting transfers between devices: 19.1 us -> 14 us
  waiting for transfers between devices: 28.2 us -> 27.5 us
    ppermute x3, starting transfers between devices: 18.9 us -> 13.7 us  [the longest x1 10.2 us: swap_before(): lax.ppermute(values, 'bricks', [(i, i + 1 if i % 2 else i - 1) for i in r...]
    ppermute x3, waiting for transfers between devices: 15 us -> 13.6 us  [the longest x1 7.48 us: next_rows(): lax.ppermute(values, 'bricks', [(i, j) for i, j in pairs if 0 <= j < n])]
    ppermute x6 -> x5, waiting for transfers between devices: 13.2 us -> 13.8 us  [swap_bits(): return lax.ppermute(values, 'bricks', [(i, i ^ bits) for i in range(n)])]
    pallas_call x1 -> x2, Pallas kernels: 3.1 us -> 3.15 us  [the longest x1 2.18 us: body(): pl.pallas_call(down_kernel, out_shape=fine + (shaped(88, 128), shaped(64,...]
  transfers between devices with their start and end apart: 9 -> 8, of which waited for: 7 -> 7; matrix products, arithmetic and copies ran while one was open for 0% -> 0% of each run, Pallas kernels for 0% -> 2%
where the time goes in v3:
time: 56.1 us; the launch traced here: 55.6 us
  waiting for transfers between devices  27.5 us (49%)
  starting transfers between devices  14 us (25%)
  Pallas kernels  12.7 us (23%)
  local copies, waits for them, and re-layouts  0.93 us (2%)
    ppermute x5, waiting for transfers between devices, swap_bits(): return lax.ppermute(values, 'bricks', [(i, i ^ bits) for i in range(n)])  13.8 us
    ppermute x1, starting transfers between devices, swap_before(): lax.ppermute(values, 'bricks', [(i, i + 1 if i % 2 else i - 1) for i in r...  10.2 us
    pallas_call x1, Pallas kernels, body(): pl.pallas_call(up_kernel, out_shape=shaped(3, 16, 16, 128), in_specs=[VME...  7.5 us
    ppermute x1, waiting for transfers between devices, next_rows(): lax.ppermute(values, 'bricks', [(i, j) for i, j in pairs if 0 <= j < n])  7.48 us
    ppermute x1, waiting for transfers between devices, swap_ring(): return lax.ppermute(values, 'bricks', sorted(pairs))  3.3 us
    ppermute x1, waiting for transfers between devices, swap_before(): lax.ppermute(values, 'bricks', [(i, i + 1 if i % 2 else i - 1) for i in r...  2.86 us
    pallas_call x1, Pallas kernels, body(): pl.pallas_call(down_kernel, out_shape=fine + (shaped(88, 128), shaped(64,...  2.18 us
    pallas_call x1, Pallas kernels, body(): pl.pallas_call(pack_kernel, out_shape=(shaped(38, 16, 128), shaped(38, 16...  2.1 us
  transfers between devices with their start and end apart: 8, of which 7 were waited for; matrix products, arithmetic and copies ran while one was open for 0% of the time, Pallas kernels for 2%

profile of v3, /device:TPU:24, one launch (start us, length us, event | category | flops | bytes accessed | tf_op | source)
XLA Modules:
  0.0 55.6 jit_solution(1883009658865050530)
XLA Ops:
  0.0 0.0 copy-start
  0.0 2.1 %pack.1 = (f32[38,16,128]{2,1,0:T(8,128)}, f32[38,16,128]{2,1,0:T(8,128)}, f32[17,16,128]{2,1,0:T(8,128)}) custom-call(f32[3,16,16,128]{3,2,1,0:T(8,128)} %load_ref.3, s32[16,16,128]{2,1,0:T(8,128)} %class_ref.1, s32[1,1,8]{2,1,0:T(1,128)} %occ_ref.1, f32[8]{0:T(128)} %moduli_ref.1), custom_call_target="tpu_custom_call" | custom-call | tf_op jit(solution)/shard_map/pack/pallas_call | solution.py:576
  2.1 0.1 collective-permute-start
  2.2 10.2 %collective-permute-start.1 = (f32[38,16,128]{2,1,0:T(8,128)}, f32[38,16,128]{2,1,0:T(8,128)S(1)}, u32[]{:S(2)}, u32[]{:S(2)}) collective-permute-start(f32[38,16,128]{2,1,0:T(8,128)} %get-tuple-element.27), channel_id=1, source_target_pairs={{1,2},{2,1},{3,4},{4,3},{5,6},{6,5},{7,8},{8,7},{9,10},{10,9},{11,... | collective-permute-start | bytes 933896 | tf_op jit(solution)/shard_map/ppermute | solution.py:557
  12.4 0.0 copy-done
  12.5 0.0 copy-start.1
  12.5 0.9 %copy-done.1 = f32[17,16,128]{2,1,0:T(8,128)S(1)} copy-done((f32[17,16,128]{2,1,0:T(8,128)S(1)}, f32[17,16,128]{2,1,0:T(8,128)}, u32[]{:S(2)}) %copy-start.1) | copy-done | bytes 139288
  13.4 1.0 %inner.1 = (f32[3,36,16,128]{3,2,1,0:T(8,128)S(1)}, f32[3,36,16,128]{3,2,1,0:T(8,128)S(1)}, f32[36,16,128]{2,1,0:T(8,128)S(1)}, f32[3,36,16,128]{3,2,1,0:T(8,128...) custom-call(f32[3,16,16,128]{3,2,1,0:T(8,128)S(1)} %copy-done, ...), custom_call_target="tpu_custom_call" | custom-call | flops 10000000 | bytes 4000000 | tf_op jit(solution)/shard_map/inner/pallas_call | solution.py:594
  14.4 0.0 collective-permute-done.x_ref
  14.4 2.9 %collective-permute-done.1.o_ref = f32[38,16,128]{2,1,0:T(8,128)S(1)} collective-permute-done((f32[38,16,128]{2,1,0:T(8,128)}, f32[38,16,128]{2,1,0:T(8,128)S(1)}, u32[]{:S(2)}, u32[]{:S(2)}) %collective-permute-start.1) | collective-permute-done | bytes 311328 | tf_op jit(solution)/shard_map/ppermute | solution.py:557
  17.2 2.2 %down.1 = (f32[3,36,16,128]{3,2,1,0:T(8,128)S(1)}, f32[3,36,16,128]{3,2,1,0:T(8,128)S(1)}, f32[36,16,128]{2,1,0:T(8,128)S(1)}, f32[3,36,16,128]{3,2,1,0:T(8,128)...) custom-call(f32[17,16,128]{2,1,0:T(8,128)S(1)} %copy-done.1, ...), custom_call_target="tpu_custom_call", output_to_operand_aliasing={{0}: (3, {}), {1}: (4, {}), {2}: (5, {}), {3}: (6, {}), {4}... | custom-call | tf_op jit(solution)/shard_map/down/pallas_call | solution.py:603
  19.4 0.1 collective-permute-start.2
  19.5 1.2 %collective-permute-done.2.msg_in_ref = f32[88,128]{1,0:T(8,128)S(1)} collective-permute-done((f32[88,128]{1,0:T(8,128)S(1)}, f32[88,128]{1,0:T(8,128)S(1)}, u32[]{:S(2)}, u32[]{:S(2)}) %collective-permute-start.2) | collective-permute-done | bytes 45088 | tf_op jit(solution)/shard_map/ppermute | solution.py:552
  20.7 0.1 slice_select_fusion.2
  20.8 1.6 %collective-permute-start.3 = (f32[104,128]{1,0:T(8,128)S(1)}, f32[104,128]{1,0:T(8,128)S(1)}, u32[]{:S(2)}, u32[]{:S(2)}) collective-permute-start(f32[104,128]{1,0:T(8,128)S(1)} %pad_maximum_fusion), channel_id=1, source_target_pairs={{0,15},{1,2},{2,1},{3,4},{4,3},{5,6},{6,5},{7,8},{8,7},{9,10},{10,... | collective-permute-start | bytes 159752 | tf_op jit(solution)/shard_map/ppermute | solution.py:566
  22.4 3.3 %collective-permute-done.3 = f32[104,128]{1,0:T(8,128)S(1)} collective-permute-done((f32[104,128]{1,0:T(8,128)S(1)}, f32[104,128]{1,0:T(8,128)S(1)}, u32[]{:S(2)}, u32[]{:S(2)}) %collective-permute-start.3) | collective-permute-done | bytes 53280 | tf_op jit(solution)/shard_map/ppermute | solution.py:566
  25.7 0.1 slice_select_fusion.1
  25.7 0.1 collective-permute-start.4
  25.9 4.8 %collective-permute-done.4 = f32[72,128]{1,0:T(8,128)S(1)} collective-permute-done((f32[72,128]{1,0:T(8,128)S(1)}, f32[72,128]{1,0:T(8,128)S(1)}, u32[]{:S(2)}, u32[]{:S(2)}) %collective-permute-start.4) | collective-permute-done | bytes 36896 | tf_op jit(solution)/shard_map/ppermute | solution.py:552
  30.7 0.1 constant_dynamic-update-slice_fusion
  30.8 0.0 collective-permute-start.5
  30.8 6.4 %collective-permute-done.5 = f32[136,128]{1,0:T(8,128)S(1)} collective-permute-done((f32[136,128]{1,0:T(8,128)S(1)}, f32[136,128]{1,0:T(8,128)S(1)}, u32[]{:S(2)}, u32[]{:S(2)}) %collective-permute-start.5) | collective-permute-done | bytes 69664 | tf_op jit(solution)/shard_map/ppermute | solution.py:552
  37.2 0.1 constant_dynamic-update-slice_fusion.5
  37.3 1.9 %collective-permute-start.6 = (f32[336,128]{1,0:T(8,128)S(1)}, f32[336,128]{1,0:T(8,128)S(1)}, u32[]{:S(2)}, u32[]{:S(2)}) collective-permute-start(f32[336,128]{1,0:T(8,128)S(1)} %slice_dynamic-update-slice_fusion.1.row_ref), channel_id=1, source_target_pairs={{0,16},{2,18},{4,20},{6,22},{8,24},{10,26},{12,28},{14,30},{16,32}... | collective-permute-start | bytes 516104 | tf_op jit(solution)/shard_map/ppermute | solution.py:572
  39.2 7.5 %collective-permute-done.6.far_ref = f32[336,128]{1,0:T(8,128)S(1)} collective-permute-done((f32[336,128]{1,0:T(8,128)S(1)}, f32[336,128]{1,0:T(8,128)S(1)}, u32[]{:S(2)}, u32[]{:S(2)}) %collective-permute-start.6) | collective-permute-done | bytes 172064 | tf_op jit(solution)/shard_map/ppermute | solution.py:572
  46.7 0.0 collective-permute-start.7
  46.7 1.4 %collective-permute-done.7.far2_ref = f32[336,128]{1,0:T(8,128)S(1)} collective-permute-done((f32[336,128]{1,0:T(8,128)S(1)}, f32[336,128]{1,0:T(8,128)S(1)}, u32[]{:S(2)}, u32[]{:S(2)}) %collective-permute-start.7) | collective-permute-done | bytes 172064 | tf_op jit(solution)/shard_map/ppermute | solution.py:552
  48.1 7.5 %up.1 = f32[3,16,16,128]{3,2,1,0:T(8,128)} custom-call(f32[336,128]{1,0:T(8,128)S(1)} %slice_dynamic-update-slice_fusion.1.row_ref, f32[336,128]{1,0:T(8,128)S(1)} %collective-permute-done.6.far_ref, f32[336,128]{1,0:T(8,128)S(1)} %collective-permute-done.7.far2_ref, f32[88,128]{1,0:T(8,128)S(1)} %collective-permute-done.2.msg_in_ref, ...), custom_call_target="tpu_custom_call" | custom-call | tf_op jit(solution)/shard_map/up/pallas_call | solution.py:639
  (12 shorter events, 0.1 us)
Async XLA Ops:
  0.0 12.4 %copy-start = (f32[3,16,16,128]{3,2,1,0:T(8,128)S(1)}, f32[3,16,16,128]{3,2,1,0:T(8,128)}, u32[]{:S(2)}) copy-start(f32[3,16,16,128]{3,2,1,0:T(8,128)} %load_ref.3) | copy-start | bytes 1179652
  2.1 12.2 %collective-permute-start = (f32[38,16,128]{2,1,0:T(8,128)}, f32[38,16,128]{2,1,0:T(8,128)S(1)}, u32[]{:S(2)}, u32[]{:S(2)}) collective-permute-start(f32[38,16,128]{2,1,0:T(8,128)} %get-tuple-element.26), channel_id=1, source_target_pairs={{0,1},{1,0},{2,3},{3,2},{4,5},{5,4},{6,7},{7,6},{8,9},{9,8},{10,11... | collective-permute-start | bytes 933896 | tf_op jit(solution)/shard_map/ppermute | solution.py:552
  2.2 15.0 %collective-permute-start.1 = (f32[38,16,128]{2,1,0:T(8,128)}, f32[38,16,128]{2,1,0:T(8,128)S(1)}, u32[]{:S(2)}, u32[]{:S(2)}) collective-permute-start(f32[38,16,128]{2,1,0:T(8,128)} %get-tuple-element.27), channel_id=1, source_target_pairs={{1,2},{2,1},{3,4},{4,3},{5,6},{6,5},{7,8},{8,7},{9,10},{10,9},{11,... | collective-permute-start | bytes 933896 | tf_op jit(solution)/shard_map/ppermute | solution.py:557
  12.5 0.9 %copy-start.1 = (f32[17,16,128]{2,1,0:T(8,128)S(1)}, f32[17,16,128]{2,1,0:T(8,128)}, u32[]{:S(2)}) copy-start(f32[17,16,128]{2,1,0:T(8,128)} %get-tuple-element.25.own_ref) | copy-start | bytes 417796
  19.4 1.3 %collective-permute-start.2 = (f32[88,128]{1,0:T(8,128)S(1)}, f32[88,128]{1,0:T(8,128)S(1)}, u32[]{:S(2)}, u32[]{:S(2)}) collective-permute-start(f32[88,128]{1,0:T(8,128)S(1)} %get-tuple-element.36), channel_id=1, source_target_pairs={{0,1},{1,0},{2,3},{3,2},{4,5},{5,4},{6,7},{7,6},{8,9},{9,8},{10,11... | collective-permute-start | bytes 135176 | tf_op jit(solution)/shard_map/ppermute | solution.py:552
  20.8 4.9 %collective-permute-start.3 = (f32[104,128]{1,0:T(8,128)S(1)}, f32[104,128]{1,0:T(8,128)S(1)}, u32[]{:S(2)}, u32[]{:S(2)}) collective-permute-start(f32[104,128]{1,0:T(8,128)S(1)} %pad_maximum_fusion), channel_id=1, source_target_pairs={{0,15},{1,2},{2,1},{3,4},{4,3},{5,6},{6,5},{7,8},{8,7},{9,10},{10,... | collective-permute-start | bytes 159752 | tf_op jit(solution)/shard_map/ppermute | solution.py:566
  25.7 4.9 %collective-permute-start.4 = (f32[72,128]{1,0:T(8,128)S(1)}, f32[72,128]{1,0:T(8,128)S(1)}, u32[]{:S(2)}, u32[]{:S(2)}) collective-permute-start(f32[72,128]{1,0:T(8,128)S(1)} %pad_maximum_fusion.1), channel_id=1, source_target_pairs={{0,4},{1,5},{2,6},{3,7},{4,0},{5,1},{6,2},{7,3},{8,12},{9,13},{10,... | collective-permute-start | bytes 110600 | tf_op jit(solution)/shard_map/ppermute | solution.py:552
  30.8 6.4 %collective-permute-start.5 = (f32[136,128]{1,0:T(8,128)S(1)}, f32[136,128]{1,0:T(8,128)S(1)}, u32[]{:S(2)}, u32[]{:S(2)}) collective-permute-start(f32[136,128]{1,0:T(8,128)S(1)} %constant_dynamic-update-slice_fusion), channel_id=1, source_target_pairs={{0,12},{1,13},{2,14},{3,15},{4,8},{5,9},{6,10},{7,11},{8,4},{9,5},... | collective-permute-start | bytes 208904 | tf_op jit(solution)/shard_map/ppermute | solution.py:552
  37.3 9.4 %collective-permute-start.6 = (f32[336,128]{1,0:T(8,128)S(1)}, f32[336,128]{1,0:T(8,128)S(1)}, u32[]{:S(2)}, u32[]{:S(2)}) collective-permute-start(f32[336,128]{1,0:T(8,128)S(1)} %slice_dynamic-update-slice_fusion.1.row_ref), channel_id=1, source_target_pairs={{0,16},{2,18},{4,20},{6,22},{8,24},{10,26},{12,28},{14,30},{16,32}... | collective-permute-start | bytes 516104 | tf_op jit(solution)/shard_map/ppermute | solution.py:572
  46.7 1.4 %collective-permute-start.7 = (f32[336,128]{1,0:T(8,128)S(1)}, f32[336,128]{1,0:T(8,128)S(1)}, u32[]{:S(2)}, u32[]{:S(2)}) collective-permute-start(f32[336,128]{1,0:T(8,128)S(1)} %collective-permute-done.6.far_ref), channel_id=1, source_target_pairs={{0,1},{1,0},{2,3},{3,2},{4,5},{5,4},{6,7},{7,6},{8,9},{9,8},{10,11... | collective-permute-start | bytes 516104 | tf_op jit(solution)/shard_map/ppermute | solution.py:552

commit v4 on v3

--- a/solution.py
+++ b/solution.py
@@ -144,7 +144,31 @@
         t_ref[c, k] = total
 
 
-def inner_kernel(load_ref, own_ref, b_ref, beta_ref, root0_ref, va_ref, d_ref, vb_ref, v0_ref, t_ref):
+def side0(before, message, own_solid, b_ref, beta_ref, root0_ref, va_ref, d_ref, vb_ref, v0_ref, t_ref):
+    side_solid = message[37]
+
+    def at(after_e, before_e):
+        return after_e + before * (before_e - after_e)
+
+    first = at(26, 0)
+    for j in range(HALO):
+        root0_ref[first + j] = safe(message[27 + j])
+    first = at(26, 1)
+    for j in range(9):
+        scale = side_solid / (center * root0_ref[first + j])
+        start0(first + j, [message[9 * c + j] for c in range(3)], scale, b_ref, beta_ref, va_ref)
+    sign = at(1, -1)
+    for j in range(9):
+        first0(at(25, 10) + sign * j, own_solid if j < 1 else side_solid, beta_ref, va_ref, d_ref, vb_ref)
+    for j in range(9):
+        second0(at(24, 11) + sign * j, own_solid if j < 2 else side_solid, beta_ref, vb_ref, d_ref, v0_ref)
+    for j in range(5):
+        sol = own_solid if j < 2 else side_solid
+        residual0(at(9, 4) + sign * j, (sol, sol), root0_ref, b_ref, v0_ref, t_ref)
+
+
+def inner_kernel(load_ref, own_ref, x_ref, b_ref, beta_ref, root0_ref, va_ref, d_ref, vb_ref, v0_ref, t_ref):
+    odd = lax.axis_index("bricks") & 1
     solid = own_ref[16]
 
     def start(z, _):
@@ -173,61 +197,26 @@
         return 0
 
     lax.fori_loop(5, 9, resid, 0, unroll=4)
+    side0(odd, x_ref, solid, b_ref, beta_ref, root0_ref, va_ref, d_ref, vb_ref, v0_ref, t_ref)
 
 
 def down_kernel(
-    own_ref, x_ref, o_ref, b_in, beta_in, root_in, va_in, d_in, vb_in, v0_in, t_in,
+    own_ref, x_solid_ref, o_ref, b_in, beta_in, root_in, va_in, d_in, vb_in, v0_in, t_in,
     b_ref, beta0_ref, root0_ref, va_ref, d_ref, vb_ref, v0_ref, t_s,
     msg_ref, edge_ref, v1_ref, beta1_ref, root1_ref, sol_ref,
-    sol_s, tr_s,
+    tr_s,
 ):
     odd = lax.axis_index("bricks") & 1
     is_odd = odd == 1
-
-    def left(k):
-        return jnp.where(is_odd, x_ref[k], o_ref[k])
-
-    def right(k):
-        return jnp.where(is_odd, o_ref[k], x_ref[k])
-
     own_solid = own_ref[16]
-    left_solid, right_solid = left(37), right(37)
+    x_solid, o_solid = x_solid_ref[37], o_ref[37]
+    left_solid = jnp.where(is_odd, x_solid, o_solid)
+    right_solid = jnp.where(is_odd, o_solid, x_solid)
     sol_ref[...] = jnp.zeros((8, 128), F32)
     sol_ref[0:1, :] = left_solid[:1]
     sol_ref[1:2, :] = own_solid[:1]
     sol_ref[2:3, :] = right_solid[:1]
-    for j in range(HALO):
-        sol_s[j] = left_solid
-        sol_s[26 + j] = right_solid
-        sol_s[HALO + j if j < 5 else 16 + j] = own_solid
-        root0_ref[j] = safe(left(27 + j))
-        root0_ref[26 + j] = safe(right(27 + j))
-    for j in range(9):
-        for e, side, solid in ((1 + j, left, left_solid), (26 + j, right, right_solid)):
-            scale = solid / (center * root0_ref[e])
-            start0(e, [side(9 * c + j) for c in range(3)], scale, b_ref, beta0_ref, va_ref)
-
-    def app1(j, _):
-        for e in (2 + j, 25 + j):
-            first0(e, sol_s[e], beta0_ref, va_ref, d_ref, vb_ref)
-        return 0
-
-    lax.fori_loop(0, 9, app1, 0, unroll=9)
-
-    def app2(j, _):
-        for e in (3 + j, 24 + j):
-            second0(e, sol_s[e], beta0_ref, vb_ref, d_ref, v0_ref)
-        return 0
-
-    lax.fori_loop(0, 9, app2, 0, unroll=9)
-
-    def resid(j, _):
-        for k in (j, 9 + j):
-            e = 4 + 2 * k
-            residual0(k, (sol_s[e], sol_s[e + 1]), root0_ref, b_ref, v0_ref, t_s)
-        return 0
-
-    lax.fori_loop(0, 5, resid, 0, unroll=5)
+    side0(1 - odd, o_ref, own_solid, b_ref, beta0_ref, root0_ref, va_ref, d_ref, vb_ref, v0_ref, t_s)
 
     def root_pair(k, _):
         tr_s[k] = root0_ref[2 * k] + root0_ref[2 * k + 1]
@@ -300,8 +289,8 @@
 def up_kernel(
     row_ref, far_ref, far2_ref, msg_in_ref,
     v0_ref, beta0_ref, root0_ref, v1_ref, beta1_ref, root1_ref, sol_ref,
-    out_ref,
-    all_s, solid_s, w_s, f_s, e2_s, pe_s, a_s, bb_s, d_s,
+    out_hbm,
+    all_s, solid_s, w_s, coef_s, f_s, e2_s, pe_s, a_s, bb_s, d_s, out_ref, sems,
 ):
     me = lax.axis_index("bricks")
     odd = me & 1
@@ -317,21 +306,24 @@
     solid_s[0:16, :] = jnp.where(is_odd, far2, far)
     solid_s[16:32, :] = row_ref[256:272, :]
     solid_s[32:48, :] = jnp.where(is_odd, far, far2)
-    base = me - odd - 16
+    chip0 = (me >> 1) - 8
     here = (me >> 1) & 7
-    for w in range(34):
-        dev = base + w
-        rel = (dev >> 4) - (me >> 4)
-        chip = (dev >> 1) & 7
+    low_rows = iota((8, 128), 0) < 4
+    for w in range(17):
+        chip = chip0 + w
+        rel = (chip >> 3) - (me >> 4)
         holder = jnp.where(rel == 0, odd, jnp.where(rel < 0, 0, 1))
         beside = (chip ^ here) & 1
-        via = (chip + beside * (1 - 2 * holder)) & 7
-        x = via ^ here
-        block = ((w & 1) ^ holder ^ beside) + 2 * beside + 4 * (((x >> 1) ^ (x >> 2)) & 1) + 8 * (x >> 2)
-        slot = (rel + 1) * 16 + block
-        for c in range(4):
-            w_s[c, 4 * w : 4 * w + 4, :] = all_s[slot, 4 * c : 4 * c + 4, :]
-        w_s[4, 4 * w : 4 * w + 4, :] = jnp.broadcast_to(solid_s[pl.ds(slot, 1), :], (4, 128))
+        x = ((chip + beside * (1 - 2 * holder)) ^ here) & 7
+        slot = (rel + 1) * 16 + 2 * beside + 4 * (((x >> 1) ^ (x >> 2)) & 1) + 8 * (x >> 2)
+        flip = holder ^ beside
+        blocks = (slot + flip, slot + 1 - flip)
+        for half in range(2):
+            first, second = (all_s[block, 8 * half : 8 * half + 8, :] for block in blocks)
+            w_s[2 * half, 8 * w : 8 * w + 8, :] = jnp.where(low_rows, first, pltpu.roll(second, 4, 0))
+            w_s[2 * half + 1, 8 * w : 8 * w + 8, :] = jnp.where(low_rows, pltpu.roll(first, 4, 0), second)
+        solid = (jnp.broadcast_to(solid_s[pl.ds(block, 1), :], (8, 128)) for block in blocks)
+        w_s[4, 8 * w : 8 * w + 8, :] = jnp.where(low_rows, *solid)
 
     lane = iota((1, 1, 128), 2)
 
@@ -349,14 +341,15 @@
     def stencil(v, level):
         n = v.shape[1]
         s = v + pltpu.roll(v, 1, 1) + pltpu.roll(v, n - 1, 1)
-        if level == 2:
-            s = s + masks_x[0] * pltpu.roll(s, 32, 2) + masks_x[1] * pltpu.roll(s, 96, 2)
-        else:
-            s = s + pltpu.roll(s, 64, 2)
         step = 2 ** (level - 2)
         low, high = masks_y[level]
-        s = s + low * pltpu.roll(s, step, 2) + high * pltpu.roll(s, 128 - step, 2)
-        return 27.5 * v - s
+        if level > 2:
+            beside = low * (pltpu.roll(s, step, 2) + pltpu.roll(s, 64 + step, 2))
+            beside = beside + high * (pltpu.roll(s, 128 - step, 2) + pltpu.roll(s, 64 - step, 2))
+            return (27.5 * v - (s + pltpu.roll(s, 64, 2))) - beside
+        lower, upper = masks_x
+        s = s + lower * pltpu.roll(s, 32, 2) + upper * pltpu.roll(s, 96, 2)
+        return 27.5 * v - (s + low * pltpu.roll(s, 1, 2) + high * pltpu.roll(s, 127, 2))
 
     def first(beta, m, level):
         v = beta * INV_MID
@@ -373,13 +366,13 @@
         d = A2 * d + C2 * (beta - m * stencil(v, level))
         return v + d
 
-    def coarsen(values, level):
+    def coarsen(values, level, room):
         k, n = values.shape[:2]
         half = (n // 2 + 7) // 8 * 8
         if 2 * half > n:
-            f_s[0:k, n : 2 * half, :] = jnp.zeros((k, 2 * half - n, 128), F32)
-        f_s[0:k, 0:n, :] = values
-        s = f_s[0:k, pl.ds(0, half, 2), :] + f_s[0:k, pl.ds(1, half, 2), :]
+            room[0:k, n : 2 * half, :] = jnp.zeros((k, 2 * half - n, 128), F32)
+        room[0:k, 0:n, :] = values
+        s = room[0:k, pl.ds(0, half, 2), :] + room[0:k, pl.ds(1, half, 2), :]
         s = lane_pair(s, 2 ** (level - 2))
         if level == 2:
             return lane_pair(s, 32) * 0.125
@@ -394,7 +387,7 @@
     both = w_s[3:5]
     roots, sols = {2: safe(both[0:1])}, {2: both[1:2]}
     for level in (2, 3, 4):
-        both = coarsen(jnp.concatenate([roots[level], sols[level]], axis=0), level)
+        both = coarsen(jnp.concatenate([roots[level], sols[level]], axis=0), level, coef_s)
         roots[level + 1], sols[level + 1] = safe(both[0:1]), both[1:2]
     sol5 = sols[5]
     sol5_safe = jnp.where(sol5 > 0.0, sol5, 1.0)
@@ -413,7 +406,7 @@
         v = first(beta, masks[level], level)
         r = b - (sols[level] * roots[level]) * (scale27 * (0.25**level / 27.0)) * stencil(v, level)
         betas[level], vs[level] = beta, v
-        b = coarsen(r, level)
+        b = coarsen(r, level, f_s)
     e = first(b * scales[5], masks[5], 5) * g5
     first_row = 0
     for level in (4, 3, 2):
@@ -485,30 +478,27 @@
 
     shift = HALO - 4
 
+    broad = {name: jnp.broadcast_to(row, (16, 128)) for name, row in rows.items()}
+
     def sol0(k):
-        row = jnp.where(k < 4, rows["left"], jnp.where(k < 20, rows["own"], rows["right"]))
-        return jnp.broadcast_to(row, (16, 128))
-
-    def begin(k, _):
+        return broad["left"] if k < 4 else broad["own"] if k < 20 else broad["right"]
+
+    for k in range(1, 23):
         g = root0_ref[k + shift] * sol0(k)
         for c in range(3):
             a_s[c, k] = v0_ref[c, k + shift] + g * pe_s[c, k >> 1]
-        return 0
-
-    lax.fori_loop(1, 23, begin, 0, unroll=11)
-
-    def app0(k, _):
+
+
+    for k in range(2, 22):
         sol = sol0(k)
         for c in range(3):
             v, t = stencil0(a_s, c, k)
             d = INV_MID * (beta0_ref[c, k + shift] - (sol * (kappa[c] / 26.5)) * t)
             d_s[c, k] = d
             bb_s[c, k] = v + d
-        return 0
-
-    lax.fori_loop(2, 22, app0, 0, unroll=10)
-
-    def app1(k, _):
+
+
+    for k in range(3, 21):
         sol = sol0(k)
         for c in range(3):
             v, t = stencil0(bb_s, c, k)
@@ -516,12 +506,11 @@
             d = A1 * d_s[c, k] + C1 * pre
             d_s[c, k] = d
             a_s[c, k] = v + d
-        return 0
-
-    lax.fori_loop(3, 21, app1, 0, unroll=9)
+
     own_solid = jnp.broadcast_to(rows["own"], (16, 128))
 
-    def app2(k, _):
+    copies = []
+    for k in range(4, 20):
         inverse = 1.0 / root0_ref[k + shift]
         x = []
         for c in range(3):
@@ -533,9 +522,13 @@
         out_ref[0, k - 4] = x[0] + third
         out_ref[1, k - 4] = x[1] + third
         out_ref[2, k - 4] = third - x[0] - x[1]
-        return 0
-
-    lax.fori_loop(4, 20, app2, 0, unroll=8)
+        if k % 4 == 3:
+            part = pl.ds(k - 7, 4)
+            copy = pltpu.make_async_copy(out_ref.at[:, part], out_hbm.at[:, part], sems.at[k // 4 - 1])
+            copy.start()
+            copies.append(copy)
+    for copy in copies:
+        copy.wait()
 
 
 VMEM = pl.BlockSpec(memory_space=pltpu.VMEM)
@@ -594,12 +587,12 @@
     inner = pl.pallas_call(
         inner_kernel,
         out_shape=fine,
-        in_specs=[VMEM] * 2,
+        in_specs=[VMEM] * 3,
         out_specs=(VMEM,) * 8,
         compiler_params=PARAMS,
         cost_estimate=pl.CostEstimate(flops=10_000_000, bytes_accessed=4_000_000, transcendentals=0),
         name="inner",
-    )(load_field, root)
+    )(load_field, root, x_in)
     _, beta0, root0, _, _, _, v0, _, msg, edge, v1, beta1, root1, solid_rows = pl.pallas_call(
         down_kernel,
         out_shape=fine
@@ -611,7 +604,6 @@
         out_specs=(VMEM,) * 14,
         input_output_aliases={3 + k: k for k in range(8)},
         scratch_shapes=[
-            pltpu.VMEM((EXT, 16, 128), F32),
             pltpu.VMEM((18, 16, 128), F32),
         ],
         compiler_params=PARAMS,
@@ -640,17 +632,20 @@
         up_kernel,
         out_shape=shaped(3, 16, 16, 128),
         in_specs=[VMEM] * 11,
-        out_specs=VMEM,
+        out_specs=HBM,
         scratch_shapes=[
             pltpu.VMEM((48, 16, 128), F32),
             pltpu.VMEM((48, 128), F32),
             pltpu.VMEM((5, 136, 128), F32),
+            pltpu.VMEM((2, 144, 128), F32),
             pltpu.VMEM((3, 144, 128), F32),
             pltpu.VMEM((3, 24, 128), F32),
             pltpu.VMEM((3, 12, 16, 128), F32),
             pltpu.VMEM((3, 24, 16, 128), F32),
             pltpu.VMEM((3, 24, 16, 128), F32),
             pltpu.VMEM((3, 24, 16, 128), F32),
+            pltpu.VMEM((3, 16, 16, 128), F32),
+            pltpu.SemaphoreType.DMA((4,)),
         ],
         compiler_params=PARAMS,
         name="up",

time: 56.1 us -> 54.7 us (0.975)
  waiting for transfers between devices: 27.5 us -> 26.8 us
  Pallas kernels: 12.7 us -> 12.1 us
    pallas_call x1, Pallas kernels: 7.5 us -> 6.76 us  [body(): pl.pallas_call(up_kernel, out_shape=shaped(3, 16, 16, 128), in_specs=[VME...]
    ppermute x1, waiting for transfers between devices: 2.86 us -> 2.21 us  [swap_before(): lax.ppermute(values, 'bricks', [(i, i + 1 if i % 2 else i - 1) for i in r...]
    pallas_call x1, Pallas kernels: 0.97 us -> 1.62 us  [body(): pl.pallas_call(inner_kernel, out_shape=fine, in_specs=[VMEM] * 3, out_spe...]
    pallas_call x1, Pallas kernels: 2.18 us -> 1.6 us  [body(): pl.pallas_call(down_kernel, out_shape=fine + (shaped(88, 128), shaped(64,...]
  transfers between devices with their start and end apart: 8 -> 8, of which waited for: 7 -> 7; matrix products, arithmetic and copies ran while one was open for 0% -> 0% of each run, Pallas kernels for 2% -> 3%
where the time goes in v4:
time: 54.7 us; the launch traced here: 54.3 us
  waiting for transfers between devices  26.8 us (49%)
  starting transfers between devices  14 us (26%)
  Pallas kernels  12.1 us (22%)
  local copies, waits for them, and re-layouts  0.93 us (2%)
    ppermute x5, waiting for transfers between devices, swap_bits(): return lax.ppermute(values, 'bricks', [(i, i ^ bits) for i in range(n)])  13.8 us
    ppermute x1, starting transfers between devices, swap_before(): lax.ppermute(values, 'bricks', [(i, i + 1 if i % 2 else i - 1) for i in r...  10.2 us
    ppermute x1, waiting for transfers between devices, next_rows(): lax.ppermute(values, 'bricks', [(i, j) for i, j in pairs if 0 <= j < n])  7.48 us
    pallas_call x1, Pallas kernels, body(): pl.pallas_call(up_kernel, out_shape=shaped(3, 16, 16, 128), in_specs=[VME...  6.76 us
    ppermute x1, waiting for transfers between devices, swap_ring(): return lax.ppermute(values, 'bricks', sorted(pairs))  3.3 us
    ppermute x1, waiting for transfers between devices, swap_before(): lax.ppermute(values, 'bricks', [(i, i + 1 if i % 2 else i - 1) for i in r...  2.21 us
    pallas_call x1, Pallas kernels, body(): pl.pallas_call(pack_kernel, out_shape=(shaped(38, 16, 128), shaped(38, 16...  2.1 us
    ppermute x1, starting transfers between devices, next_rows(): lax.ppermute(values, 'bricks', [(i, j) for i, j in pairs if 0 <= j < n])  1.91 us
  transfers between devices with their start and end apart: 8, of which 7 were waited for; matrix products, arithmetic and copies ran while one was open for 0% of the time, Pallas kernels for 3%

profile of v4, /device:TPU:24, one launch (start us, length us, event | category | flops | bytes accessed | tf_op | source)
XLA Modules:
  0.0 54.3 jit_solution(7607012568856123099)
XLA Ops:
  0.0 0.0 copy-start
  0.0 2.1 %pack.1 = (f32[38,16,128]{2,1,0:T(8,128)}, f32[38,16,128]{2,1,0:T(8,128)}, f32[17,16,128]{2,1,0:T(8,128)}) custom-call(f32[3,16,16,128]{3,2,1,0:T(8,128)} %load_ref.3, s32[16,16,128]{2,1,0:T(8,128)} %class_ref.1, s32[1,1,8]{2,1,0:T(1,128)} %occ_ref.1, f32[8]{0:T(128)} %moduli_ref.1), custom_call_target="tpu_custom_call" | custom-call | tf_op jit(solution)/shard_map/pack/pallas_call | solution.py:569
  2.1 0.1 collective-permute-start
  2.2 10.2 %collective-permute-start.1 = (f32[38,16,128]{2,1,0:T(8,128)}, f32[38,16,128]{2,1,0:T(8,128)S(1)}, u32[]{:S(2)}, u32[]{:S(2)}) collective-permute-start(f32[38,16,128]{2,1,0:T(8,128)} %get-tuple-element.27), channel_id=1, source_target_pairs={{1,2},{2,1},{3,4},{4,3},{5,6},{6,5},{7,8},{8,7},{9,10},{10,9},{11,... | collective-permute-start | bytes 933896 | tf_op jit(solution)/shard_map/ppermute | solution.py:550
  12.5 0.0 collective-permute-done.x_ref.x_solid_ref
  12.5 0.0 copy-done
  12.5 0.0 copy-start.1
  12.5 0.9 %copy-done.1 = f32[17,16,128]{2,1,0:T(8,128)S(1)} copy-done((f32[17,16,128]{2,1,0:T(8,128)S(1)}, f32[17,16,128]{2,1,0:T(8,128)}, u32[]{:S(2)}) %copy-start.1) | copy-done | bytes 139288
  13.4 1.6 %inner.1 = (f32[3,36,16,128]{3,2,1,0:T(8,128)S(1)}, f32[3,36,16,128]{3,2,1,0:T(8,128)S(1)}, f32[36,16,128]{2,1,0:T(8,128)S(1)}, f32[3,36,16,128]{3,2,1,0:T(8,128...) custom-call(f32[3,16,16,128]{3,2,1,0:T(8,128)S(1)} %copy-done, ...), custom_call_target="tpu_custom_call" | custom-call | flops 10000000 | bytes 4000000 | tf_op jit(solution)/shard_map/inner/pallas_call | solution.py:587
  15.0 2.2 %collective-permute-done.1.o_ref = f32[38,16,128]{2,1,0:T(8,128)S(1)} collective-permute-done((f32[38,16,128]{2,1,0:T(8,128)}, f32[38,16,128]{2,1,0:T(8,128)S(1)}, u32[]{:S(2)}, u32[]{:S(2)}) %collective-permute-start.1) | collective-permute-done | bytes 311328 | tf_op jit(solution)/shard_map/ppermute | solution.py:550
  17.2 1.6 %down.1 = (f32[3,36,16,128]{3,2,1,0:T(8,128)S(1)}, f32[3,36,16,128]{3,2,1,0:T(8,128)S(1)}, f32[36,16,128]{2,1,0:T(8,128)S(1)}, f32[3,36,16,128]{3,2,1,0:T(8,128)...) custom-call(f32[17,16,128]{2,1,0:T(8,128)S(1)} %copy-done.1, ...), custom_call_target="tpu_custom_call", output_to_operand_aliasing={{0}: (3, {}), {1}: (4, {}), {2}: (5, {}), {3}: (6, {}), {4}... | custom-call | tf_op jit(solution)/shard_map/down/pallas_call | solution.py:596
  18.8 0.1 collective-permute-start.2
  18.9 1.2 %collective-permute-done.2.msg_in_ref = f32[88,128]{1,0:T(8,128)S(1)} collective-permute-done((f32[88,128]{1,0:T(8,128)S(1)}, f32[88,128]{1,0:T(8,128)S(1)}, u32[]{:S(2)}, u32[]{:S(2)}) %collective-permute-start.2) | collective-permute-done | bytes 45088 | tf_op jit(solution)/shard_map/ppermute | solution.py:545
  20.1 0.1 slice_select_fusion.2
  20.2 1.6 %collective-permute-start.3 = (f32[104,128]{1,0:T(8,128)S(1)}, f32[104,128]{1,0:T(8,128)S(1)}, u32[]{:S(2)}, u32[]{:S(2)}) collective-permute-start(f32[104,128]{1,0:T(8,128)S(1)} %pad_maximum_fusion), channel_id=1, source_target_pairs={{0,15},{1,2},{2,1},{3,4},{4,3},{5,6},{6,5},{7,8},{8,7},{9,10},{10,... | collective-permute-start | bytes 159752 | tf_op jit(solution)/shard_map/ppermute | solution.py:559
  21.8 3.3 %collective-permute-done.3 = f32[104,128]{1,0:T(8,128)S(1)} collective-permute-done((f32[104,128]{1,0:T(8,128)S(1)}, f32[104,128]{1,0:T(8,128)S(1)}, u32[]{:S(2)}, u32[]{:S(2)}) %collective-permute-start.3) | collective-permute-done | bytes 53280 | tf_op jit(solution)/shard_map/ppermute | solution.py:559
  25.1 0.1 slice_select_fusion.1
  25.2 0.1 collective-permute-start.4
  25.3 4.8 %collective-permute-done.4 = f32[72,128]{1,0:T(8,128)S(1)} collective-permute-done((f32[72,128]{1,0:T(8,128)S(1)}, f32[72,128]{1,0:T(8,128)S(1)}, u32[]{:S(2)}, u32[]{:S(2)}) %collective-permute-start.4) | collective-permute-done | bytes 36896 | tf_op jit(solution)/shard_map/ppermute | solution.py:545
  30.1 0.1 constant_dynamic-update-slice_fusion
  30.2 0.0 collective-permute-start.5
  30.2 6.4 %collective-permute-done.5 = f32[136,128]{1,0:T(8,128)S(1)} collective-permute-done((f32[136,128]{1,0:T(8,128)S(1)}, f32[136,128]{1,0:T(8,128)S(1)}, u32[]{:S(2)}, u32[]{:S(2)}) %collective-permute-start.5) | collective-permute-done | bytes 69664 | tf_op jit(solution)/shard_map/ppermute | solution.py:545
  36.6 0.1 constant_dynamic-update-slice_fusion.5
  36.7 1.9 %collective-permute-start.6 = (f32[336,128]{1,0:T(8,128)S(1)}, f32[336,128]{1,0:T(8,128)S(1)}, u32[]{:S(2)}, u32[]{:S(2)}) collective-permute-start(f32[336,128]{1,0:T(8,128)S(1)} %slice_dynamic-update-slice_fusion.1.row_ref), channel_id=1, source_target_pairs={{0,16},{2,18},{4,20},{6,22},{8,24},{10,26},{12,28},{14,30},{16,32}... | collective-permute-start | bytes 516104 | tf_op jit(solution)/shard_map/ppermute | solution.py:565
  38.6 7.5 %collective-permute-done.6.far_ref = f32[336,128]{1,0:T(8,128)S(1)} collective-permute-done((f32[336,128]{1,0:T(8,128)S(1)}, f32[336,128]{1,0:T(8,128)S(1)}, u32[]{:S(2)}, u32[]{:S(2)}) %collective-permute-start.6) | collective-permute-done | bytes 172064 | tf_op jit(solution)/shard_map/ppermute | solution.py:565
  46.1 0.0 collective-permute-start.7
  46.1 1.4 %collective-permute-done.7.far2_ref = f32[336,128]{1,0:T(8,128)S(1)} collective-permute-done((f32[336,128]{1,0:T(8,128)S(1)}, f32[336,128]{1,0:T(8,128)S(1)}, u32[]{:S(2)}, u32[]{:S(2)}) %collective-permute-start.7) | collective-permute-done | bytes 172064 | tf_op jit(solution)/shard_map/ppermute | solution.py:545
  47.5 6.8 %up.1 = f32[3,16,16,128]{3,2,1,0:T(8,128)} custom-call(f32[336,128]{1,0:T(8,128)S(1)} %slice_dynamic-update-slice_fusion.1.row_ref, f32[336,128]{1,0:T(8,128)S(1)} %collective-permute-done.6.far_ref, f32[336,128]{1,0:T(8,128)S(1)} %collective-permute-done.7.far2_ref, f32[88,128]{1,0:T(8,128)S(1)} %collective-permute-done.2.msg_in_ref, ...), custom_call_target="tpu_custom_call" | custom-call | tf_op jit(solution)/shard_map/up/pallas_call | solution.py:631
  (12 shorter events, 0.1 us)
Async XLA Ops:
  0.0 12.5 %copy-start = (f32[3,16,16,128]{3,2,1,0:T(8,128)S(1)}, f32[3,16,16,128]{3,2,1,0:T(8,128)}, u32[]{:S(2)}) copy-start(f32[3,16,16,128]{3,2,1,0:T(8,128)} %load_ref.3) | copy-start | bytes 1179652
  2.1 10.4 %collective-permute-start = (f32[38,16,128]{2,1,0:T(8,128)}, f32[38,16,128]{2,1,0:T(8,128)S(1)}, u32[]{:S(2)}, u32[]{:S(2)}) collective-permute-start(f32[38,16,128]{2,1,0:T(8,128)} %get-tuple-element.26), channel_id=1, source_target_pairs={{0,1},{1,0},{2,3},{3,2},{4,5},{5,4},{6,7},{7,6},{8,9},{9,8},{10,11... | collective-permute-start | bytes 933896 | tf_op jit(solution)/shard_map/ppermute | solution.py:545
  2.2 15.0 %collective-permute-start.1 = (f32[38,16,128]{2,1,0:T(8,128)}, f32[38,16,128]{2,1,0:T(8,128)S(1)}, u32[]{:S(2)}, u32[]{:S(2)}) collective-permute-start(f32[38,16,128]{2,1,0:T(8,128)} %get-tuple-element.27), channel_id=1, source_target_pairs={{1,2},{2,1},{3,4},{4,3},{5,6},{6,5},{7,8},{8,7},{9,10},{10,9},{11,... | collective-permute-start | bytes 933896 | tf_op jit(solution)/shard_map/ppermute | solution.py:550
  12.5 0.9 %copy-start.1 = (f32[17,16,128]{2,1,0:T(8,128)S(1)}, f32[17,16,128]{2,1,0:T(8,128)}, u32[]{:S(2)}) copy-start(f32[17,16,128]{2,1,0:T(8,128)} %get-tuple-element.25.own_ref) | copy-start | bytes 417796
  18.8 1.3 %collective-permute-start.2 = (f32[88,128]{1,0:T(8,128)S(1)}, f32[88,128]{1,0:T(8,128)S(1)}, u32[]{:S(2)}, u32[]{:S(2)}) collective-permute-start(f32[88,128]{1,0:T(8,128)S(1)} %get-tuple-element.36), channel_id=1, source_target_pairs={{0,1},{1,0},{2,3},{3,2},{4,5},{5,4},{6,7},{7,6},{8,9},{9,8},{10,11... | collective-permute-start | bytes 135176 | tf_op jit(solution)/shard_map/ppermute | solution.py:545
  20.2 4.9 %collective-permute-start.3 = (f32[104,128]{1,0:T(8,128)S(1)}, f32[104,128]{1,0:T(8,128)S(1)}, u32[]{:S(2)}, u32[]{:S(2)}) collective-permute-start(f32[104,128]{1,0:T(8,128)S(1)} %pad_maximum_fusion), channel_id=1, source_target_pairs={{0,15},{1,2},{2,1},{3,4},{4,3},{5,6},{6,5},{7,8},{8,7},{9,10},{10,... | collective-permute-start | bytes 159752 | tf_op jit(solution)/shard_map/ppermute | solution.py:559
  25.2 4.9 %collective-permute-start.4 = (f32[72,128]{1,0:T(8,128)S(1)}, f32[72,128]{1,0:T(8,128)S(1)}, u32[]{:S(2)}, u32[]{:S(2)}) collective-permute-start(f32[72,128]{1,0:T(8,128)S(1)} %pad_maximum_fusion.1), channel_id=1, source_target_pairs={{0,4},{1,5},{2,6},{3,7},{4,0},{5,1},{6,2},{7,3},{8,12},{9,13},{10,... | collective-permute-start | bytes 110600 | tf_op jit(solution)/shard_map/ppermute | solution.py:545
  30.2 6.4 %collective-permute-start.5 = (f32[136,128]{1,0:T(8,128)S(1)}, f32[136,128]{1,0:T(8,128)S(1)}, u32[]{:S(2)}, u32[]{:S(2)}) collective-permute-start(f32[136,128]{1,0:T(8,128)S(1)} %constant_dynamic-update-slice_fusion), channel_id=1, source_target_pairs={{0,12},{1,13},{2,14},{3,15},{4,8},{5,9},{6,10},{7,11},{8,4},{9,5},... | collective-permute-start | bytes 208904 | tf_op jit(solution)/shard_map/ppermute | solution.py:545
  36.7 9.4 %collective-permute-start.6 = (f32[336,128]{1,0:T(8,128)S(1)}, f32[336,128]{1,0:T(8,128)S(1)}, u32[]{:S(2)}, u32[]{:S(2)}) collective-permute-start(f32[336,128]{1,0:T(8,128)S(1)} %slice_dynamic-update-slice_fusion.1.row_ref), channel_id=1, source_target_pairs={{0,16},{2,18},{4,20},{6,22},{8,24},{10,26},{12,28},{14,30},{16,32}... | collective-permute-start | bytes 516104 | tf_op jit(solution)/shard_map/ppermute | solution.py:565
  46.1 1.4 %collective-permute-start.7 = (f32[336,128]{1,0:T(8,128)S(1)}, f32[336,128]{1,0:T(8,128)S(1)}, u32[]{:S(2)}, u32[]{:S(2)}) collective-permute-start(f32[336,128]{1,0:T(8,128)S(1)} %collective-permute-done.6.far_ref), channel_id=1, source_target_pairs={{0,1},{1,0},{2,3},{3,2},{4,5},{5,4},{6,7},{7,6},{8,9},{9,8},{10,11... | collective-permute-start | bytes 516104 | tf_op jit(solution)/shard_map/ppermute | solution.py:545

commit v5 on v4

--- a/solution.py
+++ b/solution.py
@@ -261,24 +261,31 @@
         msg_ref[24 + 8 * k : 32 + 8 * k, :] = jnp.where(is_odd, before, after)
         edge_ref[8 * k : 8 * k + 8, :] = jnp.where(is_odd, after, before)
 
+    b1 = [
+        lane_pair(t_s[c, :, pl.ds(0, 8, 2), :] + t_s[c, :, pl.ds(1, 8, 2), :], 1) * 0.125 for c in range(3)
+    ]
+    m = [sol * (kappa[c] / 26.5) for c in (0, 2)]
+    m = [m[0], m[0], m[1]]
+    beta = [b1[c] * scale1 for c in range(3)]
+    v = [beta[c] * INV_MID for c in range(3)]
+    d = list(v)
+    for a, b in ((A1, C1), (A2, C2)):
+        t = [stencil1(v[c]) for c in range(3)]
+        for c in range(3):
+            d[c] = a * d[c] + b * (beta[c] - m[c] * t[c])
+            v[c] = v[c] + d[c]
+    t = [stencil1(v[c])[3:11] for c in range(3)]
+    g = (sol * rt)[3:11]
     for c in range(3):
-        b1 = lane_pair(t_s[c, :, pl.ds(0, 8, 2), :] + t_s[c, :, pl.ds(1, 8, 2), :], 1) * 0.125
-        beta = b1 * scale1
-        m = sol * (kappa[c] / 26.5)
-        v = beta * INV_MID
-        d = A1 * v + C1 * (beta - m * stencil1(v))
-        v = v + d
-        d = A2 * d + C2 * (beta - m * stencil1(v))
-        v = v + d
-        v1_ref[c] = v
-        beta1_ref[c] = beta
-        r = (b1 - (sol * rt) * (0.25 * kappa[c] / 27.0) * stencil1(v))[3:11]
+        v1_ref[c] = v[c]
+        beta1_ref[c] = beta[c]
+        r = b1[c][3:11] - g * (0.25 * kappa[c] / 27.0) * t[c]
         for z in range(4):
             msg_ref[4 * c + z : 4 * c + z + 1, :] = compact(r[2 * z] + r[2 * z + 1])
         for j in range(2):
-            send_edge(2 * c + j, pair(v[6 + 2 * j], v[7 + 2 * j]), pair(v[4 + 2 * j], v[5 + 2 * j]))
-        to_after.append(beta[7])
-        to_before.append(beta[6])
+            send_edge(2 * c + j, pair(v[c][6 + 2 * j], v[c][7 + 2 * j]), pair(v[c][4 + 2 * j], v[c][5 + 2 * j]))
+        to_after.append(beta[c][7])
+        to_before.append(beta[c][6])
     send_edge(6, pair(*to_after[:2]), pair(*to_before[:2]))
     send_edge(7, to_after[2], to_before[2])
     for z in range(4):
@@ -314,10 +321,14 @@
         rel = (chip >> 3) - (me >> 4)
         holder = jnp.where(rel == 0, odd, jnp.where(rel < 0, 0, 1))
         beside = (chip ^ here) & 1
-        x = ((chip + beside * (1 - 2 * holder)) ^ here) & 7
-        slot = (rel + 1) * 16 + 2 * beside + 4 * (((x >> 1) ^ (x >> 2)) & 1) + 8 * (x >> 2)
-        flip = holder ^ beside
-        blocks = (slot + flip, slot + 1 - flip)
+        x0, x1 = (((chip + sign * beside) ^ here) & 7 for sign in (1, -1))
+        six0, six1 = x0 >> 2, x1 >> 2
+        two0, two1 = ((x0 >> 1) & 1) ^ six0, ((x1 >> 1) & 1) ^ six1
+        slot = (rel + 1) * 16 + beside
+        block0 = slot + 2 * two0 + 4 * six0 + 8 * holder
+        block1 = slot + 2 * six1 + 4 * two1 + 8 * (1 - holder)
+        straight = beside == 0
+        blocks = (jnp.where(straight, block0, block1), jnp.where(straight, block1, block0))
         for half in range(2):
             first, second = (all_s[block, 8 * half : 8 * half + 8, :] for block in blocks)
             w_s[2 * half, 8 * w : 8 * w + 8, :] = jnp.where(low_rows, first, pltpu.roll(second, 4, 0))
@@ -440,7 +451,7 @@
     across = jnp.where(is_odd, here == 7, here == 0)
 
     def edge_slabs(k, left):
-        mine = msg_in_ref[24 + 8 * k : 32 + 8 * k, :]
+        mine = msg_in_ref[136 + 8 * k : 144 + 8 * k, :]
         other = jnp.where(across, far_ref[272 + 8 * k : 280 + 8 * k, :], row_ref[272 + 8 * k : 280 + 8 * k, :])
         p = jnp.where(is_odd == left, mine, other)
         first = jnp.where(odd_lane, pltpu.roll(p, 1, 1), p)
@@ -452,27 +463,30 @@
         slabs = [edge_slabs(k, left) for k in range(8)]
         edges[left] = [slabs[2 * c] + slabs[2 * c + 1] for c in range(3)], [slabs[6][0], slabs[6][1], slabs[7][0]]
 
+    layers_v, layers_b, layers_e = [], [], []
     for c in range(3):
-        v = jnp.concatenate(
-            edges[True][0][c] + [v1_ref[c][2:12]] + edges[False][0][c],
-            axis=0,
-        )
-        beta = jnp.concatenate([zero, edges[True][1][c], beta1_ref[c], edges[False][1][c], zero], axis=0)
+        layers_v.append(jnp.concatenate(edges[True][0][c] + [v1_ref[c][2:12]] + edges[False][0][c], axis=0))
+        layers_b.append(jnp.concatenate([zero, edges[True][1][c], beta1_ref[c], edges[False][1][c], zero], axis=0))
         slabs = []
         for j in range(10):
             row = e2_s[c, pl.ds(5 + 4 * odd + j, 1), :]
             slab = jnp.take_along_axis(jnp.broadcast_to(row, (8, 128)), spread, axis=1)[None]
             slabs += [slab, slab]
-        e = jnp.concatenate(slabs[1:19], axis=0)
-        m = sol * (kappa[c] / 26.5)
-        v = v + (root1 * sol) * e
-        d = INV_MID * (beta - m * stencil1(v))
-        v = v + d
-        d = A1 * d + C1 * (beta - m * stencil1(v))
-        v = v + d
-        d = A2 * d + C2 * (beta - m * stencil1(v))
-        v = v + d
-        e = jnp.where(sol > 0.0, v / root1, e)[3:15]
+        layers_e.append(jnp.concatenate(slabs[1:19], axis=0))
+    m = [sol * (kappa[c] / 26.5) for c in (0, 2)]
+    m = [m[0], m[0], m[1]]
+    g = root1 * sol
+    v = [layers_v[c] + g * layers_e[c] for c in range(3)]
+    d = [None] * 3
+    for a, b in ((None, INV_MID), (A1, C1), (A2, C2)):
+        t = [stencil1(v[c]) for c in range(3)]
+        for c in range(3):
+            pre = b * (layers_b[c] - m[c] * t[c])
+            d[c] = pre if a is None else a * d[c] + pre
+            v[c] = v[c] + d[c]
+    inverse1 = 1.0 / root1
+    for c in range(3):
+        e = jnp.where(sol > 0.0, v[c] * inverse1, layers_e[c])[3:15]
         pe_s[c, :, pl.ds(0, 8, 2), :] = e
         pe_s[c, :, pl.ds(1, 8, 2), :] = e
 
@@ -543,6 +557,11 @@
 def swap_bits(values, bits):
     n = lax.axis_size("bricks")
     return lax.ppermute(values, "bricks", [(i, i ^ bits) for i in range(n)])
+
+
+def swap_chips(values, bits):
+    n = lax.axis_size("bricks")
+    return lax.ppermute(values, "bricks", [(i, i ^ bits[i % 2]) for i in range(n)])
 
 
 def swap_before(values):
@@ -614,18 +633,19 @@
     def joined(a, b, bit):
         return jnp.where((row_of & bit) == 0, a, b)
 
-    msg_in = swap_bits(msg, 1)
-    blocks = jnp.concatenate([msg[:16], msg_in[:16]], axis=0)
-    solids = joined(msg[16:24], msg_in[16:24], 1)
+    blocks, solids = msg[:16], msg[16:24]
     got = swap_ring(jnp.concatenate([blocks, solids, edge], axis=0))
+    blocks = jnp.concatenate([blocks, got[:16]], axis=0)
+    solids = joined(solids, got[16:24], 1)
+    edge_in = got[24:]
+    got = swap_chips(jnp.concatenate([blocks, solids], axis=0), (4, 12))
     blocks = jnp.concatenate([blocks, got[:32]], axis=0)
-    solids = joined(solids, got[32:40], 2)
-    edge_in = got[40:]
-    got = swap_bits(jnp.concatenate([blocks, solids], axis=0), 4)
+    solids = joined(solids, got[32:], 2)
+    got = swap_chips(jnp.concatenate([blocks, solids], axis=0), (12, 4))
     blocks = jnp.concatenate([blocks, got[:64]], axis=0)
     solids = joined(solids, got[64:], 4)
-    got = swap_bits(jnp.concatenate([blocks, solids], axis=0), 12)
-    row = jnp.concatenate([blocks, got[:128], solids, got[128:], edge_in], axis=0)
+    msg_in = swap_bits(jnp.concatenate([blocks, solids, msg[24:]], axis=0), 1)
+    row = jnp.concatenate([blocks, msg_in[:128], solids, msg_in[128:136], edge_in], axis=0)
     far = next_rows(row)
     far2 = swap_bits(far, 1)
     return pl.pallas_call(

time: 54.7 us -> 54 us (0.987)
    ppermute x5 -> x3, waiting for transfers between devices: 13.8 us -> 2.7 us  [swap_bits(): return lax.ppermute(values, 'bricks', [(i, i ^ bits) for i in range(n)])]
    ppermute x0 -> x2, waiting for transfers between devices: none -> 10.7 us  [swap_chips(): lax.ppermute(values, 'bricks', [(i, i ^ bits[i % 2]) for i in range(n)])]
where the time goes in v5:
time: 54 us; the launch traced here: 53.6 us
  waiting for transfers between devices  26.3 us (49%)
  starting transfers between devices  14 us (26%)
  Pallas kernels  11.9 us (22%)
  local copies, waits for them, and re-layouts  0.94 us (2%)
    ppermute x2, waiting for transfers between devices, swap_chips(): lax.ppermute(values, 'bricks', [(i, i ^ bits[i % 2]) for i in range(n)])  10.7 us
    ppermute x1, starting transfers between devices, swap_before(): lax.ppermute(values, 'bricks', [(i, i + 1 if i % 2 else i - 1) for i in r...  10.2 us
    ppermute x1, waiting for transfers between devices, next_rows(): lax.ppermute(values, 'bricks', [(i, j) for i, j in pairs if 0 <= j < n])  7.48 us
    pallas_call x1, Pallas kernels, body(): pl.pallas_call(up_kernel, out_shape=shaped(3, 16, 16, 128), in_specs=[VME...  6.78 us
    ppermute x1, waiting for transfers between devices, swap_ring(): return lax.ppermute(values, 'bricks', sorted(pairs))  3.22 us
    ppermute x3, waiting for transfers between devices, swap_bits(): return lax.ppermute(values, 'bricks', [(i, i ^ bits) for i in range(n)])  2.7 us
    ppermute x1, waiting for transfers between devices, swap_before(): lax.ppermute(values, 'bricks', [(i, i + 1 if i % 2 else i - 1) for i in r...  2.21 us
    pallas_call x1, Pallas kernels, body(): pl.pallas_call(pack_kernel, out_shape=(shaped(38, 16, 128), shaped(38, 16...  2.1 us
  transfers between devices with their start and end apart: 8, of which 7 were waited for; matrix products, arithmetic and copies ran while one was open for 0% of the time, Pallas kernels for 3%

profile of v5, /device:TPU:24, one launch (start us, length us, event | category | flops | bytes accessed | tf_op | source)
XLA Modules:
  0.0 53.6 jit_solution(5497340858291521408)
XLA Ops:
  0.0 0.0 copy-start
  0.0 2.1 %pack.1 = (f32[38,16,128]{2,1,0:T(8,128)}, f32[38,16,128]{2,1,0:T(8,128)}, f32[17,16,128]{2,1,0:T(8,128)}) custom-call(f32[3,16,16,128]{3,2,1,0:T(8,128)} %load_ref.3, s32[16,16,128]{2,1,0:T(8,128)} %class_ref.1, s32[1,1,8]{2,1,0:T(1,128)} %occ_ref.1, f32[8]{0:T(128)} %moduli_ref.1), custom_call_target="tpu_custom_call" | custom-call | tf_op jit(solution)/shard_map/pack/pallas_call | solution.py:588
  2.1 0.1 collective-permute-start
  2.2 10.2 %collective-permute-start.1 = (f32[38,16,128]{2,1,0:T(8,128)}, f32[38,16,128]{2,1,0:T(8,128)S(1)}, u32[]{:S(2)}, u32[]{:S(2)}) collective-permute-start(f32[38,16,128]{2,1,0:T(8,128)} %get-tuple-element.27), channel_id=1, source_target_pairs={{1,2},{2,1},{3,4},{4,3},{5,6},{6,5},{7,8},{8,7},{9,10},{10,9},{11,... | collective-permute-start | bytes 933896 | tf_op jit(solution)/shard_map/ppermute | solution.py:569
  12.5 0.0 collective-permute-done.x_ref.x_solid_ref
  12.5 0.0 copy-done
  12.5 0.0 copy-start.1
  12.5 0.9 %copy-done.1 = f32[17,16,128]{2,1,0:T(8,128)S(1)} copy-done((f32[17,16,128]{2,1,0:T(8,128)S(1)}, f32[17,16,128]{2,1,0:T(8,128)}, u32[]{:S(2)}) %copy-start.1) | copy-done | bytes 139288
  13.4 1.6 %inner.1 = (f32[3,36,16,128]{3,2,1,0:T(8,128)S(1)}, f32[3,36,16,128]{3,2,1,0:T(8,128)S(1)}, f32[36,16,128]{2,1,0:T(8,128)S(1)}, f32[3,36,16,128]{3,2,1,0:T(8,128...) custom-call(f32[3,16,16,128]{3,2,1,0:T(8,128)S(1)} %copy-done, ...), custom_call_target="tpu_custom_call" | custom-call | flops 10000000 | bytes 4000000 | tf_op jit(solution)/shard_map/inner/pallas_call | solution.py:606
  15.0 2.2 %collective-permute-done.1.o_ref = f32[38,16,128]{2,1,0:T(8,128)S(1)} collective-permute-done((f32[38,16,128]{2,1,0:T(8,128)}, f32[38,16,128]{2,1,0:T(8,128)S(1)}, u32[]{:S(2)}, u32[]{:S(2)}) %collective-permute-start.1) | collective-permute-done | bytes 311328 | tf_op jit(solution)/shard_map/ppermute | solution.py:569
  17.2 1.4 %down.1 = (f32[3,36,16,128]{3,2,1,0:T(8,128)S(1)}, f32[3,36,16,128]{3,2,1,0:T(8,128)S(1)}, f32[36,16,128]{2,1,0:T(8,128)S(1)}, f32[3,36,16,128]{3,2,1,0:T(8,128)...) custom-call(f32[17,16,128]{2,1,0:T(8,128)S(1)} %copy-done.1, ...), custom_call_target="tpu_custom_call", output_to_operand_aliasing={{0}: (3, {}), {1}: (4, {}), {2}: (5, {}), {3}: (6, {}), {4}... | custom-call | tf_op jit(solution)/shard_map/down/pallas_call | solution.py:615
  18.6 1.6 %collective-permute-start.2 = (f32[88,128]{1,0:T(8,128)S(1)}, f32[88,128]{1,0:T(8,128)S(1)}, u32[]{:S(2)}, u32[]{:S(2)}) collective-permute-start(f32[88,128]{1,0:T(8,128)S(1)} %pad_maximum_fusion), channel_id=1, source_target_pairs={{0,15},{1,2},{2,1},{3,4},{4,3},{5,6},{6,5},{7,8},{8,7},{9,10},{10,... | collective-permute-start | bytes 135176 | tf_op jit(solution)/shard_map/ppermute | solution.py:578
  20.2 3.2 %collective-permute-done.2 = f32[88,128]{1,0:T(8,128)S(1)} collective-permute-done((f32[88,128]{1,0:T(8,128)S(1)}, f32[88,128]{1,0:T(8,128)S(1)}, u32[]{:S(2)}, u32[]{:S(2)}) %collective-permute-start.2) | collective-permute-done | bytes 45088 | tf_op jit(solution)/shard_map/ppermute | solution.py:578
  23.4 0.1 slice_select_fusion.2
  23.5 0.1 collective-permute-start.3
  23.6 4.7 %collective-permute-done.3 = f32[40,128]{1,0:T(8,128)S(1)} collective-permute-done((f32[40,128]{1,0:T(8,128)S(1)}, f32[40,128]{1,0:T(8,128)S(1)}, u32[]{:S(2)}, u32[]{:S(2)}) %collective-permute-start.3) | collective-permute-done | bytes 20512 | tf_op jit(solution)/shard_map/ppermute | solution.py:564
  28.2 0.1 slice_select_fusion.1
  28.3 0.1 collective-permute-start.4
  28.4 6.0 %collective-permute-done.4 = f32[72,128]{1,0:T(8,128)S(1)} collective-permute-done((f32[72,128]{1,0:T(8,128)S(1)}, f32[72,128]{1,0:T(8,128)S(1)}, u32[]{:S(2)}, u32[]{:S(2)}) %collective-permute-start.4) | collective-permute-done | bytes 36896 | tf_op jit(solution)/shard_map/ppermute | solution.py:564
  34.5 0.1 constant_dynamic-update-slice_fusion
  34.5 0.0 collective-permute-start.5
  34.6 1.3 %collective-permute-done.5.msg_in_ref = f32[200,128]{1,0:T(8,128)S(1)} collective-permute-done((f32[200,128]{1,0:T(8,128)S(1)}, f32[200,128]{1,0:T(8,128)S(1)}, u32[]{:S(2)}, u32[]{:S(2)}) %collective-permute-start.5) | collective-permute-done | bytes 102432 | tf_op jit(solution)/shard_map/ppermute | solution.py:559
  35.9 0.1 constant_dynamic-update-slice_fusion.5
  36.0 1.9 %collective-permute-start.6 = (f32[336,128]{1,0:T(8,128)S(1)}, f32[336,128]{1,0:T(8,128)S(1)}, u32[]{:S(2)}, u32[]{:S(2)}) collective-permute-start(f32[336,128]{1,0:T(8,128)S(1)} %slice_dynamic-update-slice_fusion.1.row_ref), channel_id=1, source_target_pairs={{0,16},{2,18},{4,20},{6,22},{8,24},{10,26},{12,28},{14,30},{16,32}... | collective-permute-start | bytes 516104 | tf_op jit(solution)/shard_map/ppermute | solution.py:584
  37.9 7.5 %collective-permute-done.6.far_ref = f32[336,128]{1,0:T(8,128)S(1)} collective-permute-done((f32[336,128]{1,0:T(8,128)S(1)}, f32[336,128]{1,0:T(8,128)S(1)}, u32[]{:S(2)}, u32[]{:S(2)}) %collective-permute-start.6) | collective-permute-done | bytes 172064 | tf_op jit(solution)/shard_map/ppermute | solution.py:584
  45.4 0.0 collective-permute-start.7
  45.4 1.4 %collective-permute-done.7.far2_ref = f32[336,128]{1,0:T(8,128)S(1)} collective-permute-done((f32[336,128]{1,0:T(8,128)S(1)}, f32[336,128]{1,0:T(8,128)S(1)}, u32[]{:S(2)}, u32[]{:S(2)}) %collective-permute-start.7) | collective-permute-done | bytes 172064 | tf_op jit(solution)/shard_map/ppermute | solution.py:559
  46.8 6.8 %up.1 = f32[3,16,16,128]{3,2,1,0:T(8,128)} custom-call(f32[336,128]{1,0:T(8,128)S(1)} %slice_dynamic-update-slice_fusion.1.row_ref, f32[336,128]{1,0:T(8,128)S(1)} %collective-permute-done.6.far_ref, f32[336,128]{1,0:T(8,128)S(1)} %collective-permute-done.7.far2_ref, f32[200,128]{1,0:T(8,128)S(1)} %collective-permute-done.5.msg_in_ref, ...), custom_call_target="tpu_custom_call" | custom-call | tf_op jit(solution)/shard_map/up/pallas_call | solution.py:651
  (15 shorter events, 0.1 us)
Async XLA Ops:
  0.0 12.5 %copy-start = (f32[3,16,16,128]{3,2,1,0:T(8,128)S(1)}, f32[3,16,16,128]{3,2,1,0:T(8,128)}, u32[]{:S(2)}) copy-start(f32[3,16,16,128]{3,2,1,0:T(8,128)} %load_ref.3) | copy-start | bytes 1179652
  2.1 10.4 %collective-permute-start = (f32[38,16,128]{2,1,0:T(8,128)}, f32[38,16,128]{2,1,0:T(8,128)S(1)}, u32[]{:S(2)}, u32[]{:S(2)}) collective-permute-start(f32[38,16,128]{2,1,0:T(8,128)} %get-tuple-element.26), channel_id=1, source_target_pairs={{0,1},{1,0},{2,3},{3,2},{4,5},{5,4},{6,7},{7,6},{8,9},{9,8},{10,11... | collective-permute-start | bytes 933896 | tf_op jit(solution)/shard_map/ppermute | solution.py:559
  2.2 15.0 %collective-permute-start.1 = (f32[38,16,128]{2,1,0:T(8,128)}, f32[38,16,128]{2,1,0:T(8,128)S(1)}, u32[]{:S(2)}, u32[]{:S(2)}) collective-permute-start(f32[38,16,128]{2,1,0:T(8,128)} %get-tuple-element.27), channel_id=1, source_target_pairs={{1,2},{2,1},{3,4},{4,3},{5,6},{6,5},{7,8},{8,7},{9,10},{10,9},{11,... | collective-permute-start | bytes 933896 | tf_op jit(solution)/shard_map/ppermute | solution.py:569
  12.5 0.9 %copy-start.1 = (f32[17,16,128]{2,1,0:T(8,128)S(1)}, f32[17,16,128]{2,1,0:T(8,128)}, u32[]{:S(2)}) copy-start(f32[17,16,128]{2,1,0:T(8,128)} %get-tuple-element.25.own_ref) | copy-start | bytes 417796
  18.6 4.8 %collective-permute-start.2 = (f32[88,128]{1,0:T(8,128)S(1)}, f32[88,128]{1,0:T(8,128)S(1)}, u32[]{:S(2)}, u32[]{:S(2)}) collective-permute-start(f32[88,128]{1,0:T(8,128)S(1)} %pad_maximum_fusion), channel_id=1, source_target_pairs={{0,15},{1,2},{2,1},{3,4},{4,3},{5,6},{6,5},{7,8},{8,7},{9,10},{10,... | collective-permute-start | bytes 135176 | tf_op jit(solution)/shard_map/ppermute | solution.py:578
  23.5 4.7 %collective-permute-start.3 = (f32[40,128]{1,0:T(8,128)S(1)}, f32[40,128]{1,0:T(8,128)S(1)}, u32[]{:S(2)}, u32[]{:S(2)}) collective-permute-start(f32[40,128]{1,0:T(8,128)S(1)} %pad_maximum_fusion.2), channel_id=1, source_target_pairs={{0,4},{1,13},{2,6},{3,15},{4,0},{5,9},{6,2},{7,11},{8,12},{9,5},{1... | collective-permute-start | bytes 61448 | tf_op jit(solution)/shard_map/ppermute | solution.py:564
  28.3 6.2 %collective-permute-start.4 = (f32[72,128]{1,0:T(8,128)S(1)}, f32[72,128]{1,0:T(8,128)S(1)}, u32[]{:S(2)}, u32[]{:S(2)}) collective-permute-start(f32[72,128]{1,0:T(8,128)S(1)} %pad_maximum_fusion.1), channel_id=1, source_target_pairs={{0,12},{1,5},{2,14},{3,7},{4,8},{5,1},{6,10},{7,3},{8,4},{9,13},{1... | collective-permute-start | bytes 110600 | tf_op jit(solution)/shard_map/ppermute | solution.py:564
  34.5 1.3 %collective-permute-start.5 = (f32[200,128]{1,0:T(8,128)S(1)}, f32[200,128]{1,0:T(8,128)S(1)}, u32[]{:S(2)}, u32[]{:S(2)}) collective-permute-start(f32[200,128]{1,0:T(8,128)S(1)} %slice_dynamic-update-slice_fusion.2), channel_id=1, source_target_pairs={{0,1},{1,0},{2,3},{3,2},{4,5},{5,4},{6,7},{7,6},{8,9},{9,8},{10,11... | collective-permute-start | bytes 307208 | tf_op jit(solution)/shard_map/ppermute | solution.py:559
  36.0 9.4 %collective-permute-start.6 = (f32[336,128]{1,0:T(8,128)S(1)}, f32[336,128]{1,0:T(8,128)S(1)}, u32[]{:S(2)}, u32[]{:S(2)}) collective-permute-start(f32[336,128]{1,0:T(8,128)S(1)} %slice_dynamic-update-slice_fusion.1.row_ref), channel_id=1, source_target_pairs={{0,16},{2,18},{4,20},{6,22},{8,24},{10,26},{12,28},{14,30},{16,32}... | collective-permute-start | bytes 516104 | tf_op jit(solution)/shard_map/ppermute | solution.py:584
  45.4 1.4 %collective-permute-start.7 = (f32[336,128]{1,0:T(8,128)S(1)}, f32[336,128]{1,0:T(8,128)S(1)}, u32[]{:S(2)}, u32[]{:S(2)}) collective-permute-start(f32[336,128]{1,0:T(8,128)S(1)} %collective-permute-done.6.far_ref), channel_id=1, source_target_pairs={{0,1},{1,0},{2,3},{3,2},{4,5},{5,4},{6,7},{7,6},{8,9},{9,8},{10,11... | collective-permute-start | bytes 516104 | tf_op jit(solution)/shard_map/ppermute | solution.py:559

commit v6 on v5

--- a/solution.py
+++ b/solution.py
@@ -321,12 +321,12 @@
         rel = (chip >> 3) - (me >> 4)
         holder = jnp.where(rel == 0, odd, jnp.where(rel < 0, 0, 1))
         beside = (chip ^ here) & 1
-        x0, x1 = (((chip + sign * beside) ^ here) & 7 for sign in (1, -1))
+        x0, x1 = ((chip ^ (here - sign * beside)) & 7 for sign in (1, -1))
         six0, six1 = x0 >> 2, x1 >> 2
         two0, two1 = ((x0 >> 1) & 1) ^ six0, ((x1 >> 1) & 1) ^ six1
-        slot = (rel + 1) * 16 + beside
-        block0 = slot + 2 * two0 + 4 * six0 + 8 * holder
-        block1 = slot + 2 * six1 + 4 * two1 + 8 * (1 - holder)
+        slot = (rel + 1) * 16 + 4 * beside
+        block0 = slot + two0 + 2 * six0 + 8 * holder
+        block1 = slot + two1 + 2 * six1 + 8 * (1 - holder)
         straight = beside == 0
         blocks = (jnp.where(straight, block0, block1), jnp.where(straight, block1, block0))
         for half in range(2):
@@ -557,11 +557,6 @@
 def swap_bits(values, bits):
     n = lax.axis_size("bricks")
     return lax.ppermute(values, "bricks", [(i, i ^ bits) for i in range(n)])
-
-
-def swap_chips(values, bits):
-    n = lax.axis_size("bricks")
-    return lax.ppermute(values, "bricks", [(i, i ^ bits[i % 2]) for i in range(n)])
 
 
 def swap_before(values):
@@ -633,17 +628,16 @@
     def joined(a, b, bit):
         return jnp.where((row_of & bit) == 0, a, b)
 
-    blocks, solids = msg[:16], msg[16:24]
+    mine = msg[:24]
+    parts = [mine] + [swap_bits(mine, bits) for bits in (4, 12, 8)]
+    blocks = jnp.concatenate([part[:16] for part in parts], axis=0)
+    solids = parts[0][16:]
+    for k in (1, 2, 3):
+        solids = jnp.where((row_of & 3) == k, parts[k][16:], solids)
     got = swap_ring(jnp.concatenate([blocks, solids, edge], axis=0))
-    blocks = jnp.concatenate([blocks, got[:16]], axis=0)
-    solids = joined(solids, got[16:24], 1)
-    edge_in = got[24:]
-    got = swap_chips(jnp.concatenate([blocks, solids], axis=0), (4, 12))
-    blocks = jnp.concatenate([blocks, got[:32]], axis=0)
-    solids = joined(solids, got[32:], 2)
-    got = swap_chips(jnp.concatenate([blocks, solids], axis=0), (12, 4))
     blocks = jnp.concatenate([blocks, got[:64]], axis=0)
-    solids = joined(solids, got[64:], 4)
+    solids = joined(solids, got[64:72], 4)
+    edge_in = got[72:]
     msg_in = swap_bits(jnp.concatenate([blocks, solids, msg[24:]], axis=0), 1)
     row = jnp.concatenate([blocks, msg_in[:128], solids, msg_in[128:136], edge_in], axis=0)
     far = next_rows(row)

time: 54 us -> 53.4 us (0.989)
  waiting for transfers between devices: 26.3 us -> 19.3 us
  starting transfers between devices: 14 us -> 20.4 us
    ppermute x2 -> x0, waiting for transfers between devices: 10.7 us -> none  [swap_chips(): lax.ppermute(values, 'bricks', [(i, i ^ bits[i % 2]) for i in range(n)])]
    ppermute x3 -> x6, starting transfers between devices: 0.13 us -> 6.7 us  [swap_bits(): return lax.ppermute(values, 'bricks', [(i, i ^ bits) for i in range(n)])]
    ppermute x3 -> x6, waiting for transfers between devices: 2.7 us -> 6.16 us  [swap_bits(): return lax.ppermute(values, 'bricks', [(i, i ^ bits) for i in range(n)])]
    ppermute x1, waiting for transfers between devices: 3.22 us -> 4.92 us  [swap_ring(): return lax.ppermute(values, 'bricks', sorted(pairs))]
    ppermute x1, starting transfers between devices: 1.91 us -> 3.39 us  [next_rows(): lax.ppermute(values, 'bricks', [(i, j) for i, j in pairs if 0 <= j < n])]
    ppermute x1, waiting for transfers between devices: 7.48 us -> 6 us  [next_rows(): lax.ppermute(values, 'bricks', [(i, j) for i, j in pairs if 0 <= j < n])]
    ppermute x1, starting transfers between devices: 1.55 us -> 0.08 us  [swap_ring(): return lax.ppermute(values, 'bricks', sorted(pairs))]
  transfers between devices with their start and end apart: 8 -> 9, of which waited for: 7 -> 6; matrix products, arithmetic and copies ran while one was open for 0% -> 0% of each run, Pallas kernels for 3% -> 3%
where the time goes in v6:
time: 53.4 us; the launch traced here: 52.9 us
  starting transfers between devices  20.4 us (38%)
  waiting for transfers between devices  19.3 us (36%)
  Pallas kernels  11.9 us (22%)
  local copies, waits for them, and re-layouts  0.95 us (2%)
    ppermute x1, starting transfers between devices, swap_before(): lax.ppermute(values, 'bricks', [(i, i + 1 if i % 2 else i - 1) for i in r...  10.2 us
    pallas_call x1, Pallas kernels, body(): pl.pallas_call(up_kernel, out_shape=shaped(3, 16, 16, 128), in_specs=[VME...  6.79 us
    ppermute x6, starting transfers between devices, swap_bits(): return lax.ppermute(values, 'bricks', [(i, i ^ bits) for i in range(n)])  6.7 us
    ppermute x6, waiting for transfers between devices, swap_bits(): return lax.ppermute(values, 'bricks', [(i, i ^ bits) for i in range(n)])  6.16 us
    ppermute x1, waiting for transfers between devices, next_rows(): lax.ppermute(values, 'bricks', [(i, j) for i, j in pairs if 0 <= j < n])  6 us
    ppermute x1, waiting for transfers between devices, swap_ring(): return lax.ppermute(values, 'bricks', sorted(pairs))  4.92 us
    ppermute x1, starting transfers between devices, next_rows(): lax.ppermute(values, 'bricks', [(i, j) for i, j in pairs if 0 <= j < n])  3.39 us
    ppermute x1, waiting for transfers between devices, swap_before(): lax.ppermute(values, 'bricks', [(i, i + 1 if i % 2 else i - 1) for i in r...  2.2 us
  transfers between devices with their start and end apart: 9, of which 6 were waited for; matrix products, arithmetic and copies ran while one was open for 0% of the time, Pallas kernels for 3%

profile of v6, /device:TPU:24, one launch (start us, length us, event | category | flops | bytes accessed | tf_op | source)
XLA Modules:
  0.0 52.9 jit_solution(8524423668569346220)
XLA Ops:
  0.0 0.0 copy-start
  0.0 2.1 %pack.1 = (f32[38,16,128]{2,1,0:T(8,128)}, f32[38,16,128]{2,1,0:T(8,128)}, f32[17,16,128]{2,1,0:T(8,128)}) custom-call(f32[3,16,16,128]{3,2,1,0:T(8,128)} %load_ref.3, s32[16,16,128]{2,1,0:T(8,128)} %class_ref.1, s32[1,1,8]{2,1,0:T(1,128)} %occ_ref.1, f32[8]{0:T(128)} %moduli_ref.1), custom_call_target="tpu_custom_call" | custom-call | tf_op jit(solution)/shard_map/pack/pallas_call | solution.py:583
  2.1 0.1 collective-permute-start
  2.2 10.2 %collective-permute-start.1 = (f32[38,16,128]{2,1,0:T(8,128)}, f32[38,16,128]{2,1,0:T(8,128)S(1)}, u32[]{:S(2)}, u32[]{:S(2)}) collective-permute-start(f32[38,16,128]{2,1,0:T(8,128)} %get-tuple-element.27), channel_id=1, source_target_pairs={{1,2},{2,1},{3,4},{4,3},{5,6},{6,5},{7,8},{8,7},{9,10},{10,9},{11,... | collective-permute-start | bytes 933896 | tf_op jit(solution)/shard_map/ppermute | solution.py:564
  12.5 0.0 collective-permute-done.x_ref.x_solid_ref
  12.5 0.0 copy-done
  12.5 0.0 copy-start.1
  12.5 0.9 %copy-done.1 = f32[17,16,128]{2,1,0:T(8,128)S(1)} copy-done((f32[17,16,128]{2,1,0:T(8,128)S(1)}, f32[17,16,128]{2,1,0:T(8,128)}, u32[]{:S(2)}) %copy-start.1) | copy-done | bytes 139288
  13.4 1.6 %inner.1 = (f32[3,36,16,128]{3,2,1,0:T(8,128)S(1)}, f32[3,36,16,128]{3,2,1,0:T(8,128)S(1)}, f32[36,16,128]{2,1,0:T(8,128)S(1)}, f32[3,36,16,128]{3,2,1,0:T(8,128...) custom-call(f32[3,16,16,128]{3,2,1,0:T(8,128)S(1)} %copy-done, ...), custom_call_target="tpu_custom_call" | custom-call | flops 10000000 | bytes 4000000 | tf_op jit(solution)/shard_map/inner/pallas_call | solution.py:601
  15.0 2.2 %collective-permute-done.1.o_ref = f32[38,16,128]{2,1,0:T(8,128)S(1)} collective-permute-done((f32[38,16,128]{2,1,0:T(8,128)}, f32[38,16,128]{2,1,0:T(8,128)S(1)}, u32[]{:S(2)}, u32[]{:S(2)}) %collective-permute-start.1) | collective-permute-done | bytes 311328 | tf_op jit(solution)/shard_map/ppermute | solution.py:564
  17.2 1.4 %down.1 = (f32[3,36,16,128]{3,2,1,0:T(8,128)S(1)}, f32[3,36,16,128]{3,2,1,0:T(8,128)S(1)}, f32[36,16,128]{2,1,0:T(8,128)S(1)}, f32[3,36,16,128]{3,2,1,0:T(8,128)...) custom-call(f32[17,16,128]{2,1,0:T(8,128)S(1)} %copy-done.1, ...), custom_call_target="tpu_custom_call", output_to_operand_aliasing={{0}: (3, {}), {1}: (4, {}), {2}: (5, {}), {3}: (6, {}), {4}... | custom-call | tf_op jit(solution)/shard_map/down/pallas_call | solution.py:610
  18.6 0.1 collective-permute-start.2
  18.7 2.4 %collective-permute-start.3 = (f32[24,128]{1,0:T(8,128)S(1)}, f32[24,128]{1,0:T(8,128)S(1)}, u32[]{:S(2)}, u32[]{:S(2)}) collective-permute-start(f32[24,128]{1,0:T(8,128)S(1)} %slice.48), channel_id=1, source_target_pairs={{0,12},{1,13},{2,14},{3,15},{4,8},{5,9},{6,10},{7,11},{8,4},{9,5},... | collective-permute-start | bytes 36872 | tf_op jit(solution)/shard_map/ppermute | solution.py:559
  21.1 4.1 %collective-permute-start.4 = (f32[24,128]{1,0:T(8,128)S(1)}, f32[24,128]{1,0:T(8,128)S(1)}, u32[]{:S(2)}, u32[]{:S(2)}) collective-permute-start(f32[24,128]{1,0:T(8,128)S(1)} %slice.48), channel_id=1, source_target_pairs={{0,8},{1,9},{2,10},{3,11},{4,12},{5,13},{6,14},{7,15},{8,0},{9,1},... | collective-permute-start | bytes 36872 | tf_op jit(solution)/shard_map/ppermute | solution.py:559
  25.2 0.0 collective-permute-done.2
  25.2 0.0 collective-permute-done.3
  25.2 3.5 %collective-permute-done.4 = f32[24,128]{1,0:T(8,128)S(1)} collective-permute-done((f32[24,128]{1,0:T(8,128)S(1)}, f32[24,128]{1,0:T(8,128)S(1)}, u32[]{:S(2)}, u32[]{:S(2)}) %collective-permute-start.4) | collective-permute-done | bytes 12320 | tf_op jit(solution)/shard_map/ppermute | solution.py:559
  28.7 0.1 constant_dynamic-update-slice_fusion.1
  28.8 0.1 collective-permute-start.5
  28.9 4.9 %collective-permute-done.5 = f32[136,128]{1,0:T(8,128)S(1)} collective-permute-done((f32[136,128]{1,0:T(8,128)S(1)}, f32[136,128]{1,0:T(8,128)S(1)}, u32[]{:S(2)}, u32[]{:S(2)}) %collective-permute-start.5) | collective-permute-done | bytes 69664 | tf_op jit(solution)/shard_map/ppermute | solution.py:573
  33.8 0.1 constant_dynamic-update-slice_fusion.7
  33.9 0.0 collective-permute-start.6
  33.9 1.3 %collective-permute-done.6.msg_in_ref = f32[200,128]{1,0:T(8,128)S(1)} collective-permute-done((f32[200,128]{1,0:T(8,128)S(1)}, f32[200,128]{1,0:T(8,128)S(1)}, u32[]{:S(2)}, u32[]{:S(2)}) %collective-permute-start.6) | collective-permute-done | bytes 102432 | tf_op jit(solution)/shard_map/ppermute | solution.py:559
  35.2 0.1 constant_dynamic-update-slice_fusion.15
  35.3 3.4 %collective-permute-start.7 = (f32[336,128]{1,0:T(8,128)S(1)}, f32[336,128]{1,0:T(8,128)S(1)}, u32[]{:S(2)}, u32[]{:S(2)}) collective-permute-start(f32[336,128]{1,0:T(8,128)S(1)} %constant_dynamic-update-slice_fusion.13.row_ref), channel_id=1, source_target_pairs={{0,16},{2,18},{4,20},{6,22},{8,24},{10,26},{12,28},{14,30},{16,32}... | collective-permute-start | bytes 516104 | tf_op jit(solution)/shard_map/ppermute | solution.py:579
  38.7 6.0 %collective-permute-done.7.far_ref = f32[336,128]{1,0:T(8,128)S(1)} collective-permute-done((f32[336,128]{1,0:T(8,128)S(1)}, f32[336,128]{1,0:T(8,128)S(1)}, u32[]{:S(2)}, u32[]{:S(2)}) %collective-permute-start.7) | collective-permute-done | bytes 172064 | tf_op jit(solution)/shard_map/ppermute | solution.py:579
  44.7 0.0 collective-permute-start.8
  44.7 1.4 %collective-permute-done.8.far2_ref = f32[336,128]{1,0:T(8,128)S(1)} collective-permute-done((f32[336,128]{1,0:T(8,128)S(1)}, f32[336,128]{1,0:T(8,128)S(1)}, u32[]{:S(2)}, u32[]{:S(2)}) %collective-permute-start.8) | collective-permute-done | bytes 172064 | tf_op jit(solution)/shard_map/ppermute | solution.py:559
  46.1 6.8 %up.1 = f32[3,16,16,128]{3,2,1,0:T(8,128)} custom-call(f32[336,128]{1,0:T(8,128)S(1)} %constant_dynamic-update-slice_fusion.13.row_ref, f32[336,128]{1,0:T(8,128)S(1)} %collective-permute-done.7.far_ref, f32[336,128]{1,0:T(8,128)S(1)} %collective-permute-done.8.far2_ref, f32[200,128]{1,0:T(8,128)S(1)} %collective-permute-done.6.msg_in_ref, ...), custom_call_target="tpu_custom_call" | custom-call | tf_op jit(solution)/shard_map/up/pallas_call | solution.py:645
  (14 shorter events, 0.1 us)
Async XLA Ops:
  0.0 12.5 %copy-start = (f32[3,16,16,128]{3,2,1,0:T(8,128)S(1)}, f32[3,16,16,128]{3,2,1,0:T(8,128)}, u32[]{:S(2)}) copy-start(f32[3,16,16,128]{3,2,1,0:T(8,128)} %load_ref.3) | copy-start | bytes 1179652
  2.1 10.4 %collective-permute-start = (f32[38,16,128]{2,1,0:T(8,128)}, f32[38,16,128]{2,1,0:T(8,128)S(1)}, u32[]{:S(2)}, u32[]{:S(2)}) collective-permute-start(f32[38,16,128]{2,1,0:T(8,128)} %get-tuple-element.26), channel_id=1, source_target_pairs={{0,1},{1,0},{2,3},{3,2},{4,5},{5,4},{6,7},{7,6},{8,9},{9,8},{10,11... | collective-permute-start | bytes 933896 | tf_op jit(solution)/shard_map/ppermute | solution.py:559
  2.2 15.0 %collective-permute-start.1 = (f32[38,16,128]{2,1,0:T(8,128)}, f32[38,16,128]{2,1,0:T(8,128)S(1)}, u32[]{:S(2)}, u32[]{:S(2)}) collective-permute-start(f32[38,16,128]{2,1,0:T(8,128)} %get-tuple-element.27), channel_id=1, source_target_pairs={{1,2},{2,1},{3,4},{4,3},{5,6},{6,5},{7,8},{8,7},{9,10},{10,9},{11,... | collective-permute-start | bytes 933896 | tf_op jit(solution)/shard_map/ppermute | solution.py:564
  12.5 0.9 %copy-start.1 = (f32[17,16,128]{2,1,0:T(8,128)S(1)}, f32[17,16,128]{2,1,0:T(8,128)}, u32[]{:S(2)}) copy-start(f32[17,16,128]{2,1,0:T(8,128)} %get-tuple-element.25.own_ref) | copy-start | bytes 417796
  18.6 6.6 %collective-permute-start.2 = (f32[24,128]{1,0:T(8,128)S(1)}, f32[24,128]{1,0:T(8,128)S(1)}, u32[]{:S(2)}, u32[]{:S(2)}) collective-permute-start(f32[24,128]{1,0:T(8,128)S(1)} %slice.48), channel_id=1, source_target_pairs={{0,4},{1,5},{2,6},{3,7},{4,0},{5,1},{6,2},{7,3},{8,12},{9,13},{10,... | collective-permute-start | bytes 36872 | tf_op jit(solution)/shard_map/ppermute | solution.py:559
  18.7 6.5 %collective-permute-start.3 = (f32[24,128]{1,0:T(8,128)S(1)}, f32[24,128]{1,0:T(8,128)S(1)}, u32[]{:S(2)}, u32[]{:S(2)}) collective-permute-start(f32[24,128]{1,0:T(8,128)S(1)} %slice.48), channel_id=1, source_target_pairs={{0,12},{1,13},{2,14},{3,15},{4,8},{5,9},{6,10},{7,11},{8,4},{9,5},... | collective-permute-start | bytes 36872 | tf_op jit(solution)/shard_map/ppermute | solution.py:559
  21.1 7.6 %collective-permute-start.4 = (f32[24,128]{1,0:T(8,128)S(1)}, f32[24,128]{1,0:T(8,128)S(1)}, u32[]{:S(2)}, u32[]{:S(2)}) collective-permute-start(f32[24,128]{1,0:T(8,128)S(1)} %slice.48), channel_id=1, source_target_pairs={{0,8},{1,9},{2,10},{3,11},{4,12},{5,13},{6,14},{7,15},{8,0},{9,1},... | collective-permute-start | bytes 36872 | tf_op jit(solution)/shard_map/ppermute | solution.py:559
  28.8 5.0 %collective-permute-start.5 = (f32[136,128]{1,0:T(8,128)S(1)}, f32[136,128]{1,0:T(8,128)S(1)}, u32[]{:S(2)}, u32[]{:S(2)}) collective-permute-start(f32[136,128]{1,0:T(8,128)S(1)} %constant_dynamic-update-slice_fusion), channel_id=1, source_target_pairs={{0,15},{1,2},{2,1},{3,4},{4,3},{5,6},{6,5},{7,8},{8,7},{9,10},{10,... | collective-permute-start | bytes 208904 | tf_op jit(solution)/shard_map/ppermute | solution.py:573
  33.9 1.3 %collective-permute-start.6 = (f32[200,128]{1,0:T(8,128)S(1)}, f32[200,128]{1,0:T(8,128)S(1)}, u32[]{:S(2)}, u32[]{:S(2)}) collective-permute-start(f32[200,128]{1,0:T(8,128)S(1)} %constant_dynamic-update-slice_fusion.6), channel_id=1, source_target_pairs={{0,1},{1,0},{2,3},{3,2},{4,5},{5,4},{6,7},{7,6},{8,9},{9,8},{10,11... | collective-permute-start | bytes 307208 | tf_op jit(solution)/shard_map/ppermute | solution.py:559
  35.3 9.4 %collective-permute-start.7 = (f32[336,128]{1,0:T(8,128)S(1)}, f32[336,128]{1,0:T(8,128)S(1)}, u32[]{:S(2)}, u32[]{:S(2)}) collective-permute-start(f32[336,128]{1,0:T(8,128)S(1)} %constant_dynamic-update-slice_fusion.13.row_ref), channel_id=1, source_target_pairs={{0,16},{2,18},{4,20},{6,22},{8,24},{10,26},{12,28},{14,30},{16,32}... | collective-permute-start | bytes 516104 | tf_op jit(solution)/shard_map/ppermute | solution.py:579
  44.7 1.4 %collective-permute-start.8 = (f32[336,128]{1,0:T(8,128)S(1)}, f32[336,128]{1,0:T(8,128)S(1)}, u32[]{:S(2)}, u32[]{:S(2)}) collective-permute-start(f32[336,128]{1,0:T(8,128)S(1)} %collective-permute-done.7.far_ref), channel_id=1, source_target_pairs={{0,1},{1,0},{2,3},{3,2},{4,5},{5,4},{6,7},{7,6},{8,9},{9,8},{10,11... | collective-permute-start | bytes 516104 | tf_op jit(solution)/shard_map/ppermute | solution.py:559

commit v7 on v6

--- a/solution.py
+++ b/solution.py
@@ -12,6 +12,8 @@
 sigma = cheb_mid / cheb_half
 kappa = (0.75, 0.75, 1.5)
 HALO = 10
+RING_ORDER = (12, 8, 4)
+FIRST_TWO, FIRST_SIX = 1 + RING_ORDER.index(4), 1 + RING_ORDER.index(12)
 EXT = 16 + 2 * HALO
 
 
@@ -294,7 +296,7 @@
 
 
 def up_kernel(
-    row_ref, far_ref, far2_ref, msg_in_ref,
+    mine_ref, far_ref, near_ref, other_ref,
     v0_ref, beta0_ref, root0_ref, v1_ref, beta1_ref, root1_ref, sol_ref,
     out_hbm,
     all_s, solid_s, w_s, coef_s, f_s, e2_s, pe_s, a_s, bb_s, d_s, out_ref, sems,
@@ -303,30 +305,28 @@
     odd = me & 1
     is_odd = odd == 1
 
-    for t in range(16):
-        rows = slice(16 * t, 16 * t + 16)
-        far, far2 = far_ref[rows, :], far2_ref[rows, :]
-        all_s[t] = jnp.where(is_odd, far2, far)
-        all_s[16 + t] = row_ref[rows, :]
-        all_s[32 + t] = jnp.where(is_odd, far, far2)
-    far, far2 = far_ref[256:272, :], far2_ref[256:272, :]
-    solid_s[0:16, :] = jnp.where(is_odd, far2, far)
-    solid_s[16:32, :] = row_ref[256:272, :]
-    solid_s[32:48, :] = jnp.where(is_odd, far, far2)
+    for k, ref in enumerate((far_ref, mine_ref, near_ref)):
+        start = (136, 0, 272)[k]
+        for t in range(8):
+            all_s[16 * k + t] = ref[16 * t : 16 * t + 16, :]
+            all_s[16 * k + 8 + t] = other_ref[start + 16 * t : start + 16 * t + 16, :]
+        solid_s[16 * k : 16 * k + 8, :] = ref[128:136, :]
+        solid_s[16 * k + 8 : 16 * k + 16, :] = other_ref[start + 128 : start + 136, :]
+    even_row = ((me >> 4) & 1) == 0
     chip0 = (me >> 1) - 8
     here = (me >> 1) & 7
     low_rows = iota((8, 128), 0) < 4
     for w in range(17):
         chip = chip0 + w
         rel = (chip >> 3) - (me >> 4)
-        holder = jnp.where(rel == 0, odd, jnp.where(rel < 0, 0, 1))
         beside = (chip ^ here) & 1
         x0, x1 = ((chip ^ (here - sign * beside)) & 7 for sign in (1, -1))
         six0, six1 = x0 >> 2, x1 >> 2
         two0, two1 = ((x0 >> 1) & 1) ^ six0, ((x1 >> 1) & 1) ^ six1
-        slot = (rel + 1) * 16 + 4 * beside
-        block0 = slot + two0 + 2 * six0 + 8 * holder
-        block1 = slot + two1 + 2 * six1 + 8 * (1 - holder)
+        place = jnp.where(rel == 0, 1, jnp.where((rel < 0) == even_row, 0, 2))
+        slot = 16 * place + 4 * beside
+        block0 = slot + (FIRST_TWO * two0 ^ FIRST_SIX * six0) + 8 * odd
+        block1 = slot + (FIRST_TWO * two1 ^ FIRST_SIX * six1) + 8 * (1 - odd)
         straight = beside == 0
         blocks = (jnp.where(straight, block0, block1), jnp.where(straight, block1, block0))
         for half in range(2):
@@ -451,8 +451,10 @@
     across = jnp.where(is_odd, here == 7, here == 0)
 
     def edge_slabs(k, left):
-        mine = msg_in_ref[136 + 8 * k : 144 + 8 * k, :]
-        other = jnp.where(across, far_ref[272 + 8 * k : 280 + 8 * k, :], row_ref[272 + 8 * k : 280 + 8 * k, :])
+        mine = other_ref[408 + 8 * k : 416 + 8 * k, :]
+        rows = slice(136 + 8 * k, 144 + 8 * k)
+        beyond = jnp.where(is_odd == even_row, near_ref[rows, :], far_ref[rows, :])
+        other = jnp.where(across, beyond, mine_ref[rows, :])
         p = jnp.where(is_odd == left, mine, other)
         first = jnp.where(odd_lane, pltpu.roll(p, 1, 1), p)
         second = jnp.where(odd_lane, p, pltpu.roll(p, 127, 1))
@@ -573,10 +575,9 @@
     return lax.ppermute(values, "bricks", sorted(pairs))
 
 
-def next_rows(values):
+def swap_far_rows(values):
     n = lax.axis_size("bricks")
-    pairs = [(i, i + 16 if i % 2 == 0 else i - 16) for i in range(n)]
-    return lax.ppermute(values, "bricks", [(i, j) for i, j in pairs if 0 <= j < n])
+    return lax.ppermute(values, "bricks", [(i, i + 16 if i >> 4 & 1 else i - 16) for i in range(16, n - 16)])
 
 
 def body(load_field, material_class, occupancy, moduli):
@@ -629,7 +630,7 @@
         return jnp.where((row_of & bit) == 0, a, b)
 
     mine = msg[:24]
-    parts = [mine] + [swap_bits(mine, bits) for bits in (4, 12, 8)]
+    parts = [mine] + [swap_bits(mine, bits) for bits in RING_ORDER]
     blocks = jnp.concatenate([part[:16] for part in parts], axis=0)
     solids = parts[0][16:]
     for k in (1, 2, 3):
@@ -638,10 +639,9 @@
     blocks = jnp.concatenate([blocks, got[:64]], axis=0)
     solids = joined(solids, got[64:72], 4)
     edge_in = got[72:]
-    msg_in = swap_bits(jnp.concatenate([blocks, solids, msg[24:]], axis=0), 1)
-    row = jnp.concatenate([blocks, msg_in[:128], solids, msg_in[128:136], edge_in], axis=0)
-    far = next_rows(row)
-    far2 = swap_bits(far, 1)
+    mine = jnp.concatenate([blocks, solids, edge_in], axis=0)
+    far, near = swap_far_rows(mine), swap_bits(mine, 16)
+    other = swap_bits(jnp.concatenate([mine[:136], far[:136], near[:136], msg[24:]], axis=0), 1)
     return pl.pallas_call(
         up_kernel,
         out_shape=shaped(3, 16, 16, 128),
@@ -663,7 +663,7 @@
         ],
         compiler_params=PARAMS,
         name="up",
-    )(row, far, far2, msg_in, v0, beta0, root0, v1, beta1, root1, solid_rows)
+    )(mine, far, near, other, v0, beta0, root0, v1, beta1, root1, solid_rows)
 
 
 def solution(mesh):

time: 53.4 us -> 49.7 us (0.931)
  waiting for transfers between devices: 19.3 us -> 14.6 us
  starting transfers between devices: 20.4 us -> 21.5 us
    ppermute x6, waiting for transfers between devices: 6.16 us -> 3.28 us  [swap_bits(): return lax.ppermute(values, 'bricks', [(i, i ^ bits) for i in range(n)])]
    ppermute x1, waiting for transfers between devices: 6 us -> 4.52 us  [swap_far_rows(): lax.ppermute(values, 'bricks', [(i, i + 16 if i >> 4 & 1 else i - 16) for...]
    ppermute x1, starting transfers between devices: 3.39 us -> 4.03 us  [swap_far_rows(): lax.ppermute(values, 'bricks', [(i, i + 16 if i >> 4 & 1 else i - 16) for...]
  transfers between devices with their start and end apart: 9 -> 9, of which waited for: 6 -> 7; matrix products, arithmetic and copies ran while one was open for 0% -> 0% of each run, Pallas kernels for 3% -> 3%
where the time goes in v7:
time: 49.7 us; the launch traced here: 49.3 us
  starting transfers between devices  21.5 us (43%)
  waiting for transfers between devices  14.6 us (29%)
  Pallas kernels  11.9 us (24%)
  local copies, waits for them, and re-layouts  0.95 us (2%)
    ppermute x1, starting transfers between devices, swap_before(): lax.ppermute(values, 'bricks', [(i, i + 1 if i % 2 else i - 1) for i in r...  10.2 us
    ppermute x6, starting transfers between devices, swap_bits(): return lax.ppermute(values, 'bricks', [(i, i ^ bits) for i in range(n)])  6.85 us
    pallas_call x1, Pallas kernels, body(): pl.pallas_call(up_kernel, out_shape=shaped(3, 16, 16, 128), in_specs=[VME...  6.81 us
    ppermute x1, waiting for transfers between devices, swap_ring(): return lax.ppermute(values, 'bricks', sorted(pairs))  4.59 us
    ppermute x1, waiting for transfers between devices, swap_far_rows(): lax.ppermute(values, 'bricks', [(i, i + 16 if i >> 4 & 1 else i - 16) for...  4.52 us
    ppermute x1, starting transfers between devices, swap_far_rows(): lax.ppermute(values, 'bricks', [(i, i + 16 if i >> 4 & 1 else i - 16) for...  4.03 us
    ppermute x6, waiting for transfers between devices, swap_bits(): return lax.ppermute(values, 'bricks', [(i, i ^ bits) for i in range(n)])  3.28 us
    ppermute x1, waiting for transfers between devices, swap_before(): lax.ppermute(values, 'bricks', [(i, i + 1 if i % 2 else i - 1) for i in r...  2.2 us
  transfers between devices with their start and end apart: 9, of which 7 were waited for; matrix products, arithmetic and copies ran while one was open for 0% of the time, Pallas kernels for 3%

profile of v7, /device:TPU:24, one launch (start us, length us, event | category | flops | bytes accessed | tf_op | source)
XLA Modules:
  0.0 49.3 jit_solution(2741973120531056448)
XLA Ops:
  0.0 0.0 copy-start
  0.0 2.1 %pack.1 = (f32[38,16,128]{2,1,0:T(8,128)}, f32[38,16,128]{2,1,0:T(8,128)}, f32[17,16,128]{2,1,0:T(8,128)}) custom-call(f32[3,16,16,128]{3,2,1,0:T(8,128)} %load_ref.3, s32[16,16,128]{2,1,0:T(8,128)} %class_ref.1, s32[1,1,8]{2,1,0:T(1,128)} %occ_ref.1, f32[8]{0:T(128)} %moduli_ref.1), custom_call_target="tpu_custom_call" | custom-call | tf_op jit(solution)/shard_map/pack/pallas_call | solution.py:584
  2.1 0.1 collective-permute-start
  2.2 10.2 %collective-permute-start.1 = (f32[38,16,128]{2,1,0:T(8,128)}, f32[38,16,128]{2,1,0:T(8,128)S(1)}, u32[]{:S(2)}, u32[]{:S(2)}) collective-permute-start(f32[38,16,128]{2,1,0:T(8,128)} %get-tuple-element.27), channel_id=1, source_target_pairs={{1,2},{2,1},{3,4},{4,3},{5,6},{6,5},{7,8},{8,7},{9,10},{10,9},{11,... | collective-permute-start | bytes 933896 | tf_op jit(solution)/shard_map/ppermute | solution.py:566
  12.5 0.0 collective-permute-done.x_ref.x_solid_ref
  12.5 0.0 copy-done
  12.5 0.0 copy-start.1
  12.5 0.9 %copy-done.1 = f32[17,16,128]{2,1,0:T(8,128)S(1)} copy-done((f32[17,16,128]{2,1,0:T(8,128)S(1)}, f32[17,16,128]{2,1,0:T(8,128)}, u32[]{:S(2)}) %copy-start.1) | copy-done | bytes 139288
  13.4 1.6 %inner.1 = (f32[3,36,16,128]{3,2,1,0:T(8,128)S(1)}, f32[3,36,16,128]{3,2,1,0:T(8,128)S(1)}, f32[36,16,128]{2,1,0:T(8,128)S(1)}, f32[3,36,16,128]{3,2,1,0:T(8,128...) custom-call(f32[3,16,16,128]{3,2,1,0:T(8,128)S(1)} %copy-done, ...), custom_call_target="tpu_custom_call" | custom-call | flops 10000000 | bytes 4000000 | tf_op jit(solution)/shard_map/inner/pallas_call | solution.py:602
  15.0 2.2 %collective-permute-done.1.o_ref = f32[38,16,128]{2,1,0:T(8,128)S(1)} collective-permute-done((f32[38,16,128]{2,1,0:T(8,128)}, f32[38,16,128]{2,1,0:T(8,128)S(1)}, u32[]{:S(2)}, u32[]{:S(2)}) %collective-permute-start.1) | collective-permute-done | bytes 311328 | tf_op jit(solution)/shard_map/ppermute | solution.py:566
  17.2 1.4 %down.1 = (f32[3,36,16,128]{3,2,1,0:T(8,128)S(1)}, f32[3,36,16,128]{3,2,1,0:T(8,128)S(1)}, f32[36,16,128]{2,1,0:T(8,128)S(1)}, f32[3,36,16,128]{3,2,1,0:T(8,128)...) custom-call(f32[17,16,128]{2,1,0:T(8,128)S(1)} %copy-done.1, ...), custom_call_target="tpu_custom_call", output_to_operand_aliasing={{0}: (3, {}), {1}: (4, {}), {2}: (5, {}), {3}: (6, {}), {4}... | custom-call | tf_op jit(solution)/shard_map/down/pallas_call | solution.py:611
  18.6 0.1 collective-permute-start.2
  18.7 1.9 %collective-permute-start.3 = (f32[24,128]{1,0:T(8,128)S(1)}, f32[24,128]{1,0:T(8,128)S(1)}, u32[]{:S(2)}, u32[]{:S(2)}) collective-permute-start(f32[24,128]{1,0:T(8,128)S(1)} %slice.50), channel_id=1, source_target_pairs={{0,8},{1,9},{2,10},{3,11},{4,12},{5,13},{6,14},{7,15},{8,0},{9,1},... | collective-permute-start | bytes 36872 | tf_op jit(solution)/shard_map/ppermute | solution.py:561
  20.6 4.6 %collective-permute-start.4 = (f32[24,128]{1,0:T(8,128)S(1)}, f32[24,128]{1,0:T(8,128)S(1)}, u32[]{:S(2)}, u32[]{:S(2)}) collective-permute-start(f32[24,128]{1,0:T(8,128)S(1)} %slice.50), channel_id=1, source_target_pairs={{0,4},{1,5},{2,6},{3,7},{4,0},{5,1},{6,2},{7,3},{8,12},{9,13},{10,... | collective-permute-start | bytes 36872 | tf_op jit(solution)/shard_map/ppermute | solution.py:561
  25.2 0.0 collective-permute-done.2
  25.2 1.2 %collective-permute-done.3 = f32[24,128]{1,0:T(8,128)S(1)} collective-permute-done((f32[24,128]{1,0:T(8,128)S(1)}, f32[24,128]{1,0:T(8,128)S(1)}, u32[]{:S(2)}, u32[]{:S(2)}) %collective-permute-start.3) | collective-permute-done | bytes 12320 | tf_op jit(solution)/shard_map/ppermute | solution.py:561
  26.5 0.4 collective-permute-done.4
  26.9 0.1 constant_dynamic-update-slice_fusion.1
  27.0 0.4 collective-permute-start.5
  27.4 4.6 %collective-permute-done.5 = f32[136,128]{1,0:T(8,128)S(1)} collective-permute-done((f32[136,128]{1,0:T(8,128)S(1)}, f32[136,128]{1,0:T(8,128)S(1)}, u32[]{:S(2)}, u32[]{:S(2)}) %collective-permute-start.5) | collective-permute-done | bytes 69664 | tf_op jit(solution)/shard_map/ppermute | solution.py:575
  32.0 0.1 constant_dynamic-update-slice_fusion.14
  32.1 4.0 %collective-permute-start.6 = (f32[200,128]{1,0:T(8,128)S(1)}, f32[200,128]{1,0:T(8,128)S(1)}, u32[]{:S(2)}, u32[]{:S(2)}) collective-permute-start(f32[200,128]{1,0:T(8,128)S(1)} %constant_dynamic-update-slice_fusion.6.mine_ref), channel_id=1, source_target_pairs={{16,32},{17,33},{18,34},{19,35},{20,36},{21,37},{22,38},{23,39},{2... | collective-permute-start | bytes 307208 | tf_op jit(solution)/shard_map/ppermute | solution.py:580
  36.1 0.1 collective-permute-start.7
  36.2 4.5 %collective-permute-done.6.far_ref = f32[200,128]{1,0:T(8,128)S(1)} collective-permute-done((f32[200,128]{1,0:T(8,128)S(1)}, f32[200,128]{1,0:T(8,128)S(1)}, u32[]{:S(2)}, u32[]{:S(2)}) %collective-permute-start.6) | collective-permute-done | bytes 102432 | tf_op jit(solution)/shard_map/ppermute | solution.py:580
  40.7 0.1 collective-permute-done.7.near_ref
  40.9 0.1 collective-permute-start.8
  41.0 1.5 %collective-permute-done.8.other_ref = f32[472,128]{1,0:T(8,128)S(1)} collective-permute-done((f32[472,128]{1,0:T(8,128)S(1)}, f32[472,128]{1,0:T(8,128)S(1)}, u32[]{:S(2)}, u32[]{:S(2)}) %collective-permute-start.8) | collective-permute-done | bytes 241696 | tf_op jit(solution)/shard_map/ppermute | solution.py:561
  42.4 6.8 %up.1 = f32[3,16,16,128]{3,2,1,0:T(8,128)} custom-call(f32[200,128]{1,0:T(8,128)S(1)} %constant_dynamic-update-slice_fusion.6.mine_ref, f32[200,128]{1,0:T(8,128)S(1)} %collective-permute-done.6.far_ref, f32[200,128]{1,0:T(8,128)S(1)} %collective-permute-done.7.near_ref, f32[472,128]{1,0:T(8,128)S(1)} %collective-permute-done.8.other_ref, ...), custom_call_target="tpu_custom_call" | custom-call | tf_op jit(solution)/shard_map/up/pallas_call | solution.py:645
  (14 shorter events, 0.1 us)
Async XLA Ops:
  0.0 12.5 %copy-start = (f32[3,16,16,128]{3,2,1,0:T(8,128)S(1)}, f32[3,16,16,128]{3,2,1,0:T(8,128)}, u32[]{:S(2)}) copy-start(f32[3,16,16,128]{3,2,1,0:T(8,128)} %load_ref.3) | copy-start | bytes 1179652
  2.1 10.4 %collective-permute-start = (f32[38,16,128]{2,1,0:T(8,128)}, f32[38,16,128]{2,1,0:T(8,128)S(1)}, u32[]{:S(2)}, u32[]{:S(2)}) collective-permute-start(f32[38,16,128]{2,1,0:T(8,128)} %get-tuple-element.26), channel_id=1, source_target_pairs={{0,1},{1,0},{2,3},{3,2},{4,5},{5,4},{6,7},{7,6},{8,9},{9,8},{10,11... | collective-permute-start | bytes 933896 | tf_op jit(solution)/shard_map/ppermute | solution.py:561
  2.2 15.0 %collective-permute-start.1 = (f32[38,16,128]{2,1,0:T(8,128)}, f32[38,16,128]{2,1,0:T(8,128)S(1)}, u32[]{:S(2)}, u32[]{:S(2)}) collective-permute-start(f32[38,16,128]{2,1,0:T(8,128)} %get-tuple-element.27), channel_id=1, source_target_pairs={{1,2},{2,1},{3,4},{4,3},{5,6},{6,5},{7,8},{8,7},{9,10},{10,9},{11,... | collective-permute-start | bytes 933896 | tf_op jit(solution)/shard_map/ppermute | solution.py:566
  12.5 0.9 %copy-start.1 = (f32[17,16,128]{2,1,0:T(8,128)S(1)}, f32[17,16,128]{2,1,0:T(8,128)}, u32[]{:S(2)}) copy-start(f32[17,16,128]{2,1,0:T(8,128)} %get-tuple-element.25.own_ref) | copy-start | bytes 417796
  18.6 6.6 %collective-permute-start.2 = (f32[24,128]{1,0:T(8,128)S(1)}, f32[24,128]{1,0:T(8,128)S(1)}, u32[]{:S(2)}, u32[]{:S(2)}) collective-permute-start(f32[24,128]{1,0:T(8,128)S(1)} %slice.50), channel_id=1, source_target_pairs={{0,12},{1,13},{2,14},{3,15},{4,8},{5,9},{6,10},{7,11},{8,4},{9,5},... | collective-permute-start | bytes 36872 | tf_op jit(solution)/shard_map/ppermute | solution.py:561
  18.7 7.7 %collective-permute-start.3 = (f32[24,128]{1,0:T(8,128)S(1)}, f32[24,128]{1,0:T(8,128)S(1)}, u32[]{:S(2)}, u32[]{:S(2)}) collective-permute-start(f32[24,128]{1,0:T(8,128)S(1)} %slice.50), channel_id=1, source_target_pairs={{0,8},{1,9},{2,10},{3,11},{4,12},{5,13},{6,14},{7,15},{8,0},{9,1},... | collective-permute-start | bytes 36872 | tf_op jit(solution)/shard_map/ppermute | solution.py:561
  20.6 6.2 %collective-permute-start.4 = (f32[24,128]{1,0:T(8,128)S(1)}, f32[24,128]{1,0:T(8,128)S(1)}, u32[]{:S(2)}, u32[]{:S(2)}) collective-permute-start(f32[24,128]{1,0:T(8,128)S(1)} %slice.50), channel_id=1, source_target_pairs={{0,4},{1,5},{2,6},{3,7},{4,0},{5,1},{6,2},{7,3},{8,12},{9,13},{10,... | collective-permute-start | bytes 36872 | tf_op jit(solution)/shard_map/ppermute | solution.py:561
  27.0 5.0 %collective-permute-start.5 = (f32[136,128]{1,0:T(8,128)S(1)}, f32[136,128]{1,0:T(8,128)S(1)}, u32[]{:S(2)}, u32[]{:S(2)}) collective-permute-start(f32[136,128]{1,0:T(8,128)S(1)} %constant_dynamic-update-slice_fusion), channel_id=1, source_target_pairs={{0,15},{1,2},{2,1},{3,4},{4,3},{5,6},{6,5},{7,8},{8,7},{9,10},{10,... | collective-permute-start | bytes 208904 | tf_op jit(solution)/shard_map/ppermute | solution.py:575
  32.1 8.7 %collective-permute-start.6 = (f32[200,128]{1,0:T(8,128)S(1)}, f32[200,128]{1,0:T(8,128)S(1)}, u32[]{:S(2)}, u32[]{:S(2)}) collective-permute-start(f32[200,128]{1,0:T(8,128)S(1)} %constant_dynamic-update-slice_fusion.6.mine_ref), channel_id=1, source_target_pairs={{16,32},{17,33},{18,34},{19,35},{20,36},{21,37},{22,38},{23,39},{2... | collective-permute-start | bytes 307208 | tf_op jit(solution)/shard_map/ppermute | solution.py:580
  36.1 4.7 %collective-permute-start.7 = (f32[200,128]{1,0:T(8,128)S(1)}, f32[200,128]{1,0:T(8,128)S(1)}, u32[]{:S(2)}, u32[]{:S(2)}) collective-permute-start(f32[200,128]{1,0:T(8,128)S(1)} %constant_dynamic-update-slice_fusion.6.mine_ref), channel_id=1, source_target_pairs={{0,16},{1,17},{2,18},{3,19},{4,20},{5,21},{6,22},{7,23},{8,24},{9,... | collective-permute-start | bytes 307208 | tf_op jit(solution)/shard_map/ppermute | solution.py:561
  40.9 1.6 %collective-permute-start.8 = (f32[472,128]{1,0:T(8,128)S(1)}, f32[472,128]{1,0:T(8,128)S(1)}, u32[]{:S(2)}, u32[]{:S(2)}) collective-permute-start(f32[472,128]{1,0:T(8,128)S(1)} %constant_dynamic-update-slice_fusion.13), channel_id=1, source_target_pairs={{0,1},{1,0},{2,3},{3,2},{4,5},{5,4},{6,7},{7,6},{8,9},{9,8},{10,11... | collective-permute-start | bytes 725000 | tf_op jit(solution)/shard_map/ppermute | solution.py:561

commit v8 on v7

--- a/solution.py
+++ b/solution.py
@@ -538,9 +538,9 @@
         out_ref[0, k - 4] = x[0] + third
         out_ref[1, k - 4] = x[1] + third
         out_ref[2, k - 4] = third - x[0] - x[1]
-        if k % 4 == 3:
-            part = pl.ds(k - 7, 4)
-            copy = pltpu.make_async_copy(out_ref.at[:, part], out_hbm.at[:, part], sems.at[k // 4 - 1])
+        if k % 2 == 1:
+            part = pl.ds(k - 5, 2)
+            copy = pltpu.make_async_copy(out_ref.at[:, part], out_hbm.at[:, part], sems.at[k // 2 - 2])
             copy.start()
             copies.append(copy)
     for copy in copies:
@@ -659,7 +659,7 @@
             pltpu.VMEM((3, 24, 16, 128), F32),
             pltpu.VMEM((3, 24, 16, 128), F32),
             pltpu.VMEM((3, 16, 16, 128), F32),
-            pltpu.SemaphoreType.DMA((4,)),
+            pltpu.SemaphoreType.DMA((8,)),
         ],
         compiler_params=PARAMS,
         name="up",

time: 49.7 us -> 49.7 us (level)
  no operation moved by 1% of the time
where the time goes in v8:
time: 49.7 us; the launch traced here: 49.3 us
  starting transfers between devices  21.5 us (43%)
  waiting for transfers between devices  14.6 us (29%)
  Pallas kernels  11.9 us (24%)
  local copies, waits for them, and re-layouts  0.95 us (2%)
    ppermute x1, starting transfers between devices, swap_before(): lax.ppermute(values, 'bricks', [(i, i + 1 if i % 2 else i - 1) for i in r...  10.2 us
    ppermute x6, starting transfers between devices, swap_bits(): return lax.ppermute(values, 'bricks', [(i, i ^ bits) for i in range(n)])  6.85 us
    pallas_call x1, Pallas kernels, body(): pl.pallas_call(up_kernel, out_shape=shaped(3, 16, 16, 128), in_specs=[VME...  6.82 us
    ppermute x1, waiting for transfers between devices, swap_ring(): return lax.ppermute(values, 'bricks', sorted(pairs))  4.59 us
    ppermute x1, waiting for transfers between devices, swap_far_rows(): lax.ppermute(values, 'bricks', [(i, i + 16 if i >> 4 & 1 else i - 16) for...  4.52 us
    ppermute x1, starting transfers between devices, swap_far_rows(): lax.ppermute(values, 'bricks', [(i, i + 16 if i >> 4 & 1 else i - 16) for...  4.03 us
    ppermute x6, waiting for transfers between devices, swap_bits(): return lax.ppermute(values, 'bricks', [(i, i ^ bits) for i in range(n)])  3.28 us
    ppermute x1, waiting for transfers between devices, swap_before(): lax.ppermute(values, 'bricks', [(i, i + 1 if i % 2 else i - 1) for i in r...  2.2 us
  transfers between devices with their start and end apart: 9, of which 7 were waited for; matrix products, arithmetic and copies ran while one was open for 0% of the time, Pallas kernels for 3%

profile of v8, /device:TPU:24, one launch (start us, length us, event | category | flops | bytes accessed | tf_op | source)
XLA Modules:
  0.0 49.3 jit_solution(5785555345030999985)
XLA Ops:
  0.0 0.0 copy-start
  0.0 2.1 %pack.1 = (f32[38,16,128]{2,1,0:T(8,128)}, f32[38,16,128]{2,1,0:T(8,128)}, f32[17,16,128]{2,1,0:T(8,128)}) custom-call(f32[3,16,16,128]{3,2,1,0:T(8,128)} %load_ref.3, s32[16,16,128]{2,1,0:T(8,128)} %class_ref.1, s32[1,1,8]{2,1,0:T(1,128)} %occ_ref.1, f32[8]{0:T(128)} %moduli_ref.1), custom_call_target="tpu_custom_call" | custom-call | tf_op jit(solution)/shard_map/pack/pallas_call | solution.py:584
  2.1 0.1 collective-permute-start
  2.2 10.2 %collective-permute-start.1 = (f32[38,16,128]{2,1,0:T(8,128)}, f32[38,16,128]{2,1,0:T(8,128)S(1)}, u32[]{:S(2)}, u32[]{:S(2)}) collective-permute-start(f32[38,16,128]{2,1,0:T(8,128)} %get-tuple-element.27), channel_id=1, source_target_pairs={{1,2},{2,1},{3,4},{4,3},{5,6},{6,5},{7,8},{8,7},{9,10},{10,9},{11,... | collective-permute-start | bytes 933896 | tf_op jit(solution)/shard_map/ppermute | solution.py:566
  12.5 0.0 collective-permute-done.x_ref.x_solid_ref
  12.5 0.0 copy-done
  12.5 0.0 copy-start.1
  12.5 0.9 %copy-done.1 = f32[17,16,128]{2,1,0:T(8,128)S(1)} copy-done((f32[17,16,128]{2,1,0:T(8,128)S(1)}, f32[17,16,128]{2,1,0:T(8,128)}, u32[]{:S(2)}) %copy-start.1) | copy-done | bytes 139288
  13.4 1.6 %inner.1 = (f32[3,36,16,128]{3,2,1,0:T(8,128)S(1)}, f32[3,36,16,128]{3,2,1,0:T(8,128)S(1)}, f32[36,16,128]{2,1,0:T(8,128)S(1)}, f32[3,36,16,128]{3,2,1,0:T(8,128...) custom-call(f32[3,16,16,128]{3,2,1,0:T(8,128)S(1)} %copy-done, ...), custom_call_target="tpu_custom_call" | custom-call | flops 10000000 | bytes 4000000 | tf_op jit(solution)/shard_map/inner/pallas_call | solution.py:602
  15.0 2.2 %collective-permute-done.1.o_ref = f32[38,16,128]{2,1,0:T(8,128)S(1)} collective-permute-done((f32[38,16,128]{2,1,0:T(8,128)}, f32[38,16,128]{2,1,0:T(8,128)S(1)}, u32[]{:S(2)}, u32[]{:S(2)}) %collective-permute-start.1) | collective-permute-done | bytes 311328 | tf_op jit(solution)/shard_map/ppermute | solution.py:566
  17.2 1.4 %down.1 = (f32[3,36,16,128]{3,2,1,0:T(8,128)S(1)}, f32[3,36,16,128]{3,2,1,0:T(8,128)S(1)}, f32[36,16,128]{2,1,0:T(8,128)S(1)}, f32[3,36,16,128]{3,2,1,0:T(8,128)...) custom-call(f32[17,16,128]{2,1,0:T(8,128)S(1)} %copy-done.1, ...), custom_call_target="tpu_custom_call", output_to_operand_aliasing={{0}: (3, {}), {1}: (4, {}), {2}: (5, {}), {3}: (6, {}), {4}... | custom-call | tf_op jit(solution)/shard_map/down/pallas_call | solution.py:611
  18.6 0.1 collective-permute-start.2
  18.7 1.9 %collective-permute-start.3 = (f32[24,128]{1,0:T(8,128)S(1)}, f32[24,128]{1,0:T(8,128)S(1)}, u32[]{:S(2)}, u32[]{:S(2)}) collective-permute-start(f32[24,128]{1,0:T(8,128)S(1)} %slice.50), channel_id=1, source_target_pairs={{0,8},{1,9},{2,10},{3,11},{4,12},{5,13},{6,14},{7,15},{8,0},{9,1},... | collective-permute-start | bytes 36872 | tf_op jit(solution)/shard_map/ppermute | solution.py:561
  20.6 4.6 %collective-permute-start.4 = (f32[24,128]{1,0:T(8,128)S(1)}, f32[24,128]{1,0:T(8,128)S(1)}, u32[]{:S(2)}, u32[]{:S(2)}) collective-permute-start(f32[24,128]{1,0:T(8,128)S(1)} %slice.50), channel_id=1, source_target_pairs={{0,4},{1,5},{2,6},{3,7},{4,0},{5,1},{6,2},{7,3},{8,12},{9,13},{10,... | collective-permute-start | bytes 36872 | tf_op jit(solution)/shard_map/ppermute | solution.py:561
  25.2 0.0 collective-permute-done.2
  25.2 1.2 %collective-permute-done.3 = f32[24,128]{1,0:T(8,128)S(1)} collective-permute-done((f32[24,128]{1,0:T(8,128)S(1)}, f32[24,128]{1,0:T(8,128)S(1)}, u32[]{:S(2)}, u32[]{:S(2)}) %collective-permute-start.3) | collective-permute-done | bytes 12320 | tf_op jit(solution)/shard_map/ppermute | solution.py:561
  26.5 0.4 collective-permute-done.4
  26.9 0.1 constant_dynamic-update-slice_fusion.1
  27.0 0.4 collective-permute-start.5
  27.4 4.6 %collective-permute-done.5 = f32[136,128]{1,0:T(8,128)S(1)} collective-permute-done((f32[136,128]{1,0:T(8,128)S(1)}, f32[136,128]{1,0:T(8,128)S(1)}, u32[]{:S(2)}, u32[]{:S(2)}) %collective-permute-start.5) | collective-permute-done | bytes 69664 | tf_op jit(solution)/shard_map/ppermute | solution.py:575
  32.0 0.1 constant_dynamic-update-slice_fusion.14
  32.1 4.0 %collective-permute-start.6 = (f32[200,128]{1,0:T(8,128)S(1)}, f32[200,128]{1,0:T(8,128)S(1)}, u32[]{:S(2)}, u32[]{:S(2)}) collective-permute-start(f32[200,128]{1,0:T(8,128)S(1)} %constant_dynamic-update-slice_fusion.6.mine_ref), channel_id=1, source_target_pairs={{16,32},{17,33},{18,34},{19,35},{20,36},{21,37},{22,38},{23,39},{2... | collective-permute-start | bytes 307208 | tf_op jit(solution)/shard_map/ppermute | solution.py:580
  36.1 0.1 collective-permute-start.7
  36.2 4.5 %collective-permute-done.6.far_ref = f32[200,128]{1,0:T(8,128)S(1)} collective-permute-done((f32[200,128]{1,0:T(8,128)S(1)}, f32[200,128]{1,0:T(8,128)S(1)}, u32[]{:S(2)}, u32[]{:S(2)}) %collective-permute-start.6) | collective-permute-done | bytes 102432 | tf_op jit(solution)/shard_map/ppermute | solution.py:580
  40.7 0.1 collective-permute-done.7.near_ref
  40.9 0.1 collective-permute-start.8
  41.0 1.5 %collective-permute-done.8.other_ref = f32[472,128]{1,0:T(8,128)S(1)} collective-permute-done((f32[472,128]{1,0:T(8,128)S(1)}, f32[472,128]{1,0:T(8,128)S(1)}, u32[]{:S(2)}, u32[]{:S(2)}) %collective-permute-start.8) | collective-permute-done | bytes 241696 | tf_op jit(solution)/shard_map/ppermute | solution.py:561
  42.4 6.8 %up.1 = f32[3,16,16,128]{3,2,1,0:T(8,128)} custom-call(f32[200,128]{1,0:T(8,128)S(1)} %constant_dynamic-update-slice_fusion.6.mine_ref, f32[200,128]{1,0:T(8,128)S(1)} %collective-permute-done.6.far_ref, f32[200,128]{1,0:T(8,128)S(1)} %collective-permute-done.7.near_ref, f32[472,128]{1,0:T(8,128)S(1)} %collective-permute-done.8.other_ref, ...), custom_call_target="tpu_custom_call" | custom-call | tf_op jit(solution)/shard_map/up/pallas_call | solution.py:645
  (14 shorter events, 0.1 us)
Async XLA Ops:
  0.0 12.5 %copy-start = (f32[3,16,16,128]{3,2,1,0:T(8,128)S(1)}, f32[3,16,16,128]{3,2,1,0:T(8,128)}, u32[]{:S(2)}) copy-start(f32[3,16,16,128]{3,2,1,0:T(8,128)} %load_ref.3) | copy-start | bytes 1179652
  2.1 10.4 %collective-permute-start = (f32[38,16,128]{2,1,0:T(8,128)}, f32[38,16,128]{2,1,0:T(8,128)S(1)}, u32[]{:S(2)}, u32[]{:S(2)}) collective-permute-start(f32[38,16,128]{2,1,0:T(8,128)} %get-tuple-element.26), channel_id=1, source_target_pairs={{0,1},{1,0},{2,3},{3,2},{4,5},{5,4},{6,7},{7,6},{8,9},{9,8},{10,11... | collective-permute-start | bytes 933896 | tf_op jit(solution)/shard_map/ppermute | solution.py:561
  2.2 15.0 %collective-permute-start.1 = (f32[38,16,128]{2,1,0:T(8,128)}, f32[38,16,128]{2,1,0:T(8,128)S(1)}, u32[]{:S(2)}, u32[]{:S(2)}) collective-permute-start(f32[38,16,128]{2,1,0:T(8,128)} %get-tuple-element.27), channel_id=1, source_target_pairs={{1,2},{2,1},{3,4},{4,3},{5,6},{6,5},{7,8},{8,7},{9,10},{10,9},{11,... | collective-permute-start | bytes 933896 | tf_op jit(solution)/shard_map/ppermute | solution.py:566
  12.5 0.9 %copy-start.1 = (f32[17,16,128]{2,1,0:T(8,128)S(1)}, f32[17,16,128]{2,1,0:T(8,128)}, u32[]{:S(2)}) copy-start(f32[17,16,128]{2,1,0:T(8,128)} %get-tuple-element.25.own_ref) | copy-start | bytes 417796
  18.6 6.6 %collective-permute-start.2 = (f32[24,128]{1,0:T(8,128)S(1)}, f32[24,128]{1,0:T(8,128)S(1)}, u32[]{:S(2)}, u32[]{:S(2)}) collective-permute-start(f32[24,128]{1,0:T(8,128)S(1)} %slice.50), channel_id=1, source_target_pairs={{0,12},{1,13},{2,14},{3,15},{4,8},{5,9},{6,10},{7,11},{8,4},{9,5},... | collective-permute-start | bytes 36872 | tf_op jit(solution)/shard_map/ppermute | solution.py:561
  18.7 7.7 %collective-permute-start.3 = (f32[24,128]{1,0:T(8,128)S(1)}, f32[24,128]{1,0:T(8,128)S(1)}, u32[]{:S(2)}, u32[]{:S(2)}) collective-permute-start(f32[24,128]{1,0:T(8,128)S(1)} %slice.50), channel_id=1, source_target_pairs={{0,8},{1,9},{2,10},{3,11},{4,12},{5,13},{6,14},{7,15},{8,0},{9,1},... | collective-permute-start | bytes 36872 | tf_op jit(solution)/shard_map/ppermute | solution.py:561
  20.6 6.2 %collective-permute-start.4 = (f32[24,128]{1,0:T(8,128)S(1)}, f32[24,128]{1,0:T(8,128)S(1)}, u32[]{:S(2)}, u32[]{:S(2)}) collective-permute-start(f32[24,128]{1,0:T(8,128)S(1)} %slice.50), channel_id=1, source_target_pairs={{0,4},{1,5},{2,6},{3,7},{4,0},{5,1},{6,2},{7,3},{8,12},{9,13},{10,... | collective-permute-start | bytes 36872 | tf_op jit(solution)/shard_map/ppermute | solution.py:561
  27.0 5.0 %collective-permute-start.5 = (f32[136,128]{1,0:T(8,128)S(1)}, f32[136,128]{1,0:T(8,128)S(1)}, u32[]{:S(2)}, u32[]{:S(2)}) collective-permute-start(f32[136,128]{1,0:T(8,128)S(1)} %constant_dynamic-update-slice_fusion), channel_id=1, source_target_pairs={{0,15},{1,2},{2,1},{3,4},{4,3},{5,6},{6,5},{7,8},{8,7},{9,10},{10,... | collective-permute-start | bytes 208904 | tf_op jit(solution)/shard_map/ppermute | solution.py:575
  32.1 8.7 %collective-permute-start.6 = (f32[200,128]{1,0:T(8,128)S(1)}, f32[200,128]{1,0:T(8,128)S(1)}, u32[]{:S(2)}, u32[]{:S(2)}) collective-permute-start(f32[200,128]{1,0:T(8,128)S(1)} %constant_dynamic-update-slice_fusion.6.mine_ref), channel_id=1, source_target_pairs={{16,32},{17,33},{18,34},{19,35},{20,36},{21,37},{22,38},{23,39},{2... | collective-permute-start | bytes 307208 | tf_op jit(solution)/shard_map/ppermute | solution.py:580
  36.1 4.7 %collective-permute-start.7 = (f32[200,128]{1,0:T(8,128)S(1)}, f32[200,128]{1,0:T(8,128)S(1)}, u32[]{:S(2)}, u32[]{:S(2)}) collective-permute-start(f32[200,128]{1,0:T(8,128)S(1)} %constant_dynamic-update-slice_fusion.6.mine_ref), channel_id=1, source_target_pairs={{0,16},{1,17},{2,18},{3,19},{4,20},{5,21},{6,22},{7,23},{8,24},{9,... | collective-permute-start | bytes 307208 | tf_op jit(solution)/shard_map/ppermute | solution.py:561
  40.9 1.6 %collective-permute-start.8 = (f32[472,128]{1,0:T(8,128)S(1)}, f32[472,128]{1,0:T(8,128)S(1)}, u32[]{:S(2)}, u32[]{:S(2)}) collective-permute-start(f32[472,128]{1,0:T(8,128)S(1)} %constant_dynamic-update-slice_fusion.13), channel_id=1, source_target_pairs={{0,1},{1,0},{2,3},{3,2},{4,5},{5,4},{6,7},{7,6},{8,9},{9,8},{10,11... | collective-permute-start | bytes 725000 | tf_op jit(solution)/shard_map/ppermute | solution.py:561
